TPU v7x, 32 devices: a whole 2x2x4 slice. The times are simulated.
32 devices in a mesh: dp: 8 (over z, x), mp: 4 (over y, core).
Axes of the slice: x: 2, y: 2, z: 4, core: 2. Of those that a mesh axis runs over, the one named last changes fastest.
Arguments:
- partial_grads: bfloat16 [8, 1536, 2048], P('dp', None, 'mp'), may hold values from -1.75 to 1.75
- band_owner: int32 [8], replicated, may hold values from 0 to 7, as said below
- left_factor: float32 [1536, 2048], P('dp', 'mp'), may hold values from -1 to 2.5
- right_factor: float32 [1536, 2048], P('dp', 'mp'), may hold values from -1 to 2.5
- left_root: bfloat16 [1536, 2048], P('dp', 'mp'), may hold values from -1 to 2.5, as said below
- right_root: bfloat16 [1536, 2048], P('dp', 'mp'), may hold values from -1 to 2.5, as said below
Outputs:
- direction: bfloat16 [1536, 2048], P(None, 'mp')
- left_updated: float32 [1536, 2048], P('dp', 'mp')
- right_updated: float32 [1536, 2048], P('dp', 'mp')
Inputs may be any that keep to these rules, and one draw needn't show every extreme that they name: `band_owner`: a permutation: every index of dp owns exactly one band. `left_root`: in band order, every 512 x 512 block is symmetric. `right_root`: in band order, every 512 x 512 block is symmetric.
All inputs are finite; a program needn't handle non-finite values.
Results may differ from a plain program's by a relative error of at most 0.01.
Values may be sent and summed in bfloat16 or wider, within the bound.
No kernel may reach another device: no remote copies, remote signals or barrier semaphores. Data moves between devices by JAX's collectives and lax.ppermute only.
A program may use at most 64 MiB of HBM per device.

v0:
```python
import jax
import jax.numpy as jnp
from jax import lax
from jax.sharding import PartitionSpec as P

BETA = 0.95


def against(band_rows, whole_rows, select):
    nblocks = select.shape[1]
    breadth = whole_rows.shape[1]
    blocks = whole_rows.reshape(nblocks, breadth, breadth)
    products = jnp.einsum("rk,bck->rbc", band_rows, blocks, preferred_element_type=jnp.float32)
    return jnp.sum(select[:, :, None] * products, axis=1)


def to_band_order(gathered, owners, members):
    shaped = gathered.reshape(members, -1, gathered.shape[1])
    return jnp.take(shaped, owners, axis=0).reshape(gathered.shape)


def shards(partial_grads, band_owner, left_factor, right_factor, left_root, right_root):
    members = lax.axis_size("dp")
    band_size = left_factor.shape[0]
    breadth = left_factor.shape[1]
    stacked = partial_grads.shape[1]
    nblocks = stacked // breadth
    devices = jnp.arange(members, dtype=jnp.int32)
    inverse = jnp.sum(
        jnp.where(band_owner[None, :] == devices[:, None], devices[None, :], 0), axis=1
    )
    own_band = inverse[lax.axis_index("dp")]
    partial_value = partial_grads[0]
    even_rows = lax.psum_scatter(
        partial_value.astype(jnp.float32), "dp", scatter_dimension=0, tiled=True
    ).astype(jnp.bfloat16)
    grad_full = lax.all_gather(even_rows, "dp", axis=0, tiled=True)
    grad_rows = lax.dynamic_slice_in_dim(grad_full, own_band * band_size, band_size, 0)
    global_rows = own_band * band_size + jnp.arange(band_size, dtype=jnp.int32)
    block_ids = global_rows // breadth
    within = global_rows % breadth
    block_range = jnp.arange(nblocks, dtype=jnp.int32)
    select = (block_ids[:, None] == block_range[None, :]).astype(jnp.float32)
    left_term = against(grad_rows, grad_full, select)
    left_updated = BETA * left_factor + (1.0 - BETA) * left_term
    column_range = jnp.arange(breadth, dtype=jnp.int32)
    onehot = (
        (block_range[:, None, None] == block_ids[None, None, :])
        & (column_range[None, :, None] == within[None, None, :])
    ).astype(jnp.bfloat16)
    blocks = grad_full.reshape(nblocks, breadth, breadth)
    columns = jnp.einsum("bkc,bcr->kr", blocks, onehot, preferred_element_type=jnp.float32).astype(
        jnp.bfloat16
    )
    right_products = jnp.einsum("kr,bkc->rbc", columns, blocks, preferred_element_type=jnp.float32)
    right_term = jnp.sum(select[:, :, None] * right_products, axis=1)
    right_updated = BETA * right_factor + (1.0 - BETA) * right_term
    mixed_rows = against(right_root, grad_full, select).astype(jnp.bfloat16)
    mixed_full = to_band_order(
        lax.all_gather(mixed_rows, "dp", axis=0, tiled=True), band_owner, members
    )
    direction_rows = against(left_root, mixed_full, select).astype(jnp.bfloat16)
    direction = to_band_order(
        lax.all_gather(direction_rows, "dp", axis=0, tiled=True), band_owner, members
    )
    return (direction, left_updated, right_updated)


def solution(mesh):
    placed = (P("dp", None, "mp"), P(), P("dp", "mp"), P("dp", "mp"), P("dp", "mp"), P("dp", "mp"))
    return jax.shard_map(
        shards,
        mesh=mesh,
        in_specs=placed,
        out_specs=(P(None, "mp"), P("dp", "mp"), P("dp", "mp")),
        check_vma=False,
    )
```

profile of v0, /device:TPU:0, one launch (start us, length us, event | category | flops | bytes accessed | tf_op | source)
XLA Modules:
  0.0 238.5 jit_solution(16337113449079552254)
XLA Ops:
  7.2 0.0 copy-start
  7.2 0.0 reduce-scatter.2.cloned.1.call-start
  7.2 3.5 %bitcast_convert_fusion = f32[1536,512]{1,0:T(8,128)} fusion(bf16[1,1536,512]{2,1,0:T(8,128)(2,1)} %param.8), kind=kLoop, calls=%fused_computation.2 | loop fusion | flops 786432 | bytes 4718592 | tf_op jit(solution)/shard_map/convert_element_type | solution.py:35
  10.8 0.0 copy-start.5
  10.8 0.0 reduce-scatter.2.cloned.1.call-update
  10.8 0.0 all-gather.4.cloned.1.call-start
  10.8 77.9 %reduce-scatter.2.cloned.1.call-done = f32[192,512]{1,0:T(8,128)} async-done(((f32[1536,512]{1,0:T(8,128)}), f32[192,512]{1,0:T(8,128)}) %reduce-scatter.2.cloned.1.call-update) | async-done | bytes 393232 | tf_op jit(solution)/shard_map/reduce_scatter | solution.py:34
  88.8 1.7 convert_element_type.30
  90.5 0.0 all-gather.4.cloned.1.call-update
  90.5 0.0 all-gather.6.cloned.1.call-start
  90.5 0.0 copy-done.5
  90.5 0.1 select_reduce_fusion
  90.7 0.6 dynamic_slice.6
  91.9 43.1 %all-gather.4.cloned.1.call-done = bf16[1536,512]{1,0:T(8,128)(2,1)} async-done(((bf16[192,512]{1,0:T(8,128)(2,1)}), bf16[1536,512]{1,0:T(8,128)(2,1)}) %all-gather.4.cloned.1.call-update) | async-done | bytes 1572880 | tf_op jit(solution)/shard_map/all_gather | solution.py:37
  135.1 0.0 copy-done
  135.1 2.8 %fusion.1 = bf16[192,512]{1,0:T(8,128)(2,1)} fusion(bf16[3,512,512]{2,1,0:T(8,128)(2,1)} %bitcast.45, f32[192,3]{0,1:T(4,128)S(1)} %fusion.13, bf16[192,512]{1,0:T(8,128)(2,1)S(1)} %copy-done), kind=kOutput, calls=%fused_computation.11 | convolution fusion | flops 302481408 | bytes 1968384 | tf_op jit(solution)/shard_map/rk,bck->rbc/dot_general | solution.py:13
  137.9 0.0 all-gather.6.cloned.1.call-update
  137.9 0.0 all-gather.8.cloned.1.call-start
  138.0 43.1 %all-gather.6.cloned.1.call-done = bf16[1536,512]{1,0:T(8,128)(2,1)} async-done(((bf16[192,512]{1,0:T(8,128)(2,1)}), bf16[1536,512]{1,0:T(8,128)(2,1)}) %all-gather.6.cloned.1.call-update) | async-done | bytes 1572880 | tf_op jit(solution)/shard_map/all_gather | solution.py:60
  181.1 2.1 gather_fusion
  183.1 0.0 copy-start.4
  183.1 0.2 broadcast_select_fusion
  183.3 0.0 copy-start.3
  183.4 0.7 copy-done.4
  184.0 1.4 fusion.2
  185.4 0.0 copy-start.1
  185.4 0.0 all-gather.8.cloned.1.call-update
  185.5 0.1 iota_compare_fusion
  185.5 0.0 copy-done.3
  185.6 0.7 fusion.3
  186.2 0.2 copy-done.1
  186.4 0.8 multiply_add_fusion.1
  187.2 0.0 copy-start.2
  187.2 1.0 fusion.4
  188.3 0.0 copy-done.2
  188.3 0.8 multiply_add_fusion
  189.1 39.5 %all-gather.8.cloned.1.call-done = bf16[1536,512]{1,0:T(8,128)(2,1)} async-done(((bf16[192,512]{1,0:T(8,128)(2,1)}), bf16[1536,512]{1,0:T(8,128)(2,1)}) %all-gather.8.cloned.1.call-update) | async-done | bytes 1572880 | tf_op jit(solution)/shard_map/all_gather | solution.py:64
  228.6 2.1 gather_fusion.1
  230.6 1.4 broadcast_select_fusion.1
  (6 shorter events, 0.0 us)
Async XLA Ops:
  7.2 127.9 %copy-start = (bf16[192,512]{1,0:T(8,128)(2,1)S(1)}, bf16[192,512]{1,0:T(8,128)(2,1)}, u32[]{:S(2)}) copy-start(bf16[192,512]{1,0:T(8,128)(2,1)} %param.13) | copy-start | bytes 589828
  7.2 81.6 %reduce-scatter.2.cloned.1.call-start = ((), (), s32[]{:S(2)}) async-start(), calls=%async_computation.1 | async-start | bytes 3538944 | tf_op jit(solution)/shard_map/reduce_scatter | solution.py:34
  10.8 79.8 %copy-start.5 = (s32[8]{0:T(128)S(1)}, s32[8]{0:T(128)}, u32[]{:S(2)}) copy-start(s32[8]{0:T(128)} %param.9) | copy-start | bytes 100
  10.8 124.3 %all-gather.4.cloned.1.call-start = ((), (), s32[]{:S(2)}) async-start(), calls=%async_computation.2 | async-start | bytes 1769472 | tf_op jit(solution)/shard_map/all_gather | solution.py:37
  90.5 90.6 %all-gather.6.cloned.1.call-start = ((), (), s32[]{:S(2)}) async-start(), calls=%async_computation.3 | async-start | bytes 1769472 | tf_op jit(solution)/shard_map/all_gather | solution.py:60
  137.9 90.7 %all-gather.8.cloned.1.call-start = ((), (), s32[]{:S(2)}) async-start(), calls=%async_computation.4 | async-start | bytes 1769472 | tf_op jit(solution)/shard_map/all_gather | solution.py:64
  183.1 0.9 copy-start.4
  183.3 2.2 copy-start.3
  185.4 1.0 copy-start.1
  187.2 1.0 copy-start.2
Sparse Core Ops, SparseCore 0:
  11.6 77.1 reduce-scatter.1
  91.5 43.5 all-gather.3
  138.0 42.9 all-gather.5
  185.6 42.9 all-gather.7
where the time goes:
time: 239 us
  waiting for transfers between devices  204 us (85%)
  between operations  14.6 us (6%)
  other arithmetic  8.71 us (4%)
  matrix products  5.86 us (2%)
  local copies, waits for them, and re-layouts  5.58 us (2%)
    reduce_scatter x1, waiting for transfers between devices, shards(): lax.psum_scatter(partial_value.astype(jnp.float32), 'dp', scatter_dimensi...  77.9 us
    all_gather x1, waiting for transfers between devices, shards(): grad_full = lax.all_gather(even_rows, 'dp', axis=0, tiled=True)  43.1 us
    all_gather x1, waiting for transfers between devices, shards(): lax.all_gather(mixed_rows, 'dp', axis=0, tiled=True)  43.1 us
    all_gather x1, waiting for transfers between devices, shards(): lax.all_gather(direction_rows, 'dp', axis=0, tiled=True)  39.5 us
    dot_general x3, matrix products, against(): jnp.einsum('rk,bck->rbc', band_rows, blocks, preferred_element_type=jnp.f...  4.83 us
  transfers between devices with their start and end apart: 4, of which 4 were waited for; matrix products, arithmetic and copies ran while one was open for 2% of the time, Pallas kernels for 0%

commit v1 on v0

--- a/solution.py
+++ b/solution.py
@@ -1,9 +1,19 @@
+import functools
+
 import jax
 import jax.numpy as jnp
 from jax import lax
+from jax.experimental import pallas as pl
+from jax.experimental.pallas import tpu as pltpu
 from jax.sharding import PartitionSpec as P
 
 BETA = 0.95
+TILE = 64
+CHUNK = 32
+F32 = jnp.float32
+BF16 = jnp.bfloat16
+NT = (((1,), (1,)), ((), ()))
+VMEM_LIMIT = 40 * 1024 * 1024
 
 
 def against(band_rows, whole_rows, select):
@@ -19,7 +29,7 @@
     return jnp.take(shaped, owners, axis=0).reshape(gathered.shape)
 
 
-def shards(partial_grads, band_owner, left_factor, right_factor, left_root, right_root):
+def general(partial_grads, band_owner, left_factor, right_factor, left_root, right_root):
     members = lax.axis_size("dp")
     band_size = left_factor.shape[0]
     breadth = left_factor.shape[1]
@@ -66,10 +76,326 @@
     return (direction, left_updated, right_updated)
 
 
+def seat_of(device, n):
+    return jnp.where((device & 1) == 0, device >> 1, n - ((device + 1) >> 1))
+
+
+def device_at(seat, n):
+    seat = jnp.where(seat < 0, seat + n, seat)
+    seat = jnp.where(seat >= n, seat - n, seat)
+    return jnp.where(seat < n // 2, 2 * seat, 2 * (n - 1 - seat) + 1)
+
+
+def away(me, offset, n):
+    return device_at(seat_of(me, n) + offset, n)
+
+
+def band_of(owner_ref, device, n):
+    band = jnp.int32(0)
+    for k in range(n):
+        band = band + jnp.where(owner_ref[k] == device, k, 0)
+    return band
+
+
+def whole(*shape):
+    return pl.BlockSpec(shape, lambda i, *_: (0,) * len(shape))
+
+
+def params(limit=VMEM_LIMIT):
+    return pltpu.CompilerParams(vmem_limit_bytes=limit)
+
+
+def first_sends(me, partial, n):
+    band, breadth = partial.shape[1] // n, partial.shape[2]
+    half = band // 2
+
+    def kernel(me_ref, far_ref, right_ref, left_ref):
+        right_ref[...] = far_ref[0, :half]
+        left_ref[...] = far_ref[0, half:]
+
+    out = jax.ShapeDtypeStruct((half, breadth), BF16)
+    return pl.pallas_call(
+        kernel,
+        out_shape=(out, out),
+        grid_spec=pltpu.PrefetchScalarGridSpec(
+            num_scalar_prefetch=1,
+            grid=(1,),
+            in_specs=[
+                pl.BlockSpec((1, band, breadth), lambda i, m: (0, away(m[0], n // 2, n), 0)),
+            ],
+            out_specs=(whole(half, breadth), whole(half, breadth)),
+        ),
+        compiler_params=params(),
+        name="first_sends",
+    )(me, partial)
+
+
+def add_sends(me, partial, right, left, distance, n):
+    band, breadth = partial.shape[1] // n, partial.shape[2]
+    half = band // 2
+    rows = right.shape[0]
+
+    def kernel(me_ref, ahead_ref, behind_ref, r_ref, l_ref, right_ref, left_ref):
+        if rows == half:
+            right_ref[:half] = (ahead_ref[0, :half].astype(F32) + r_ref[...].astype(F32)).astype(BF16)
+            right_ref[half:] = ahead_ref[0, half:]
+            left_ref[half:] = (behind_ref[0, half:].astype(F32) + l_ref[...].astype(F32)).astype(BF16)
+            left_ref[:half] = behind_ref[0, :half]
+        else:
+            right_ref[...] = (ahead_ref[0].astype(F32) + r_ref[...].astype(F32)).astype(BF16)
+            left_ref[...] = (behind_ref[0].astype(F32) + l_ref[...].astype(F32)).astype(BF16)
+
+    out = jax.ShapeDtypeStruct((band, breadth), BF16)
+    return pl.pallas_call(
+        kernel,
+        out_shape=(out, out),
+        grid_spec=pltpu.PrefetchScalarGridSpec(
+            num_scalar_prefetch=1,
+            grid=(1,),
+            in_specs=[
+                pl.BlockSpec((1, band, breadth), lambda i, m: (0, away(m[0], distance, n), 0)),
+                pl.BlockSpec((1, band, breadth), lambda i, m: (0, away(m[0], -distance, n), 0)),
+                whole(rows, breadth),
+                whole(rows, breadth),
+            ],
+            out_specs=(whole(band, breadth), whole(band, breadth)),
+        ),
+        compiler_params=params(),
+        name="add_sends",
+    )(me, partial, partial, right, left)
+
+
+def add_own(me, partial, right, left, n):
+    band, breadth = partial.shape[1] // n, partial.shape[2]
+
+    def kernel(me_ref, own_ref, r_ref, l_ref, out_ref):
+        total = own_ref[0].astype(F32) + r_ref[...].astype(F32) + l_ref[...].astype(F32)
+        out_ref[...] = total.astype(BF16)
+
+    return pl.pallas_call(
+        kernel,
+        out_shape=jax.ShapeDtypeStruct((band, breadth), BF16),
+        grid_spec=pltpu.PrefetchScalarGridSpec(
+            num_scalar_prefetch=1,
+            grid=(1,),
+            in_specs=[
+                pl.BlockSpec((1, band, breadth), lambda i, m: (0, m[0], 0)),
+                whole(band, breadth),
+                whole(band, breadth),
+            ],
+            out_specs=whole(band, breadth),
+        ),
+        compiler_params=params(),
+        name="add_own",
+    )(me, partial, right, left)
+
+
+def kept(breadth):
+    return breadth // 2 + TILE
+
+
+def pack_roots(me, owner, left_root, right_root, n):
+    band, breadth = left_root.shape
+    tiles = breadth // TILE
+    width = kept(breadth)
+    edge = width - TILE
+
+    def kernel(me_ref, owner_ref, l_ref, r_ref, out_ref):
+        k = band_of(owner_ref, me_ref[0], n)
+        low = lax.broadcasted_iota(jnp.int32, (TILE, 2 * TILE), 1) < TILE
+        for row in range(0, band, TILE):
+            tile = ((k * band + row) // TILE) % tiles
+            rows = slice(row, row + TILE)
+            left = pltpu.roll(l_ref[rows].astype(F32), ((tiles - tile) % tiles) * TILE, 1)
+            right = pltpu.roll(r_ref[rows].astype(F32), ((tiles - tile + 1) % tiles) * TILE, 1)
+            out_ref[rows, :edge] = left[:, :edge].astype(BF16)
+            out_ref[rows, edge : edge + 2 * TILE] = jnp.where(
+                low, left[:, edge : edge + 2 * TILE], right[:, : 2 * TILE]
+            ).astype(BF16)
+            out_ref[rows, edge + 2 * TILE :] = right[:, 2 * TILE : width + TILE].astype(BF16)
+
+    return pl.pallas_call(
+        kernel,
+        out_shape=jax.ShapeDtypeStruct((band, 2 * width), BF16),
+        grid_spec=pltpu.PrefetchScalarGridSpec(
+            num_scalar_prefetch=2,
+            grid=(1,),
+            in_specs=[whole(band, breadth), whole(band, breadth)],
+            out_specs=whole(band, 2 * width),
+        ),
+        compiler_params=params(),
+        name="pack_roots",
+    )(me, owner, left_root, right_root)
+
+
+def unpack_roots(me, owner, pieces, stacked, breadth, n):
+    band = stacked // n
+    tiles = breadth // TILE
+    width = kept(breadth)
+    edge = width - TILE
+    nblocks = stacked // breadth
+
+    def kernel(me_ref, owner_ref, *refs):
+        refs, (left_ref, right_ref, half_l, half_r) = refs[: len(pieces)], refs[len(pieces) :]
+        span = edge + 2 * TILE
+        lane = lax.broadcasted_iota(jnp.int32, (CHUNK, span), 1)
+        rest = jnp.zeros((CHUNK, breadth - span), F32)
+        bands = {}
+        for (offset, first, _), ref in zip(pieces, refs):
+            if offset not in bands:
+                bands[offset] = band_of(owner_ref, away(me_ref[0], offset, n), n)
+            for row in range(0, ref.shape[0], CHUNK):
+                place = bands[offset] * band + first + row
+                tile = (place // TILE) % tiles
+                left = jnp.where(lane < width, ref[row : row + CHUNK, :span].astype(F32), 0.0)
+                left = pltpu.roll(jnp.concatenate([left, rest], 1), tile * TILE, 1)
+                right = jnp.where(lane >= TILE, ref[row : row + CHUNK, edge:].astype(F32), 0.0)
+                right = pltpu.roll(
+                    jnp.concatenate([right, rest], 1), ((tile + tiles - 1) % tiles) * TILE, 1
+                )
+                at = pl.ds(pl.multiple_of(place, CHUNK), CHUNK)
+                half_l[at, :] = left.astype(BF16)
+                half_r[at, :] = right.astype(BF16)
+        down = lax.broadcasted_iota(jnp.int32, (breadth, breadth), 0)
+        over = lax.broadcasted_iota(jnp.int32, (breadth, breadth), 1)
+        apart = (over // TILE - down // TILE + tiles) % tiles
+        mirrored = (apart > 0) & (apart < tiles // 2)
+        eye = (down == over).astype(BF16)
+        for half, out in ((half_l, left_ref), (half_r, right_ref)):
+            for b in range(nblocks):
+                rows = slice(b * breadth, (b + 1) * breadth)
+                upper = half[rows]
+                flipped = lax.dot_general(
+                    eye,
+                    jnp.where(mirrored, upper, jnp.zeros_like(upper)),
+                    NT,
+                    preferred_element_type=F32,
+                )
+                out[rows] = (upper.astype(F32) + flipped).astype(BF16)
+
+    out = jax.ShapeDtypeStruct((stacked, breadth), BF16)
+    return pl.pallas_call(
+        kernel,
+        out_shape=(out, out),
+        grid_spec=pltpu.PrefetchScalarGridSpec(
+            num_scalar_prefetch=2,
+            grid=(1,),
+            in_specs=[whole(*x.shape) for _, _, x in pieces],
+            out_specs=(whole(stacked, breadth), whole(stacked, breadth)),
+            scratch_shapes=[pltpu.VMEM((stacked, breadth), BF16)] * 2,
+        ),
+        compiler_params=params(),
+        name="unpack_roots",
+    )(me, owner, *[x for _, _, x in pieces])
+
+
+def finish(me, owner, pieces, left_root, right_root, left_factor, right_factor, n):
+    stacked, breadth = left_root.shape
+    band = stacked // n
+    nblocks = stacked // breadth
+
+    def kernel(me_ref, owner_ref, *refs):
+        parts, refs = refs[: len(pieces)], refs[len(pieces) :]
+        lroot, rroot, lfac, rfac, dir_ref, lout, rout, grad = refs
+        for (offset, first, _), ref in zip(pieces, parts):
+            place = away(me_ref[0], offset, n) * band + first
+            grad[pl.ds(pl.multiple_of(place, CHUNK), ref.shape[0]), :] = ref[...]
+        for b in range(nblocks):
+            rows = slice(b * breadth, (b + 1) * breadth)
+            mixed = jnp.dot(grad[rows], rroot[rows], preferred_element_type=F32).astype(BF16)
+            dir_ref[rows] = jnp.dot(lroot[rows], mixed, preferred_element_type=F32).astype(BF16)
+        start = band_of(owner_ref, me_ref[0], n) * band
+        mine = grad[pl.ds(pl.multiple_of(start, CHUNK), band), :]
+        first_block = start // breadth
+        last_block = (start + band - 1) // breadth
+        row = start + lax.broadcasted_iota(jnp.int32, (band, breadth), 0)
+        column = lax.broadcasted_iota(jnp.int32, (band, breadth), 1)
+
+        def terms(block):
+            g = grad[pl.ds(pl.multiple_of(block * breadth, breadth), breadth), :]
+            left = lax.dot_general(mine, g, NT, preferred_element_type=F32)
+            pick = (row - block * breadth == column).astype(BF16)
+            turned = lax.dot_general(pick, g, NT, preferred_element_type=F32).astype(BF16)
+            return left, jnp.dot(turned, g, preferred_element_type=F32)
+
+        left, right = terms(first_block)
+        lout[...] = BETA * lfac[...] + (1.0 - BETA) * left
+        rout[...] = BETA * rfac[...] + (1.0 - BETA) * right
+
+        @pl.when(last_block != first_block)
+        def _():
+            left, right = terms(last_block)
+            later = row >= last_block * breadth
+            lout[...] = jnp.where(later, BETA * lfac[...] + (1.0 - BETA) * left, lout[...])
+            rout[...] = jnp.where(later, BETA * rfac[...] + (1.0 - BETA) * right, rout[...])
+
+    own = jax.ShapeDtypeStruct((band, breadth), F32)
+    return pl.pallas_call(
+        kernel,
+        out_shape=(jax.ShapeDtypeStruct((stacked, breadth), BF16), own, own),
+        grid_spec=pltpu.PrefetchScalarGridSpec(
+            num_scalar_prefetch=2,
+            grid=(1,),
+            in_specs=[whole(*x.shape) for _, _, x in pieces]
+            + [whole(stacked, breadth)] * 2
+            + [whole(band, breadth)] * 2,
+            out_specs=(whole(stacked, breadth), whole(band, breadth), whole(band, breadth)),
+            scratch_shapes=[pltpu.VMEM((stacked, breadth), BF16)],
+        ),
+        compiler_params=params(),
+        name="finish",
+    )(me, owner, *[x for _, _, x in pieces], left_root, right_root, left_factor, right_factor)
+
+
+def ring(n, partial_grads, band_owner, left_factor, right_factor, left_root, right_root):
+    stacked, breadth = partial_grads.shape[1:]
+    band = stacked // n
+    half = band // 2
+    me = lax.axis_index("dp").astype(jnp.int32).reshape(1)
+    order = [2 * q for q in range(n // 2)] + [2 * (n - 1 - q) + 1 for q in range(n // 2, n)]
+    onward = [(order[q], order[(q + 1) % n]) for q in range(n)]
+    backward = [(b, a) for a, b in onward]
+
+    def send_right(x):
+        return lax.ppermute(x, "dp", onward)
+
+    def send_left(x):
+        return lax.ppermute(x, "dp", backward)
+
+    def gather(own):
+        pieces = [(0, 0, own)]
+        right, left = own, own
+        for hop in range(1, n // 2):
+            right, left = send_right(right), send_left(left)
+            pieces += [(-hop, 0, right), (hop, 0, left)]
+        cut = own.shape[0] // 2
+        pieces.append((n // 2, 0, send_right(right[:cut])))
+        pieces.append((n // 2, cut, send_left(left[cut:])))
+        return pieces
+
+    right, left = first_sends(me, partial_grads, n)
+    right, left = send_right(right), send_left(left)
+    for distance in range(n // 2 - 1, 0, -1):
+        right, left = add_sends(me, partial_grads, right, left, distance, n)
+        right, left = send_right(right), send_left(left)
+    own = add_own(me, partial_grads, right, left, n)
+    packed = pack_roots(me, band_owner, left_root, right_root, n)
+    roots = unpack_roots(me, band_owner, gather(packed), stacked, breadth, n)
+    return finish(me, band_owner, gather(own), *roots, left_factor, right_factor, n)
+
+
+def shards(n, partial_grads, *rest):
+    stacked, breadth = partial_grads.shape[1:]
+    band = stacked // n
+    if 4 <= n <= 16 and n % 2 == 0 and band % TILE == 0 and breadth % (4 * TILE) == 0:
+        return ring(n, partial_grads, *rest)
+    return general(partial_grads, *rest)
+
+
 def solution(mesh):
     placed = (P("dp", None, "mp"), P(), P("dp", "mp"), P("dp", "mp"), P("dp", "mp"), P("dp", "mp"))
     return jax.shard_map(
-        shards,
+        functools.partial(shards, mesh.shape["dp"]),
         mesh=mesh,
         in_specs=placed,
         out_specs=(P(None, "mp"), P("dp", "mp"), P("dp", "mp")),

time: 239 us -> 72.1 us (0.30)
  waiting for transfers between devices: 204 us -> 33.4 us
  starting transfers between devices: 0.16 us -> 26.3 us
  between operations: 14.6 us -> 0.79 us
  Pallas kernels: 0 us -> 10.4 us
  other arithmetic: 8.71 us -> 0 us
  matrix products: 5.86 us -> 0 us
  local copies, waits for them, and re-layouts: 5.58 us -> 1.47 us
    all_gather x3 -> x0, waiting for transfers between devices: 126 us -> none  [the longest x1 43.1 us: shards(): grad_full = lax.all_gather(even_rows, 'dp', axis=0, tiled=True)]
    reduce_scatter x1 -> x0, waiting for transfers between devices: 77.9 us -> none  [shards(): lax.psum_scatter(partial_value.astype(jnp.float32), 'dp', scatter_dimensi...]
    ppermute x0 -> x24, waiting for transfers between devices: none -> 33.4 us  [the longest x12 20.8 us: send_left(): return lax.ppermute(x, 'dp', backward)]
    ppermute x0 -> x24, starting transfers between devices: none -> 26.3 us  [the longest x12 24.1 us: send_right(): return lax.ppermute(x, 'dp', onward)]
    pallas_call x0 -> x8, Pallas kernels: none -> 10.4 us  [the longest x1 5.27 us: finish(): pl.pallas_call(kernel, out_shape=(jax.ShapeDtypeStruct((stacked, breadth)...]
    dot_general x4 -> x0, matrix products: 5.86 us -> none  [the longest x3 4.83 us: against(): jnp.einsum('rk,bck->rbc', band_rows, blocks, preferred_element_type=jnp.f...]
    convert_element_type x3 -> x0, other arithmetic: 5.25 us -> none  [the longest x1 3.55 us: shards(): partial_value.astype(jnp.float32)]
    gather x2 -> x0, local copies, waits for them, and re-layouts: 4.11 us -> none  [to_band_order(): return jnp.take(shaped, owners, axis=0).reshape(gathered.shape)]
  transfers between devices with their start and end apart: 4 -> 24, of which waited for: 4 -> 15; matrix products, arithmetic and copies ran while one was open for 2% -> 0% of each run, Pallas kernels for 0% -> 7%
where the time goes in v1:
time: 72.1 us; the launch traced here: 72.4 us
  waiting for transfers between devices  33.4 us (46%)
  starting transfers between devices  26.3 us (36%)
  Pallas kernels  10.4 us (14%)
  local copies, waits for them, and re-layouts  1.47 us (2%)
  between operations  0.79 us (1%)
    ppermute x12, starting transfers between devices, send_right(): return lax.ppermute(x, 'dp', onward)  24.1 us
    ppermute x12, waiting for transfers between devices, send_left(): return lax.ppermute(x, 'dp', backward)  20.8 us
    ppermute x12, waiting for transfers between devices, send_right(): return lax.ppermute(x, 'dp', onward)  12.5 us
    pallas_call x1, Pallas kernels, finish(): pl.pallas_call(kernel, out_shape=(jax.ShapeDtypeStruct((stacked, breadth)...  5.27 us
    pallas_call x1, Pallas kernels, unpack_roots(): pl.pallas_call(kernel, out_shape=(out, out), grid_spec=pltpu.PrefetchScal...  4.03 us
    ppermute x12, starting transfers between devices, send_left(): return lax.ppermute(x, 'dp', backward)  2.26 us
  transfers between devices with their start and end apart: 24, of which 15 were waited for; matrix products, arithmetic and copies ran while one was open for 0% of the time, Pallas kernels for 7%

profile of v1, /device:TPU:0, one launch (start us, length us, event | category | flops | bytes accessed | tf_op | source)
XLA Modules:
  0.0 72.4 jit_solution(18186770494936216000)
XLA Ops:
  0.6 0.0 copy-start
  0.6 1.4 %copy-done = bf16[1,1536,512]{2,1,0:T(8,128)(2,1)S(1)} copy-done((bf16[1,1536,512]{2,1,0:T(8,128)(2,1)S(1)}, bf16[1,1536,512]{2,1,0:T(8,128)(2,1)}, u32[]{:S(2)}) %copy-start) | copy-done | bytes 1572888
  2.1 3.1 %collective-permute-start = (bf16[96,512]{1,0:T(8,128)(2,1)S(1)}, bf16[96,512]{1,0:T(8,128)(2,1)S(1)}, u32[]{:S(2)}, u32[]{:S(2)}) collective-permute-start(bf16[96,512]{1,0:T(8,128)(2,1)S(1)} %get-tuple-element.13), channel_id=1, source_target_pairs={{0,8},{8,16},{16,24},{24,28},{28,20},{20,12},{12,4},{4,0},{1,9},{9... | collective-permute-start | bytes 294920 | tf_op jit(solution)/shard_map/ppermute | solution.py:360
  5.1 2.7 %collective-permute-done.r_ref = bf16[96,512]{1,0:T(8,128)(2,1)S(1)} collective-permute-done((bf16[96,512]{1,0:T(8,128)(2,1)S(1)}, bf16[96,512]{1,0:T(8,128)(2,1)S(1)}, u32[]{:S(2)}, u32[]{:S(2)}) %collective-permute-start) | collective-permute-done | bytes 98336 | tf_op jit(solution)/shard_map/ppermute | solution.py:360
  7.8 1.9 %collective-permute-done.1.l_ref = bf16[96,512]{1,0:T(8,128)(2,1)S(1)} collective-permute-done((bf16[96,512]{1,0:T(8,128)(2,1)S(1)}, bf16[96,512]{1,0:T(8,128)(2,1)S(1)}, u32[]{:S(2)}, u32[]{:S(2)}) %collective-permute-start.1) | collective-permute-done | bytes 98336 | tf_op jit(solution)/shard_map/ppermute | solution.py:363
  9.8 0.1 add_sends.3
  9.8 1.6 %collective-permute-start.2 = (bf16[192,512]{1,0:T(8,128)(2,1)S(1)}, bf16[192,512]{1,0:T(8,128)(2,1)S(1)}, u32[]{:S(2)}, u32[]{:S(2)}) collective-permute-start(bf16[192,512]{1,0:T(8,128)(2,1)S(1)} %get-tuple-element.15), channel_id=1, source_target_pairs={{0,8},{8,16},{16,24},{24,28},{28,20},{20,12},{12,4},{4,0},{1,9},{9... | collective-permute-start | bytes 589832 | tf_op jit(solution)/shard_map/ppermute | solution.py:360
  11.4 0.4 collective-permute-start.3
  11.9 3.6 %collective-permute-done.2.r_ref = bf16[192,512]{1,0:T(8,128)(2,1)S(1)} collective-permute-done((bf16[192,512]{1,0:T(8,128)(2,1)S(1)}, bf16[192,512]{1,0:T(8,128)(2,1)S(1)}, u32[]{:S(2)}, u32[]{:S(2)}) %collective-permute-start.2) | collective-permute-done | bytes 196640 | tf_op jit(solution)/shard_map/ppermute | solution.py:360
  15.5 1.6 %collective-permute-done.3.l_ref = bf16[192,512]{1,0:T(8,128)(2,1)S(1)} collective-permute-done((bf16[192,512]{1,0:T(8,128)(2,1)S(1)}, bf16[192,512]{1,0:T(8,128)(2,1)S(1)}, u32[]{:S(2)}, u32[]{:S(2)}) %collective-permute-start.3) | collective-permute-done | bytes 196640 | tf_op jit(solution)/shard_map/ppermute | solution.py:363
  17.1 0.1 add_sends.4
  17.2 1.6 %collective-permute-start.4 = (bf16[192,512]{1,0:T(8,128)(2,1)S(1)}, bf16[192,512]{1,0:T(8,128)(2,1)S(1)}, u32[]{:S(2)}, u32[]{:S(2)}) collective-permute-start(bf16[192,512]{1,0:T(8,128)(2,1)S(1)} %get-tuple-element.17), channel_id=1, source_target_pairs={{0,8},{8,16},{16,24},{24,28},{28,20},{20,12},{12,4},{4,0},{1,9},{9... | collective-permute-start | bytes 589832 | tf_op jit(solution)/shard_map/ppermute | solution.py:360
  18.9 0.5 collective-permute-start.5
  19.4 3.6 %collective-permute-done.4.r_ref = bf16[192,512]{1,0:T(8,128)(2,1)S(1)} collective-permute-done((bf16[192,512]{1,0:T(8,128)(2,1)S(1)}, bf16[192,512]{1,0:T(8,128)(2,1)S(1)}, u32[]{:S(2)}, u32[]{:S(2)}) %collective-permute-start.4) | collective-permute-done | bytes 196640 | tf_op jit(solution)/shard_map/ppermute | solution.py:360
  22.9 1.6 %collective-permute-done.5.l_ref = bf16[192,512]{1,0:T(8,128)(2,1)S(1)} collective-permute-done((bf16[192,512]{1,0:T(8,128)(2,1)S(1)}, bf16[192,512]{1,0:T(8,128)(2,1)S(1)}, u32[]{:S(2)}, u32[]{:S(2)}) %collective-permute-start.5) | collective-permute-done | bytes 196640 | tf_op jit(solution)/shard_map/ppermute | solution.py:363
  24.6 0.1 add_sends.5
  24.7 2.5 %collective-permute-start.6 = (bf16[192,512]{1,0:T(8,128)(2,1)S(1)}, bf16[192,512]{1,0:T(8,128)(2,1)S(1)}, u32[]{:S(2)}, u32[]{:S(2)}) collective-permute-start(bf16[192,512]{1,0:T(8,128)(2,1)S(1)} %get-tuple-element.19), channel_id=1, source_target_pairs={{0,8},{8,16},{16,24},{24,28},{28,20},{20,12},{12,4},{4,0},{1,9},{9... | collective-permute-start | bytes 589832 | tf_op jit(solution)/shard_map/ppermute | solution.py:360
  27.2 0.8 %pack_roots.1.refs_0_ = bf16[192,640]{1,0:T(8,128)(2,1)S(1)} custom-call(s32[1]{0:T(128)} %bitcast.me_ref, s32[8]{0:T(128)S(1)} %copy-done.6, bf16[192,512]{1,0:T(8,128)(2,1)S(1)} %copy-done.4, bf16[192,512]{1,0:T(8,128)(2,1)S(1)} %copy-done.5), custom_call_target="tpu_custom_call" | custom-call | tf_op jit(solution)/shard_map/pack_roots/pallas_call | solution.py:217
  28.0 0.1 collective-permute-start.17
  28.1 2.0 %collective-permute-start.16 = (bf16[192,640]{1,0:T(8,128)(2,1)S(1)}, bf16[192,640]{1,0:T(8,128)(2,1)S(1)}, u32[]{:S(2)}, u32[]{:S(2)}) collective-permute-start(bf16[192,640]{1,0:T(8,128)(2,1)S(1)} %pack_roots.1.refs_0_), channel_id=1, source_target_pairs={{0,8},{8,16},{16,24},{24,28},{28,20},{20,12},{12,4},{4,0},{1,9},{9... | collective-permute-start | bytes 737288 | tf_op jit(solution)/shard_map/ppermute | solution.py:360
  30.1 2.0 %collective-permute-done.6.r_ref = bf16[192,512]{1,0:T(8,128)(2,1)S(1)} collective-permute-done((bf16[192,512]{1,0:T(8,128)(2,1)S(1)}, bf16[192,512]{1,0:T(8,128)(2,1)S(1)}, u32[]{:S(2)}, u32[]{:S(2)}) %collective-permute-start.6) | collective-permute-done | bytes 196640 | tf_op jit(solution)/shard_map/ppermute | solution.py:360
  32.1 2.9 %collective-permute-done.7.l_ref = bf16[192,512]{1,0:T(8,128)(2,1)S(1)} collective-permute-done((bf16[192,512]{1,0:T(8,128)(2,1)S(1)}, bf16[192,512]{1,0:T(8,128)(2,1)S(1)}, u32[]{:S(2)}, u32[]{:S(2)}) %collective-permute-start.7) | collective-permute-done | bytes 196640 | tf_op jit(solution)/shard_map/ppermute | solution.py:363
  35.0 0.1 add_own.1.refs_0_
  35.1 0.0 copy-start.2
  35.1 0.0 copy-start.3
  35.1 0.1 collective-permute-start.9
  35.2 2.0 %collective-permute-start.8 = (bf16[192,512]{1,0:T(8,128)(2,1)S(1)}, bf16[192,512]{1,0:T(8,128)(2,1)S(1)}, u32[]{:S(2)}, u32[]{:S(2)}) collective-permute-start(bf16[192,512]{1,0:T(8,128)(2,1)S(1)} %add_own.1.refs_0_), channel_id=1, source_target_pairs={{0,8},{8,16},{16,24},{24,28},{28,20},{20,12},{12,4},{4,0},{1,9},{9... | collective-permute-start | bytes 589832 | tf_op jit(solution)/shard_map/ppermute | solution.py:360
  37.2 3.1 %collective-permute-done.17.refs_2_ = bf16[192,640]{1,0:T(8,128)(2,1)S(1)} collective-permute-done((bf16[192,640]{1,0:T(8,128)(2,1)S(1)}, bf16[192,640]{1,0:T(8,128)(2,1)S(1)}, u32[]{:S(2)}, u32[]{:S(2)}) %collective-permute-start.17) | collective-permute-done | bytes 245792 | tf_op jit(solution)/shard_map/ppermute | solution.py:363
  40.3 0.0 collective-permute-done.16.refs_1_
  40.3 2.0 %collective-permute-start.18 = (bf16[192,640]{1,0:T(8,128)(2,1)S(1)}, bf16[192,640]{1,0:T(8,128)(2,1)S(1)}, u32[]{:S(2)}, u32[]{:S(2)}) collective-permute-start(bf16[192,640]{1,0:T(8,128)(2,1)S(1)} %collective-permute-done.16.refs_1_), channel_id=1, source_target_pairs={{0,8},{8,16},{16,24},{24,28},{28,20},{20,12},{12,4},{4,0},{1,9},{9... | collective-permute-start | bytes 737288 | tf_op jit(solution)/shard_map/ppermute | solution.py:360
  42.3 2.2 %collective-permute-done.9.refs_2_ = bf16[192,512]{1,0:T(8,128)(2,1)S(1)} collective-permute-done((bf16[192,512]{1,0:T(8,128)(2,1)S(1)}, bf16[192,512]{1,0:T(8,128)(2,1)S(1)}, u32[]{:S(2)}, u32[]{:S(2)}) %collective-permute-start.9) | collective-permute-done | bytes 196640 | tf_op jit(solution)/shard_map/ppermute | solution.py:363
  44.5 0.0 collective-permute-start.11
  44.5 0.0 collective-permute-done.8.refs_1_
  44.5 2.0 %collective-permute-start.10 = (bf16[192,512]{1,0:T(8,128)(2,1)S(1)}, bf16[192,512]{1,0:T(8,128)(2,1)S(1)}, u32[]{:S(2)}, u32[]{:S(2)}) collective-permute-start(bf16[192,512]{1,0:T(8,128)(2,1)S(1)} %collective-permute-done.8.refs_1_), channel_id=1, source_target_pairs={{0,8},{8,16},{16,24},{24,28},{28,20},{20,12},{12,4},{4,0},{1,9},{9... | collective-permute-start | bytes 589832 | tf_op jit(solution)/shard_map/ppermute | solution.py:360
  46.5 3.2 %collective-permute-done.19.refs_4_ = bf16[192,640]{1,0:T(8,128)(2,1)S(1)} collective-permute-done((bf16[192,640]{1,0:T(8,128)(2,1)S(1)}, bf16[192,640]{1,0:T(8,128)(2,1)S(1)}, u32[]{:S(2)}, u32[]{:S(2)}) %collective-permute-start.19) | collective-permute-done | bytes 245792 | tf_op jit(solution)/shard_map/ppermute | solution.py:363
  49.8 2.0 %collective-permute-start.20 = (bf16[192,640]{1,0:T(8,128)(2,1)S(1)}, bf16[192,640]{1,0:T(8,128)(2,1)S(1)}, u32[]{:S(2)}, u32[]{:S(2)}) collective-permute-start(bf16[192,640]{1,0:T(8,128)(2,1)S(1)} %collective-permute-done.18.refs_3_), channel_id=1, source_target_pairs={{0,8},{8,16},{16,24},{24,28},{28,20},{20,12},{12,4},{4,0},{1,9},{9... | collective-permute-start | bytes 737288 | tf_op jit(solution)/shard_map/ppermute | solution.py:360
  51.8 2.1 %collective-permute-done.11.refs_4_ = bf16[192,512]{1,0:T(8,128)(2,1)S(1)} collective-permute-done((bf16[192,512]{1,0:T(8,128)(2,1)S(1)}, bf16[192,512]{1,0:T(8,128)(2,1)S(1)}, u32[]{:S(2)}, u32[]{:S(2)}) %collective-permute-start.11) | collective-permute-done | bytes 196640 | tf_op jit(solution)/shard_map/ppermute | solution.py:363
  53.8 0.1 collective-permute-start.13
  54.0 1.9 %collective-permute-start.12 = (bf16[192,512]{1,0:T(8,128)(2,1)S(1)}, bf16[192,512]{1,0:T(8,128)(2,1)S(1)}, u32[]{:S(2)}, u32[]{:S(2)}) collective-permute-start(bf16[192,512]{1,0:T(8,128)(2,1)S(1)} %collective-permute-done.10.refs_3_), channel_id=1, source_target_pairs={{0,8},{8,16},{16,24},{24,28},{28,20},{20,12},{12,4},{4,0},{1,9},{9... | collective-permute-start | bytes 589832 | tf_op jit(solution)/shard_map/ppermute | solution.py:360
  55.9 1.7 %collective-permute-done.21.refs_6_ = bf16[192,640]{1,0:T(8,128)(2,1)S(1)} collective-permute-done((bf16[192,640]{1,0:T(8,128)(2,1)S(1)}, bf16[192,640]{1,0:T(8,128)(2,1)S(1)}, u32[]{:S(2)}, u32[]{:S(2)}) %collective-permute-start.21) | collective-permute-done | bytes 245792 | tf_op jit(solution)/shard_map/ppermute | solution.py:363
  57.5 0.5 collective-permute-start.23
  58.1 1.6 %collective-permute-start.22 = (bf16[96,640]{1,0:T(8,128)(2,1)S(1)}, bf16[96,640]{1,0:T(8,128)(2,1)S(1)}, u32[]{:S(2)}, u32[]{:S(2)}) collective-permute-start(bf16[96,640]{1,0:T(8,128)(2,1)S(1)} %slice.18), channel_id=1, source_target_pairs={{0,8},{8,16},{16,24},{24,28},{28,20},{20,12},{12,4},{4,0},{1,9},{9... | collective-permute-start | bytes 368648 | tf_op jit(solution)/shard_map/ppermute | solution.py:360
  59.7 0.5 collective-permute-start.15
  60.2 1.6 %collective-permute-start.14 = (bf16[96,512]{1,0:T(8,128)(2,1)S(1)}, bf16[96,512]{1,0:T(8,128)(2,1)S(1)}, u32[]{:S(2)}, u32[]{:S(2)}) collective-permute-start(bf16[96,512]{1,0:T(8,128)(2,1)S(1)} %slice.16), channel_id=1, source_target_pairs={{0,8},{8,16},{16,24},{24,28},{28,20},{20,12},{12,4},{4,0},{1,9},{9... | collective-permute-start | bytes 294920 | tf_op jit(solution)/shard_map/ppermute | solution.py:360
  61.9 0.6 collective-permute-done.23.refs_8_
  62.5 0.5 collective-permute-done.22.refs_7_
  63.0 4.0 %unpack_roots.1 = (bf16[1536,512]{1,0:T(8,128)(2,1)S(1)}, bf16[1536,512]{1,0:T(8,128)(2,1)S(1)}) custom-call(s32[1]{0:T(128)} %bitcast.me_ref, s32[8]{0:T(128)S(1)} %copy-done.6, bf16[192,640]{1,0:T(8,128)(2,1)S(1)} %pack_roots.1.refs_0_, bf16[192,640]{1,0:T(8,128)(2,1)S(1)} %collective-permute-done.16.refs_1_, ...), custom_call_target="tpu_custom_call" | custom-call | tf_op jit(solution)/shard_map/unpack_roots/pallas_call | solution.py:277
  67.1 5.3 %finish.1 = (bf16[1536,512]{1,0:T(8,128)(2,1)}, f32[192,512]{1,0:T(8,128)}, f32[192,512]{1,0:T(8,128)}) custom-call(s32[1]{0:T(128)} %bitcast.me_ref, s32[8]{0:T(128)S(1)} %copy-done.6, bf16[192,512]{1,0:T(8,128)(2,1)S(1)} %add_own.1.refs_0_, bf16[192,512]{1,0:T(8,128)(2,1)S(1)} %collective-permute-done.8.refs_1_, ...), custom_call_target="tpu_custom_call" | custom-call | tf_op jit(solution)/shard_map/finish/pallas_call | solution.py:333
  (26 shorter events, 0.1 us)
Async XLA Ops:
  0.6 1.4 %copy-start = (bf16[1,1536,512]{2,1,0:T(8,128)(2,1)S(1)}, bf16[1,1536,512]{2,1,0:T(8,128)(2,1)}, u32[]{:S(2)}) copy-start(bf16[1,1536,512]{2,1,0:T(8,128)(2,1)} %own_ref.1) | copy-start | bytes 4718596
  2.1 5.8 %collective-permute-start = (bf16[96,512]{1,0:T(8,128)(2,1)S(1)}, bf16[96,512]{1,0:T(8,128)(2,1)S(1)}, u32[]{:S(2)}, u32[]{:S(2)}) collective-permute-start(bf16[96,512]{1,0:T(8,128)(2,1)S(1)} %get-tuple-element.13), channel_id=1, source_target_pairs={{0,8},{8,16},{16,24},{24,28},{28,20},{20,12},{12,4},{4,0},{1,9},{9... | collective-permute-start | bytes 294920 | tf_op jit(solution)/shard_map/ppermute | solution.py:360
  5.1 4.6 %collective-permute-start.1 = (bf16[96,512]{1,0:T(8,128)(2,1)S(1)}, bf16[96,512]{1,0:T(8,128)(2,1)S(1)}, u32[]{:S(2)}, u32[]{:S(2)}) collective-permute-start(bf16[96,512]{1,0:T(8,128)(2,1)S(1)} %get-tuple-element.14), channel_id=1, source_target_pairs={{8,0},{16,8},{24,16},{28,24},{20,28},{12,20},{4,12},{0,4},{9,1},{1... | collective-permute-start | bytes 294920 | tf_op jit(solution)/shard_map/ppermute | solution.py:363
  9.8 5.7 %collective-permute-start.2 = (bf16[192,512]{1,0:T(8,128)(2,1)S(1)}, bf16[192,512]{1,0:T(8,128)(2,1)S(1)}, u32[]{:S(2)}, u32[]{:S(2)}) collective-permute-start(bf16[192,512]{1,0:T(8,128)(2,1)S(1)} %get-tuple-element.15), channel_id=1, source_target_pairs={{0,8},{8,16},{16,24},{24,28},{28,20},{20,12},{12,4},{4,0},{1,9},{9... | collective-permute-start | bytes 589832 | tf_op jit(solution)/shard_map/ppermute | solution.py:360
  11.4 5.7 %collective-permute-start.3 = (bf16[192,512]{1,0:T(8,128)(2,1)S(1)}, bf16[192,512]{1,0:T(8,128)(2,1)S(1)}, u32[]{:S(2)}, u32[]{:S(2)}) collective-permute-start(bf16[192,512]{1,0:T(8,128)(2,1)S(1)} %get-tuple-element.16), channel_id=1, source_target_pairs={{8,0},{16,8},{24,16},{28,24},{20,28},{12,20},{4,12},{0,4},{9,1},{1... | collective-permute-start | bytes 589832 | tf_op jit(solution)/shard_map/ppermute | solution.py:363
  17.2 5.7 %collective-permute-start.4 = (bf16[192,512]{1,0:T(8,128)(2,1)S(1)}, bf16[192,512]{1,0:T(8,128)(2,1)S(1)}, u32[]{:S(2)}, u32[]{:S(2)}) collective-permute-start(bf16[192,512]{1,0:T(8,128)(2,1)S(1)} %get-tuple-element.17), channel_id=1, source_target_pairs={{0,8},{8,16},{16,24},{24,28},{28,20},{20,12},{12,4},{4,0},{1,9},{9... | collective-permute-start | bytes 589832 | tf_op jit(solution)/shard_map/ppermute | solution.py:360
  18.9 8.3 %copy-start.4 = (bf16[192,512]{1,0:T(8,128)(2,1)S(1)}, bf16[192,512]{1,0:T(8,128)(2,1)}, u32[]{:S(2)}) copy-start(bf16[192,512]{1,0:T(8,128)(2,1)} %l_ref.1) | copy-start | bytes 589828
  18.9 8.3 %copy-start.5 = (bf16[192,512]{1,0:T(8,128)(2,1)S(1)}, bf16[192,512]{1,0:T(8,128)(2,1)}, u32[]{:S(2)}) copy-start(bf16[192,512]{1,0:T(8,128)(2,1)} %r_ref.1) | copy-start | bytes 589828
  18.9 8.3 %copy-start.6 = (s32[8]{0:T(128)S(1)}, s32[8]{0:T(128)}, u32[]{:S(2)}) copy-start(s32[8]{0:T(128)} %owner_ref.5) | copy-start | bytes 100
  18.9 16.1 %copy-start.1 = (bf16[1,1536,512]{2,1,0:T(8,128)(2,1)S(1)}, bf16[1,1536,512]{2,1,0:T(8,128)(2,1)}, u32[]{:S(2)}) copy-start(bf16[1,1536,512]{2,1,0:T(8,128)(2,1)} %own_ref.1) | copy-start | bytes 4718596
  18.9 5.7 %collective-permute-start.5 = (bf16[192,512]{1,0:T(8,128)(2,1)S(1)}, bf16[192,512]{1,0:T(8,128)(2,1)S(1)}, u32[]{:S(2)}, u32[]{:S(2)}) collective-permute-start(bf16[192,512]{1,0:T(8,128)(2,1)S(1)} %get-tuple-element.18), channel_id=1, source_target_pairs={{8,0},{16,8},{24,16},{28,24},{20,28},{12,20},{4,12},{0,4},{9,1},{1... | collective-permute-start | bytes 589832 | tf_op jit(solution)/shard_map/ppermute | solution.py:363
  24.7 7.4 %collective-permute-start.6 = (bf16[192,512]{1,0:T(8,128)(2,1)S(1)}, bf16[192,512]{1,0:T(8,128)(2,1)S(1)}, u32[]{:S(2)}, u32[]{:S(2)}) collective-permute-start(bf16[192,512]{1,0:T(8,128)(2,1)S(1)} %get-tuple-element.19), channel_id=1, source_target_pairs={{0,8},{8,16},{16,24},{24,28},{28,20},{20,12},{12,4},{4,0},{1,9},{9... | collective-permute-start | bytes 589832 | tf_op jit(solution)/shard_map/ppermute | solution.py:360
  27.2 7.8 %collective-permute-start.7 = (bf16[192,512]{1,0:T(8,128)(2,1)S(1)}, bf16[192,512]{1,0:T(8,128)(2,1)S(1)}, u32[]{:S(2)}, u32[]{:S(2)}) collective-permute-start(bf16[192,512]{1,0:T(8,128)(2,1)S(1)} %get-tuple-element.20), channel_id=1, source_target_pairs={{8,0},{16,8},{24,16},{28,24},{20,28},{12,20},{4,12},{0,4},{9,1},{1... | collective-permute-start | bytes 589832 | tf_op jit(solution)/shard_map/ppermute | solution.py:363
  28.0 12.3 %collective-permute-start.17 = (bf16[192,640]{1,0:T(8,128)(2,1)S(1)}, bf16[192,640]{1,0:T(8,128)(2,1)S(1)}, u32[]{:S(2)}, u32[]{:S(2)}) collective-permute-start(bf16[192,640]{1,0:T(8,128)(2,1)S(1)} %pack_roots.1.refs_0_), channel_id=1, source_target_pairs={{8,0},{16,8},{24,16},{28,24},{20,28},{12,20},{4,12},{0,4},{9,1},{1... | collective-permute-start | bytes 737288 | tf_op jit(solution)/shard_map/ppermute | solution.py:363
  28.1 12.2 %collective-permute-start.16 = (bf16[192,640]{1,0:T(8,128)(2,1)S(1)}, bf16[192,640]{1,0:T(8,128)(2,1)S(1)}, u32[]{:S(2)}, u32[]{:S(2)}) collective-permute-start(bf16[192,640]{1,0:T(8,128)(2,1)S(1)} %pack_roots.1.refs_0_), channel_id=1, source_target_pairs={{0,8},{8,16},{16,24},{24,28},{28,20},{20,12},{12,4},{4,0},{1,9},{9... | collective-permute-start | bytes 737288 | tf_op jit(solution)/shard_map/ppermute | solution.py:360
  35.1 32.0 %copy-start.2 = (f32[192,512]{1,0:T(8,128)S(1)}, f32[192,512]{1,0:T(8,128)}, u32[]{:S(2)}) copy-start(f32[192,512]{1,0:T(8,128)} %refs_11_.1) | copy-start | bytes 1179652
  35.1 32.0 %copy-start.3 = (f32[192,512]{1,0:T(8,128)S(1)}, f32[192,512]{1,0:T(8,128)}, u32[]{:S(2)}) copy-start(f32[192,512]{1,0:T(8,128)} %refs_12_.1) | copy-start | bytes 1179652
  35.1 9.4 %collective-permute-start.9 = (bf16[192,512]{1,0:T(8,128)(2,1)S(1)}, bf16[192,512]{1,0:T(8,128)(2,1)S(1)}, u32[]{:S(2)}, u32[]{:S(2)}) collective-permute-start(bf16[192,512]{1,0:T(8,128)(2,1)S(1)} %add_own.1.refs_0_), channel_id=1, source_target_pairs={{8,0},{16,8},{24,16},{28,24},{20,28},{12,20},{4,12},{0,4},{9,1},{1... | collective-permute-start | bytes 589832 | tf_op jit(solution)/shard_map/ppermute | solution.py:363
  35.2 9.3 %collective-permute-start.8 = (bf16[192,512]{1,0:T(8,128)(2,1)S(1)}, bf16[192,512]{1,0:T(8,128)(2,1)S(1)}, u32[]{:S(2)}, u32[]{:S(2)}) collective-permute-start(bf16[192,512]{1,0:T(8,128)(2,1)S(1)} %add_own.1.refs_0_), channel_id=1, source_target_pairs={{0,8},{8,16},{16,24},{24,28},{28,20},{20,12},{12,4},{4,0},{1,9},{9... | collective-permute-start | bytes 589832 | tf_op jit(solution)/shard_map/ppermute | solution.py:360
  40.3 9.5 %collective-permute-start.19 = (bf16[192,640]{1,0:T(8,128)(2,1)S(1)}, bf16[192,640]{1,0:T(8,128)(2,1)S(1)}, u32[]{:S(2)}, u32[]{:S(2)}) collective-permute-start(bf16[192,640]{1,0:T(8,128)(2,1)S(1)} %collective-permute-done.17.refs_2_), channel_id=1, source_target_pairs={{8,0},{16,8},{24,16},{28,24},{20,28},{12,20},{4,12},{0,4},{9,1},{1... | collective-permute-start | bytes 737288 | tf_op jit(solution)/shard_map/ppermute | solution.py:363
  40.3 9.5 %collective-permute-start.18 = (bf16[192,640]{1,0:T(8,128)(2,1)S(1)}, bf16[192,640]{1,0:T(8,128)(2,1)S(1)}, u32[]{:S(2)}, u32[]{:S(2)}) collective-permute-start(bf16[192,640]{1,0:T(8,128)(2,1)S(1)} %collective-permute-done.16.refs_1_), channel_id=1, source_target_pairs={{0,8},{8,16},{16,24},{24,28},{28,20},{20,12},{12,4},{4,0},{1,9},{9... | collective-permute-start | bytes 737288 | tf_op jit(solution)/shard_map/ppermute | solution.py:360
  44.5 9.4 %collective-permute-start.11 = (bf16[192,512]{1,0:T(8,128)(2,1)S(1)}, bf16[192,512]{1,0:T(8,128)(2,1)S(1)}, u32[]{:S(2)}, u32[]{:S(2)}) collective-permute-start(bf16[192,512]{1,0:T(8,128)(2,1)S(1)} %collective-permute-done.9.refs_2_), channel_id=1, source_target_pairs={{8,0},{16,8},{24,16},{28,24},{20,28},{12,20},{4,12},{0,4},{9,1},{1... | collective-permute-start | bytes 589832 | tf_op jit(solution)/shard_map/ppermute | solution.py:363
  44.5 9.5 %collective-permute-start.10 = (bf16[192,512]{1,0:T(8,128)(2,1)S(1)}, bf16[192,512]{1,0:T(8,128)(2,1)S(1)}, u32[]{:S(2)}, u32[]{:S(2)}) collective-permute-start(bf16[192,512]{1,0:T(8,128)(2,1)S(1)} %collective-permute-done.8.refs_1_), channel_id=1, source_target_pairs={{0,8},{8,16},{16,24},{24,28},{28,20},{20,12},{12,4},{4,0},{1,9},{9... | collective-permute-start | bytes 589832 | tf_op jit(solution)/shard_map/ppermute | solution.py:360
  49.7 7.8 %collective-permute-start.21 = (bf16[192,640]{1,0:T(8,128)(2,1)S(1)}, bf16[192,640]{1,0:T(8,128)(2,1)S(1)}, u32[]{:S(2)}, u32[]{:S(2)}) collective-permute-start(bf16[192,640]{1,0:T(8,128)(2,1)S(1)} %collective-permute-done.19.refs_4_), channel_id=1, source_target_pairs={{8,0},{16,8},{24,16},{28,24},{20,28},{12,20},{4,12},{0,4},{9,1},{1... | collective-permute-start | bytes 737288 | tf_op jit(solution)/shard_map/ppermute | solution.py:363
  49.8 8.3 %collective-permute-start.20 = (bf16[192,640]{1,0:T(8,128)(2,1)S(1)}, bf16[192,640]{1,0:T(8,128)(2,1)S(1)}, u32[]{:S(2)}, u32[]{:S(2)}) collective-permute-start(bf16[192,640]{1,0:T(8,128)(2,1)S(1)} %collective-permute-done.18.refs_3_), channel_id=1, source_target_pairs={{0,8},{8,16},{16,24},{24,28},{28,20},{20,12},{12,4},{4,0},{1,9},{9... | collective-permute-start | bytes 737288 | tf_op jit(solution)/shard_map/ppermute | solution.py:360
  53.8 5.9 %collective-permute-start.13 = (bf16[192,512]{1,0:T(8,128)(2,1)S(1)}, bf16[192,512]{1,0:T(8,128)(2,1)S(1)}, u32[]{:S(2)}, u32[]{:S(2)}) collective-permute-start(bf16[192,512]{1,0:T(8,128)(2,1)S(1)} %collective-permute-done.11.refs_4_), channel_id=1, source_target_pairs={{8,0},{16,8},{24,16},{28,24},{20,28},{12,20},{4,12},{0,4},{9,1},{1... | collective-permute-start | bytes 589832 | tf_op jit(solution)/shard_map/ppermute | solution.py:363
  54.0 6.3 %collective-permute-start.12 = (bf16[192,512]{1,0:T(8,128)(2,1)S(1)}, bf16[192,512]{1,0:T(8,128)(2,1)S(1)}, u32[]{:S(2)}, u32[]{:S(2)}) collective-permute-start(bf16[192,512]{1,0:T(8,128)(2,1)S(1)} %collective-permute-done.10.refs_3_), channel_id=1, source_target_pairs={{0,8},{8,16},{16,24},{24,28},{28,20},{20,12},{12,4},{4,0},{1,9},{9... | collective-permute-start | bytes 589832 | tf_op jit(solution)/shard_map/ppermute | solution.py:360
  57.5 4.9 %collective-permute-start.23 = (bf16[96,640]{1,0:T(8,128)(2,1)S(1)}, bf16[96,640]{1,0:T(8,128)(2,1)S(1)}, u32[]{:S(2)}, u32[]{:S(2)}) collective-permute-start(bf16[96,640]{1,0:T(8,128)(2,1)S(1)} %slice.19), channel_id=1, source_target_pairs={{8,0},{16,8},{24,16},{28,24},{20,28},{12,20},{4,12},{0,4},{9,1},{1... | collective-permute-start | bytes 368648 | tf_op jit(solution)/shard_map/ppermute | solution.py:363
  58.1 4.9 %collective-permute-start.22 = (bf16[96,640]{1,0:T(8,128)(2,1)S(1)}, bf16[96,640]{1,0:T(8,128)(2,1)S(1)}, u32[]{:S(2)}, u32[]{:S(2)}) collective-permute-start(bf16[96,640]{1,0:T(8,128)(2,1)S(1)} %slice.18), channel_id=1, source_target_pairs={{0,8},{8,16},{16,24},{24,28},{28,20},{20,12},{12,4},{4,0},{1,9},{9... | collective-permute-start | bytes 368648 | tf_op jit(solution)/shard_map/ppermute | solution.py:360
  59.7 7.3 %collective-permute-start.15 = (bf16[96,512]{1,0:T(8,128)(2,1)S(1)}, bf16[96,512]{1,0:T(8,128)(2,1)S(1)}, u32[]{:S(2)}, u32[]{:S(2)}) collective-permute-start(bf16[96,512]{1,0:T(8,128)(2,1)S(1)} %slice.17), channel_id=1, source_target_pairs={{8,0},{16,8},{24,16},{28,24},{20,28},{12,20},{4,12},{0,4},{9,1},{1... | collective-permute-start | bytes 294920 | tf_op jit(solution)/shard_map/ppermute | solution.py:363
  60.2 6.8 %collective-permute-start.14 = (bf16[96,512]{1,0:T(8,128)(2,1)S(1)}, bf16[96,512]{1,0:T(8,128)(2,1)S(1)}, u32[]{:S(2)}, u32[]{:S(2)}) collective-permute-start(bf16[96,512]{1,0:T(8,128)(2,1)S(1)} %slice.16), channel_id=1, source_target_pairs={{0,8},{8,16},{16,24},{24,28},{28,20},{20,12},{12,4},{4,0},{1,9},{9... | collective-permute-start | bytes 294920 | tf_op jit(solution)/shard_map/ppermute | solution.py:360

commit v2 on v1

v2 whole, which is shorter than its diff:
```python
import functools

import jax
import jax.numpy as jnp
from jax import lax
from jax.experimental import pallas as pl
from jax.experimental.pallas import tpu as pltpu
from jax.sharding import PartitionSpec as P

BETA = 0.95
TILE = 64
CHUNK = 32
GRAD_PARTS = 2
F32 = jnp.float32
BF16 = jnp.bfloat16
NT = (((1,), (1,)), ((), ()))
TN = (((0,), (0,)), ((), ()))
VMEM_LIMIT = 40 * 1024 * 1024
OPEN_LIMIT = 62 * 1024 * 1024


def against(band_rows, whole_rows, select):
    nblocks = select.shape[1]
    breadth = whole_rows.shape[1]
    blocks = whole_rows.reshape(nblocks, breadth, breadth)
    products = jnp.einsum("rk,bck->rbc", band_rows, blocks, preferred_element_type=jnp.float32)
    return jnp.sum(select[:, :, None] * products, axis=1)


def to_band_order(gathered, owners, members):
    shaped = gathered.reshape(members, -1, gathered.shape[1])
    return jnp.take(shaped, owners, axis=0).reshape(gathered.shape)


def general(partial_grads, band_owner, left_factor, right_factor, left_root, right_root):
    members = lax.axis_size("dp")
    band_size = left_factor.shape[0]
    breadth = left_factor.shape[1]
    stacked = partial_grads.shape[1]
    nblocks = stacked // breadth
    devices = jnp.arange(members, dtype=jnp.int32)
    inverse = jnp.sum(
        jnp.where(band_owner[None, :] == devices[:, None], devices[None, :], 0), axis=1
    )
    own_band = inverse[lax.axis_index("dp")]
    partial_value = partial_grads[0]
    even_rows = lax.psum_scatter(
        partial_value.astype(jnp.float32), "dp", scatter_dimension=0, tiled=True
    ).astype(jnp.bfloat16)
    grad_full = lax.all_gather(even_rows, "dp", axis=0, tiled=True)
    grad_rows = lax.dynamic_slice_in_dim(grad_full, own_band * band_size, band_size, 0)
    global_rows = own_band * band_size + jnp.arange(band_size, dtype=jnp.int32)
    block_ids = global_rows // breadth
    within = global_rows % breadth
    block_range = jnp.arange(nblocks, dtype=jnp.int32)
    select = (block_ids[:, None] == block_range[None, :]).astype(jnp.float32)
    left_term = against(grad_rows, grad_full, select)
    left_updated = BETA * left_factor + (1.0 - BETA) * left_term
    column_range = jnp.arange(breadth, dtype=jnp.int32)
    onehot = (
        (block_range[:, None, None] == block_ids[None, None, :])
        & (column_range[None, :, None] == within[None, None, :])
    ).astype(jnp.bfloat16)
    blocks = grad_full.reshape(nblocks, breadth, breadth)
    columns = jnp.einsum("bkc,bcr->kr", blocks, onehot, preferred_element_type=jnp.float32).astype(
        jnp.bfloat16
    )
    right_products = jnp.einsum("kr,bkc->rbc", columns, blocks, preferred_element_type=jnp.float32)
    right_term = jnp.sum(select[:, :, None] * right_products, axis=1)
    right_updated = BETA * right_factor + (1.0 - BETA) * right_term
    mixed_rows = against(right_root, grad_full, select).astype(jnp.bfloat16)
    mixed_full = to_band_order(
        lax.all_gather(mixed_rows, "dp", axis=0, tiled=True), band_owner, members
    )
    direction_rows = against(left_root, mixed_full, select).astype(jnp.bfloat16)
    direction = to_band_order(
        lax.all_gather(direction_rows, "dp", axis=0, tiled=True), band_owner, members
    )
    return (direction, left_updated, right_updated)


def seat_of(device, n):
    return jnp.where((device & 1) == 0, device >> 1, n - ((device + 1) >> 1))


def device_at(seat, n):
    seat = jnp.where(seat < 0, seat + n, seat)
    seat = jnp.where(seat >= n, seat - n, seat)
    return jnp.where(seat < n // 2, 2 * seat, 2 * (n - 1 - seat) + 1)


def away(me, offset, n):
    return device_at(seat_of(me, n) + offset, n)


def band_of(owner_ref, device, n):
    band = jnp.int32(0)
    for k in range(n):
        band = band + jnp.where(owner_ref[k] == device, k, 0)
    return band


def whole(*shape):
    return pl.BlockSpec(shape, lambda i, *_: (0,) * len(shape))


def params(limit=VMEM_LIMIT):
    return pltpu.CompilerParams(vmem_limit_bytes=limit)


def add_send(me, partial, arrived, distance, n, first, *after):
    band, breadth = partial.shape[1] // n, partial.shape[2]
    rows = arrived.shape[0]

    def kernel(me_ref, own_ref, a_ref, *refs):
        out_ref = refs[-1]
        if rows == band:
            out_ref[...] = (own_ref[0].astype(F32) + a_ref[...].astype(F32)).astype(BF16)
        else:
            got, other = slice(first, first + rows), slice(rows - first, band - first)
            out_ref[got] = (own_ref[0, got].astype(F32) + a_ref[...].astype(F32)).astype(BF16)
            out_ref[other] = own_ref[0, other]

    return pl.pallas_call(
        kernel,
        out_shape=jax.ShapeDtypeStruct((band, breadth), BF16),
        grid_spec=pltpu.PrefetchScalarGridSpec(
            num_scalar_prefetch=1,
            grid=(1,),
            in_specs=[
                pl.BlockSpec((1, band, breadth), lambda i, m: (0, away(m[0], distance, n), 0)),
                whole(rows, breadth),
            ]
            + [pl.BlockSpec(memory_space=pl.ANY)] * len(after),
            out_specs=whole(band, breadth),
        ),
        compiler_params=params(),
        name="add_send",
    )(me, partial, arrived, *after)


def add_own(me, partial, right, left, n, *after):
    band, breadth = partial.shape[1] // n, partial.shape[2]

    def kernel(me_ref, own_ref, r_ref, l_ref, *refs):
        out_ref = refs[-1]
        total = own_ref[0].astype(F32) + r_ref[...].astype(F32) + l_ref[...].astype(F32)
        out_ref[...] = total.astype(BF16)

    return pl.pallas_call(
        kernel,
        out_shape=jax.ShapeDtypeStruct((band, breadth), BF16),
        grid_spec=pltpu.PrefetchScalarGridSpec(
            num_scalar_prefetch=1,
            grid=(1,),
            in_specs=[
                pl.BlockSpec((1, band, breadth), lambda i, m: (0, m[0], 0)),
                whole(band, breadth),
                whole(band, breadth),
            ]
            + [pl.BlockSpec(memory_space=pl.ANY)] * len(after),
            out_specs=whole(band, breadth),
        ),
        compiler_params=params(),
        name="add_own",
    )(me, partial, right, left, *after)


PAIR = 2 * TILE


def kept(breadth):
    return breadth // 2 + TILE


def pairs_of(tile, breadth):
    pairs = breadth // PAIR
    odd = tile & 1
    whole_pair = (tile + odd) >> 1
    half_pair = whole_pair + pairs // 2 + (pairs // 2 - 1) * odd
    return whole_pair, half_pair, odd == 0


def lanes(pair, breadth):
    return pl.ds(pl.multiple_of((pair & (breadth // PAIR - 1)) * PAIR, PAIR), PAIR)


def open_ring(me, owner, partial, left_root, right_root, n):
    band, breadth = left_root.shape
    half = band // 2
    tiles = breadth // TILE
    whole_pairs = tiles // 4
    width = kept(breadth)

    def kernel(me_ref, owner_ref, p_ref, lr_ref, rr_ref, right_ref, left_ref, out_ref, l_ref, r_ref, sems):
        start = away(me_ref[0], n // 2, n) * band
        copies = [
            pltpu.make_async_copy(lr_ref, l_ref, sems.at[0]),
            pltpu.make_async_copy(rr_ref, r_ref, sems.at[1]),
            pltpu.make_async_copy(
                p_ref.at[0, pl.ds(pl.multiple_of(start, half), half)], right_ref, sems.at[2]
            ),
            pltpu.make_async_copy(
                p_ref.at[0, pl.ds(pl.multiple_of(start + half, half), half)], left_ref, sems.at[3]
            ),
        ]
        for copy in copies:
            copy.start()
        k = band_of(owner_ref, me_ref[0], n)
        low = lax.broadcasted_iota(jnp.int32, (TILE, PAIR), 1) < TILE
        copies[0].wait()
        copies[1].wait()
        for row in range(0, band, TILE):
            tile = (k * (band // TILE) + row // TILE) & (tiles - 1)
            first, half_pair, even = pairs_of(tile, breadth)
            rows = slice(row, row + TILE)
            for i in range(whole_pairs):
                pair = lanes(first + i, breadth)
                out_ref[rows, i * PAIR : (i + 1) * PAIR] = l_ref[rows, pair]
                out_ref[rows, (whole_pairs + i) * PAIR : (whole_pairs + i + 1) * PAIR] = r_ref[rows, pair]
            left = l_ref[rows, lanes(half_pair, breadth)].astype(F32)
            right = pltpu.roll(r_ref[rows, lanes(half_pair, breadth)].astype(F32), TILE, 1)
            mine = jnp.where(low == even, left, right)
            out_ref[rows, 2 * whole_pairs * PAIR :] = mine.astype(BF16)
        copies[2].wait()
        copies[3].wait()

    sent = jax.ShapeDtypeStruct((half, breadth), BF16)
    return pl.pallas_call(
        kernel,
        out_shape=(sent, sent, jax.ShapeDtypeStruct((band, 2 * width), BF16)),
        grid_spec=pltpu.PrefetchScalarGridSpec(
            num_scalar_prefetch=2,
            grid=(1,),
            in_specs=[pl.BlockSpec(memory_space=pltpu.HBM)] * 3,
            out_specs=(whole(half, breadth), whole(half, breadth), whole(band, 2 * width)),
            scratch_shapes=[pltpu.VMEM((band, breadth), BF16)] * 2 + [pltpu.SemaphoreType.DMA((4,))],
        ),
        compiler_params=params(OPEN_LIMIT),
        name="open_ring",
    )(me, owner, partial, left_root, right_root)


def unpack_roots(me, owner, pieces, stacked, breadth, n):
    band = stacked // n
    tiles = breadth // TILE
    whole_pairs = tiles // 4
    nblocks = stacked // breadth

    def kernel(me_ref, owner_ref, *refs):
        refs, (left_ref, right_ref, half_l, half_r) = refs[: len(pieces)], refs[len(pieces) :]
        lower = lax.broadcasted_iota(jnp.int32, (TILE, PAIR), 1) < TILE
        nothing = jnp.zeros((TILE, PAIR), BF16)
        bands = {}
        for (offset, first, _), ref in zip(pieces, refs):
            if offset not in bands:
                bands[offset] = band_of(owner_ref, away(me_ref[0], offset, n), n)
            edges = sorted({first, first + ref.shape[0], *range(0, band + 1, TILE)})
            edges = [x for x in edges if first <= x <= first + ref.shape[0]]
            for row, end in zip(edges[:-1], edges[1:]):
                tile = (bands[offset] * (band // TILE) + row // TILE) & (tiles - 1)
                start, half_pair, even = pairs_of(tile, breadth)
                at = pl.ds(pl.multiple_of(bands[offset] * band + row, CHUNK), end - row)
                rows = slice(row - first, end - first)
                low = lower[: end - row]
                zeros = nothing[: end - row]
                shared = ref[rows, 2 * whole_pairs * PAIR :].astype(F32)
                left = jnp.where(low == even, shared, 0.0).astype(BF16)
                right = jnp.where(low == even, pltpu.roll(shared, TILE, 1), 0.0).astype(BF16)
                for i in range(2 * whole_pairs):
                    pair = lanes(start + i, breadth)
                    if i < whole_pairs:
                        half_l[at, pair] = ref[rows, i * PAIR : (i + 1) * PAIR]
                        half_r[at, pair] = ref[
                            rows, (whole_pairs + i) * PAIR : (whole_pairs + i + 1) * PAIR
                        ]
                    else:
                        half_l[at, pair] = zeros
                        half_r[at, pair] = zeros
                half_l[at, lanes(half_pair, breadth)] = left
                half_r[at, lanes(half_pair, breadth)] = right
        shift = TILE.bit_length() - 1
        down = lax.broadcasted_iota(jnp.int32, (breadth, breadth), 0) >> shift
        over = lax.broadcasted_iota(jnp.int32, (breadth, breadth), 1) >> shift
        apart = over - down + jnp.where(over < down, tiles, 0)
        mirrored = (apart > 0) & (apart < tiles // 2)
        for half, out in ((half_r, right_ref), (half_l, left_ref)):
            for b in range(nblocks):
                rows = slice(b * breadth, (b + 1) * breadth)
                upper = half[rows]
                out[rows] = upper + jnp.where(mirrored, upper, jnp.zeros_like(upper)).T

    out = jax.ShapeDtypeStruct((stacked, breadth), BF16)
    return pl.pallas_call(
        kernel,
        out_shape=(out, out),
        grid_spec=pltpu.PrefetchScalarGridSpec(
            num_scalar_prefetch=2,
            grid=(1,),
            in_specs=[whole(*x.shape) for _, _, x in pieces],
            out_specs=(whole(stacked, breadth), whole(stacked, breadth)),
            scratch_shapes=[pltpu.VMEM((stacked, breadth), BF16)] * 2,
        ),
        compiler_params=params(),
        name="unpack_roots",
    )(me, owner, *[x for _, _, x in pieces])


def begin(me, pieces, left_root, right_root, n):
    stacked, breadth = left_root.shape
    band = stacked // n
    nblocks = stacked // breadth

    def kernel(me_ref, *refs):
        parts, refs = refs[: len(pieces)], refs[len(pieces) :]
        lroot, rroot, dir_ref, grad, rest_ref = refs
        for (offset, first, _), ref in zip(pieces, parts):
            place = away(me_ref[0], offset, n) * band + first
            grad[pl.ds(pl.multiple_of(place, CHUNK), ref.shape[0]), :] = ref[...]
        start = away(me_ref[0], n // 2, n) * band
        grad[pl.ds(pl.multiple_of(start, CHUNK), band), :] = jnp.zeros((band, breadth), BF16)
        for b in range(nblocks):
            rows = slice(b * breadth, (b + 1) * breadth)
            mixed = jnp.dot(grad[rows], rroot[rows], preferred_element_type=F32).astype(BF16)
            block = jnp.dot(lroot[rows], mixed, preferred_element_type=F32)
            dir_ref[rows] = block.astype(BF16)
            for slot, at in enumerate((start, start + band - 1)):

                @pl.when(at >> (breadth.bit_length() - 1) == b)
                def _():
                    rest_ref[slot] = block

    return pl.pallas_call(
        kernel,
        out_shape=(
            jax.ShapeDtypeStruct((stacked, breadth), BF16),
            jax.ShapeDtypeStruct((stacked, breadth), BF16),
            jax.ShapeDtypeStruct((2, breadth, breadth), F32),
        ),
        grid_spec=pltpu.PrefetchScalarGridSpec(
            num_scalar_prefetch=1,
            grid=(1,),
            in_specs=[whole(*x.shape) for _, _, x in pieces] + [whole(stacked, breadth)] * 2,
            out_specs=(
                whole(stacked, breadth),
                whole(stacked, breadth),
                whole(2, breadth, breadth),
            ),
        ),
        compiler_params=params(),
        name="begin",
    )(me, *[x for _, _, x in pieces], left_root, right_root)


def finish(me, owner, pieces, directions, grad, rest, left_root, right_root, left_factor, right_factor, n):
    stacked, breadth = left_root.shape
    band = stacked // n

    def kernel(me_ref, owner_ref, *refs):
        parts, refs = refs[: len(pieces)], refs[len(pieces) :]
        _, grad_ref, rest_ref, lroot, rroot, lfac, rfac, *refs = refs
        dir_ref, lout_ref, rout_ref, late, block, lout, rout, sems = refs
        far = away(me_ref[0], n // 2, n) * band
        for (_, first, _), ref in zip(pieces, parts):
            late[first : first + ref.shape[0]] = ref[...]
        shift = breadth.bit_length() - 1
        row = (far + lax.broadcasted_iota(jnp.int32, (band, breadth), 0)) >> shift
        there = pl.ds(pl.multiple_of(far, CHUNK), band)
        first_block = far >> shift
        last_block = (far + band - 1) >> shift

        def span(number):
            return pl.ds(pl.multiple_of(number * breadth, breadth), breadth)

        def copy(slot, number):
            return pltpu.make_async_copy(block.at[slot], dir_ref.at[span(number)], sems.at[slot])

        def complete(slot, number):
            some = jnp.where(row == number, late[...].astype(F32), 0.0).astype(BF16)
            mixed = jnp.dot(some, rroot[span(number), :], preferred_element_type=F32).astype(BF16)
            more = lax.dot_general(lroot[there, :], mixed, TN, preferred_element_type=F32)
            block[slot] = (rest_ref[slot] + more).astype(BF16)
            copy(slot, number).start()

        complete(0, first_block)

        @pl.when(last_block != first_block)
        def _():
            complete(1, last_block)

        start = band_of(owner_ref, me_ref[0], n) * band
        grad_ref[there, :] = late[...]
        mine = grad_ref[pl.ds(pl.multiple_of(start, CHUNK), band), :]
        own_first = start >> shift
        own_last = (start + band - 1) >> shift
        own_row = start + lax.broadcasted_iota(jnp.int32, (band, breadth), 0)
        column = lax.broadcasted_iota(jnp.int32, (band, breadth), 1)

        def left_term(number):
            return lax.dot_general(mine, grad_ref[span(number), :], NT, preferred_element_type=F32)

        def right_term(number):
            g = grad_ref[span(number), :]
            pick = (own_row - number * breadth == column).astype(BF16)
            turned = lax.dot_general(pick, g, NT, preferred_element_type=F32).astype(BF16)
            return jnp.dot(turned, g, preferred_element_type=F32)

        later = own_row >= own_last * breadth
        outs = []
        for slot, (term, fac, out, ref) in enumerate(
            ((left_term, lfac, lout, lout_ref), (right_term, rfac, rout, rout_ref))
        ):
            out[...] = BETA * fac[...] + (1.0 - BETA) * term(own_first)

            @pl.when(own_last != own_first)
            def _():
                new = BETA * fac[...] + (1.0 - BETA) * term(own_last)
                out[...] = jnp.where(later, new, out[...])

            outs.append(pltpu.make_async_copy(out, ref, sems.at[2 + slot]))
            outs[-1].start()
        copy(0, first_block).wait()

        @pl.when(last_block != first_block)
        def _():
            copy(1, last_block).wait()

        for out in outs:
            out.wait()

    own = jax.ShapeDtypeStruct((band, breadth), F32)
    return pl.pallas_call(
        kernel,
        out_shape=(jax.ShapeDtypeStruct((stacked, breadth), BF16), own, own),
        grid_spec=pltpu.PrefetchScalarGridSpec(
            num_scalar_prefetch=2,
            grid=(1,),
            in_specs=[whole(*x.shape) for _, _, x in pieces]
            + [pl.BlockSpec(memory_space=pl.ANY), whole(stacked, breadth), whole(2, breadth, breadth)]
            + [whole(stacked, breadth)] * 2
            + [whole(band, breadth)] * 2,
            out_specs=[pl.BlockSpec(memory_space=pl.ANY)] * 3,
            scratch_shapes=[
                pltpu.VMEM((band, breadth), BF16),
                pltpu.VMEM((2, breadth, breadth), BF16),
                pltpu.VMEM((band, breadth), F32),
                pltpu.VMEM((band, breadth), F32),
                pltpu.SemaphoreType.DMA((4,)),
            ],
        ),
        input_output_aliases={2 + len(pieces): 0},
        compiler_params=params(),
        name="finish",
    )(
        me,
        owner,
        *[x for _, _, x in pieces],
        directions,
        grad,
        rest,
        left_root,
        right_root,
        left_factor,
        right_factor,
    )


def ring(n, partial_grads, band_owner, left_factor, right_factor, left_root, right_root):
    stacked, breadth = partial_grads.shape[1:]
    band = stacked // n
    half = band // 2
    me = lax.axis_index("dp").astype(jnp.int32).reshape(1)
    order = [2 * q for q in range(n // 2)] + [2 * (n - 1 - q) + 1 for q in range(n // 2, n)]
    onward = [(order[q], order[(q + 1) % n]) for q in range(n)]
    backward = [(b, a) for a, b in onward]

    def send_right(x):
        return lax.ppermute(x, "dp", onward)

    def send_left(x):
        return lax.ppermute(x, "dp", backward)

    def gather(own, parts):
        rows = own.shape[0] // 2
        pieces = [(0, 0, own)]
        if parts == 1:
            right, left = own, own
            for hop in range(1, n // 2):
                right, left = send_right(right), send_left(left)
                pieces += [(-hop, 0, right), (hop, 0, left)]
            right, left = send_right(right[:rows]), send_left(left[rows:])
        else:
            upper, lower = own[:rows], own[rows:]
            ways = [upper, upper, lower, lower]
            for hop in range(1, n // 2):
                ways = [
                    send_right(ways[0]),
                    send_left(ways[1]),
                    send_right(ways[2]),
                    send_left(ways[3]),
                ]
                pieces += [(-hop, 0, ways[0]), (hop, 0, ways[1])]
                pieces += [(-hop, rows, ways[2]), (hop, rows, ways[3])]
            right, left = send_right(ways[0]), send_left(ways[3])
        return pieces + [(n // 2, 0, right), (n // 2, rows, left)]

    right, left, packed = open_ring(me, band_owner, partial_grads, left_root, right_root, n)
    right, left = send_right(right), send_left(left)
    root_pieces = gather(packed, 1)
    for distance in range(n // 2 - 1, 0, -1):
        right = add_send(me, partial_grads, right, distance, n, 0)
        left = add_send(me, partial_grads, left, -distance, n, half if left.shape[0] == half else 0)
        right, left = send_right(right), send_left(left)
    roots = unpack_roots(me, band_owner, root_pieces, stacked, breadth, n)
    own = add_own(me, partial_grads, right, left, n)
    pieces = gather(own, GRAD_PARTS)
    begun = begin(me, pieces[:-2], *roots, n)
    return finish(me, band_owner, pieces[-2:], *begun, *roots, left_factor, right_factor, n)


def shards(n, partial_grads, *rest):
    stacked, breadth = partial_grads.shape[1:]
    band = stacked // n
    fits = band % TILE == 0 and breadth % (4 * TILE) == 0 and breadth & (breadth - 1) == 0
    if 4 <= n <= 16 and n % 2 == 0 and fits:
        return ring(n, partial_grads, *rest)
    return general(partial_grads, *rest)


def solution(mesh):
    placed = (P("dp", None, "mp"), P(), P("dp", "mp"), P("dp", "mp"), P("dp", "mp"), P("dp", "mp"))
    return jax.shard_map(
        functools.partial(shards, mesh.shape["dp"]),
        mesh=mesh,
        in_specs=placed,
        out_specs=(P(None, "mp"), P("dp", "mp"), P("dp", "mp")),
        check_vma=False,
    )
```

time: 72.1 us -> 66.8 us (0.926)
  waiting for transfers between devices: 33.4 us -> 20.3 us
  starting transfers between devices: 26.3 us -> 33.3 us
  Pallas kernels: 10.4 us -> 12.1 us
  local copies, waits for them, and re-layouts: 1.47 us -> 0.07 us
    ppermute x12 -> x15, starting transfers between devices: 2.26 us -> 27.9 us  [send_left(): return lax.ppermute(x, 'dp', backward)]
    ppermute x12 -> x15, starting transfers between devices: 24.1 us -> 5.46 us  [send_right(): return lax.ppermute(x, 'dp', onward)]
    ppermute x12 -> x15, waiting for transfers between devices: 12.5 us -> 2.74 us  [send_right(): return lax.ppermute(x, 'dp', onward)]
    pallas_call x5 -> x8, Pallas kernels: 1.05 us -> 6.76 us  [the longest x1 3.74 us: begin(): pl.pallas_call(kernel, out_shape=(jax.ShapeDtypeStruct((stacked, breadth)...]
    ppermute x12 -> x15, waiting for transfers between devices: 20.8 us -> 17.6 us  [send_left(): return lax.ppermute(x, 'dp', backward)]
    pallas_call x1, Pallas kernels: 5.27 us -> 2.75 us  [finish(): pl.pallas_call(kernel, out_shape=(jax.ShapeDtypeStruct((stacked, breadth)...]
    pallas_call x1, Pallas kernels: 4.03 us -> 2.54 us  [unpack_roots(): pl.pallas_call(kernel, out_shape=(out, out), grid_spec=pltpu.PrefetchScal...]
    unnamed x14 -> x10, local copies, waits for them, and re-layouts: 1.43 us -> 0.03 us
  transfers between devices with their start and end apart: 24 -> 30, of which waited for: 15 -> 12; matrix products, arithmetic and copies ran while one was open for 0% -> 0% of each run, Pallas kernels for 7% -> 10%
where the time goes in v2:
time: 66.8 us; the launch traced here: 66.6 us
  starting transfers between devices  33.3 us (50%)
  waiting for transfers between devices  20.3 us (30%)
  Pallas kernels  12.1 us (18%)
  between operations  0.82 us (1%)
    ppermute x15, starting transfers between devices, send_left(): return lax.ppermute(x, 'dp', backward)  27.9 us
    ppermute x15, waiting for transfers between devices, send_left(): return lax.ppermute(x, 'dp', backward)  17.6 us
    ppermute x15, starting transfers between devices, send_right(): return lax.ppermute(x, 'dp', onward)  5.46 us
    pallas_call x1, Pallas kernels, begin(): pl.pallas_call(kernel, out_shape=(jax.ShapeDtypeStruct((stacked, breadth)...  3.74 us
    pallas_call x1, Pallas kernels, finish(): pl.pallas_call(kernel, out_shape=(jax.ShapeDtypeStruct((stacked, breadth)...  2.75 us
    ppermute x15, waiting for transfers between devices, send_right(): return lax.ppermute(x, 'dp', onward)  2.74 us
    pallas_call x1, Pallas kernels, open_ring(): pl.pallas_call(kernel, out_shape=(sent, sent, jax.ShapeDtypeStruct((band,...  2.73 us
    pallas_call x1, Pallas kernels, unpack_roots(): pl.pallas_call(kernel, out_shape=(out, out), grid_spec=pltpu.PrefetchScal...  2.54 us
  transfers between devices with their start and end apart: 30, of which 12 were waited for; matrix products, arithmetic and copies ran while one was open for 0% of the time, Pallas kernels for 10%

profile of v2, /device:TPU:0, one launch (start us, length us, event | category | flops | bytes accessed | tf_op | source)
XLA Modules:
  0.0 66.6 jit_solution(18096862361580688663)
XLA Ops:
  0.6 2.7 %open_ring.1 = (bf16[96,512]{1,0:T(8,128)(2,1)}, bf16[96,512]{1,0:T(8,128)(2,1)}, bf16[192,640]{1,0:T(8,128)(2,1)}) custom-call(s32[1]{0:T(128)} %bitcast.me_ref, s32[8]{0:T(128)} %owner_ref.5, bf16[1,1536,512]{2,1,0:T(8,128)(2,1)} %own_ref.13, bf16[192,512]{1,0:T(8,128)(2,1)} %lr_ref.1, bf16[192,512]{1,0:T(8,128)(2,1)} %rr_ref.1), custom_call_target="tpu_custom_call" | custom-call | tf_op jit(solution)/shard_map/open_ring/pallas_call | solution.py:229
  3.4 3.0 %collective-permute-start.4 = (bf16[96,512]{1,0:T(8,128)(2,1)}, bf16[96,512]{1,0:T(8,128)(2,1)S(1)}, u32[]{:S(2)}, u32[]{:S(2)}) collective-permute-start(bf16[96,512]{1,0:T(8,128)(2,1)} %get-tuple-element.12), channel_id=1, source_target_pairs={{8,0},{16,8},{24,16},{28,24},{20,28},{12,20},{4,12},{0,4},{9,1},{1... | collective-permute-start | bytes 294920 | tf_op jit(solution)/shard_map/ppermute | solution.py:481
  6.4 0.2 collective-permute-start
  6.5 2.9 %collective-permute-done.4.a_ref = bf16[96,512]{1,0:T(8,128)(2,1)S(1)} collective-permute-done((bf16[96,512]{1,0:T(8,128)(2,1)}, bf16[96,512]{1,0:T(8,128)(2,1)S(1)}, u32[]{:S(2)}, u32[]{:S(2)}) %collective-permute-start.4) | collective-permute-done | bytes 98336 | tf_op jit(solution)/shard_map/ppermute | solution.py:481
  9.5 1.8 %collective-permute-start.5 = (bf16[192,512]{1,0:T(8,128)(2,1)S(1)}, bf16[192,512]{1,0:T(8,128)(2,1)S(1)}, u32[]{:S(2)}, u32[]{:S(2)}) collective-permute-start(bf16[192,512]{1,0:T(8,128)(2,1)S(1)} %add_send.9), channel_id=1, source_target_pairs={{8,0},{16,8},{24,16},{28,24},{20,28},{12,20},{4,12},{0,4},{9,1},{1... | collective-permute-start | bytes 589832 | tf_op jit(solution)/shard_map/ppermute | solution.py:481
  11.3 0.3 collective-permute-start.1
  11.7 1.7 %collective-permute-start.23 = (bf16[192,640]{1,0:T(8,128)(2,1)S(1)}, bf16[192,640]{1,0:T(8,128)(2,1)S(1)}, u32[]{:S(2)}, u32[]{:S(2)}) collective-permute-start(bf16[192,640]{1,0:T(8,128)(2,1)S(1)} %copy-done.3), channel_id=1, source_target_pairs={{8,0},{16,8},{24,16},{28,24},{20,28},{12,20},{4,12},{0,4},{9,1},{1... | collective-permute-start | bytes 737288 | tf_op jit(solution)/shard_map/ppermute | solution.py:481
  13.4 0.3 collective-permute-start.22
  13.7 3.7 %collective-permute-done.5.a_ref = bf16[192,512]{1,0:T(8,128)(2,1)S(1)} collective-permute-done((bf16[192,512]{1,0:T(8,128)(2,1)S(1)}, bf16[192,512]{1,0:T(8,128)(2,1)S(1)}, u32[]{:S(2)}, u32[]{:S(2)}) %collective-permute-start.5) | collective-permute-done | bytes 196640 | tf_op jit(solution)/shard_map/ppermute | solution.py:481
  17.4 0.1 add_send.10
  17.5 1.8 %collective-permute-start.6 = (bf16[192,512]{1,0:T(8,128)(2,1)S(1)}, bf16[192,512]{1,0:T(8,128)(2,1)S(1)}, u32[]{:S(2)}, u32[]{:S(2)}) collective-permute-start(bf16[192,512]{1,0:T(8,128)(2,1)S(1)} %add_send.10), channel_id=1, source_target_pairs={{8,0},{16,8},{24,16},{28,24},{20,28},{12,20},{4,12},{0,4},{9,1},{1... | collective-permute-start | bytes 589832 | tf_op jit(solution)/shard_map/ppermute | solution.py:481
  19.3 0.1 add_send.7
  19.3 0.3 collective-permute-start.2
  19.7 3.0 %collective-permute-done.23.refs_2_ = bf16[192,640]{1,0:T(8,128)(2,1)S(1)} collective-permute-done((bf16[192,640]{1,0:T(8,128)(2,1)S(1)}, bf16[192,640]{1,0:T(8,128)(2,1)S(1)}, u32[]{:S(2)}, u32[]{:S(2)}) %collective-permute-start.23) | collective-permute-done | bytes 245792 | tf_op jit(solution)/shard_map/ppermute | solution.py:481
  22.7 1.7 %collective-permute-start.25 = (bf16[192,640]{1,0:T(8,128)(2,1)S(1)}, bf16[192,640]{1,0:T(8,128)(2,1)S(1)}, u32[]{:S(2)}, u32[]{:S(2)}) collective-permute-start(bf16[192,640]{1,0:T(8,128)(2,1)S(1)} %collective-permute-done.23.refs_2_), channel_id=1, source_target_pairs={{8,0},{16,8},{24,16},{28,24},{20,28},{12,20},{4,12},{0,4},{9,1},{1... | collective-permute-start | bytes 737288 | tf_op jit(solution)/shard_map/ppermute | solution.py:481
  24.4 0.1 collective-permute-done.22.refs_1_
  24.5 0.3 collective-permute-start.24
  24.8 2.1 %collective-permute-done.6.a_ref = bf16[192,512]{1,0:T(8,128)(2,1)S(1)} collective-permute-done((bf16[192,512]{1,0:T(8,128)(2,1)S(1)}, bf16[192,512]{1,0:T(8,128)(2,1)S(1)}, u32[]{:S(2)}, u32[]{:S(2)}) %collective-permute-start.6) | collective-permute-done | bytes 196640 | tf_op jit(solution)/shard_map/ppermute | solution.py:481
  26.9 0.1 add_send.11
  26.9 1.8 %collective-permute-start.7 = (bf16[192,512]{1,0:T(8,128)(2,1)S(1)}, bf16[192,512]{1,0:T(8,128)(2,1)S(1)}, u32[]{:S(2)}, u32[]{:S(2)}) collective-permute-start(bf16[192,512]{1,0:T(8,128)(2,1)S(1)} %add_send.11), channel_id=1, source_target_pairs={{8,0},{16,8},{24,16},{28,24},{20,28},{12,20},{4,12},{0,4},{9,1},{1... | collective-permute-start | bytes 589832 | tf_op jit(solution)/shard_map/ppermute | solution.py:481
  28.8 0.3 collective-permute-start.3
  29.2 3.0 %collective-permute-done.25.refs_4_ = bf16[192,640]{1,0:T(8,128)(2,1)S(1)} collective-permute-done((bf16[192,640]{1,0:T(8,128)(2,1)S(1)}, bf16[192,640]{1,0:T(8,128)(2,1)S(1)}, u32[]{:S(2)}, u32[]{:S(2)}) %collective-permute-start.25) | collective-permute-done | bytes 245792 | tf_op jit(solution)/shard_map/ppermute | solution.py:481
  32.1 1.7 %collective-permute-start.27 = (bf16[192,640]{1,0:T(8,128)(2,1)S(1)}, bf16[192,640]{1,0:T(8,128)(2,1)S(1)}, u32[]{:S(2)}, u32[]{:S(2)}) collective-permute-start(bf16[192,640]{1,0:T(8,128)(2,1)S(1)} %collective-permute-done.25.refs_4_), channel_id=1, source_target_pairs={{8,0},{16,8},{24,16},{28,24},{20,28},{12,20},{4,12},{0,4},{9,1},{1... | collective-permute-start | bytes 737288 | tf_op jit(solution)/shard_map/ppermute | solution.py:481
  33.9 0.1 collective-permute-done.24.refs_3_
  34.0 0.3 collective-permute-start.26
  34.3 2.1 %collective-permute-done.7.l_ref = bf16[192,512]{1,0:T(8,128)(2,1)S(1)} collective-permute-done((bf16[192,512]{1,0:T(8,128)(2,1)S(1)}, bf16[192,512]{1,0:T(8,128)(2,1)S(1)}, u32[]{:S(2)}, u32[]{:S(2)}) %collective-permute-start.7) | collective-permute-done | bytes 196640 | tf_op jit(solution)/shard_map/ppermute | solution.py:481
  36.4 1.8 %collective-permute-done.3.r_ref = bf16[192,512]{1,0:T(8,128)(2,1)S(1)} collective-permute-done((bf16[192,512]{1,0:T(8,128)(2,1)S(1)}, bf16[192,512]{1,0:T(8,128)(2,1)S(1)}, u32[]{:S(2)}, u32[]{:S(2)}) %collective-permute-start.3) | collective-permute-done | bytes 196640 | tf_op jit(solution)/shard_map/ppermute | solution.py:478
  38.2 0.1 add_own.1.refs_0_
  38.3 1.6 %collective-permute-start.12 = (bf16[96,512]{1,0:T(8,128)(2,1)S(1)}, bf16[96,512]{1,0:T(8,128)(2,1)S(1)}, u32[]{:S(2)}, u32[]{:S(2)}) collective-permute-start(bf16[96,512]{1,0:T(8,128)(2,1)S(1)} %get-tuple-element.19), channel_id=1, source_target_pairs={{8,0},{16,8},{24,16},{28,24},{20,28},{12,20},{4,12},{0,4},{9,1},{1... | collective-permute-start | bytes 294920 | tf_op jit(solution)/shard_map/ppermute | solution.py:481
  39.9 0.4 collective-permute-start.8
  40.4 0.3 collective-permute-start.17
  40.7 0.3 collective-permute-done.27.refs_6_
  41.0 1.7 %collective-permute-start.16 = (bf16[96,512]{1,0:T(8,128)(2,1)S(1)}, bf16[96,512]{1,0:T(8,128)(2,1)S(1)}, u32[]{:S(2)}, u32[]{:S(2)}) collective-permute-start(bf16[96,512]{1,0:T(8,128)(2,1)S(1)} %get-tuple-element.20), channel_id=1, source_target_pairs={{8,0},{16,8},{24,16},{28,24},{20,28},{12,20},{4,12},{0,4},{9,1},{1... | collective-permute-start | bytes 294920 | tf_op jit(solution)/shard_map/ppermute | solution.py:481
  42.7 0.4 collective-permute-done.12.refs_4_
  43.1 2.5 %collective-permute-start.13 = (bf16[96,512]{1,0:T(8,128)(2,1)S(1)}, bf16[96,512]{1,0:T(8,128)(2,1)S(1)}, u32[]{:S(2)}, u32[]{:S(2)}) collective-permute-start(bf16[96,512]{1,0:T(8,128)(2,1)S(1)} %collective-permute-done.12.refs_4_), channel_id=1, source_target_pairs={{8,0},{16,8},{24,16},{28,24},{20,28},{12,20},{4,12},{0,4},{9,1},{1... | collective-permute-start | bytes 294920 | tf_op jit(solution)/shard_map/ppermute | solution.py:481
  45.6 2.1 %collective-permute-start.29 = (bf16[96,640]{1,0:T(8,128)(2,1)S(1)}, bf16[96,640]{1,0:T(8,128)(2,1)S(1)}, u32[]{:S(2)}, u32[]{:S(2)}) collective-permute-start(bf16[96,640]{1,0:T(8,128)(2,1)S(1)} %slice.19), channel_id=1, source_target_pairs={{8,0},{16,8},{24,16},{28,24},{20,28},{12,20},{4,12},{0,4},{9,1},{1... | collective-permute-start | bytes 368648 | tf_op jit(solution)/shard_map/ppermute | solution.py:481
  47.7 2.0 %collective-permute-start.18 = (bf16[96,512]{1,0:T(8,128)(2,1)S(1)}, bf16[96,512]{1,0:T(8,128)(2,1)S(1)}, u32[]{:S(2)}, u32[]{:S(2)}) collective-permute-start(bf16[96,512]{1,0:T(8,128)(2,1)S(1)} %collective-permute-done.16.refs_2_), channel_id=1, source_target_pairs={{8,0},{16,8},{24,16},{28,24},{20,28},{12,20},{4,12},{0,4},{9,1},{1... | collective-permute-start | bytes 294920 | tf_op jit(solution)/shard_map/ppermute | solution.py:481
  49.7 1.6 %collective-permute-start.14 = (bf16[96,512]{1,0:T(8,128)(2,1)S(1)}, bf16[96,512]{1,0:T(8,128)(2,1)S(1)}, u32[]{:S(2)}, u32[]{:S(2)}) collective-permute-start(bf16[96,512]{1,0:T(8,128)(2,1)S(1)} %collective-permute-done.13.refs_8_), channel_id=1, source_target_pairs={{8,0},{16,8},{24,16},{28,24},{20,28},{12,20},{4,12},{0,4},{9,1},{1... | collective-permute-start | bytes 294920 | tf_op jit(solution)/shard_map/ppermute | solution.py:481
  51.3 0.5 collective-permute-start.10
  51.8 0.9 %collective-permute-start.28 = (bf16[96,640]{1,0:T(8,128)(2,1)S(1)}, bf16[96,640]{1,0:T(8,128)(2,1)S(1)}, u32[]{:S(2)}, u32[]{:S(2)}) collective-permute-start(bf16[96,640]{1,0:T(8,128)(2,1)S(1)} %slice.18), channel_id=1, source_target_pairs={{0,8},{8,16},{16,24},{24,28},{28,20},{20,12},{12,4},{4,0},{1,9},{9... | collective-permute-start | bytes 368648 | tf_op jit(solution)/shard_map/ppermute | solution.py:478
  52.7 0.7 %collective-permute-done.19.refs_7_ = bf16[96,512]{1,0:T(8,128)(2,1)S(1)} collective-permute-done((bf16[96,512]{1,0:T(8,128)(2,1)S(1)}, bf16[96,512]{1,0:T(8,128)(2,1)S(1)}, u32[]{:S(2)}, u32[]{:S(2)}) %collective-permute-start.19) | collective-permute-done | bytes 98336 | tf_op jit(solution)/shard_map/ppermute | solution.py:478
  53.4 0.9 %collective-permute-start.21 = (bf16[96,512]{1,0:T(8,128)(2,1)S(1)}, bf16[96,512]{1,0:T(8,128)(2,1)S(1)}, u32[]{:S(2)}, u32[]{:S(2)}) collective-permute-start(bf16[96,512]{1,0:T(8,128)(2,1)S(1)} %collective-permute-done.19.refs_7_), channel_id=1, source_target_pairs={{0,8},{8,16},{16,24},{24,28},{28,20},{20,12},{12,4},{4,0},{1,9},{9... | collective-permute-start | bytes 294920 | tf_op jit(solution)/shard_map/ppermute | solution.py:478
  54.3 1.1 %collective-permute-start.20 = (bf16[96,512]{1,0:T(8,128)(2,1)S(1)}, bf16[96,512]{1,0:T(8,128)(2,1)S(1)}, u32[]{:S(2)}, u32[]{:S(2)}) collective-permute-start(bf16[96,512]{1,0:T(8,128)(2,1)S(1)} %collective-permute-done.18.refs_6_), channel_id=1, source_target_pairs={{8,0},{16,8},{24,16},{28,24},{20,28},{12,20},{4,12},{0,4},{9,1},{1... | collective-permute-start | bytes 294920 | tf_op jit(solution)/shard_map/ppermute | solution.py:481
  55.5 1.6 %collective-permute-start.15 = (bf16[96,512]{1,0:T(8,128)(2,1)S(1)}, bf16[96,512]{1,0:T(8,128)(2,1)S(1)}, u32[]{:S(2)}, u32[]{:S(2)}) collective-permute-start(bf16[96,512]{1,0:T(8,128)(2,1)S(1)} %collective-permute-done.14.refs_12_), channel_id=1, source_target_pairs={{8,0},{16,8},{24,16},{28,24},{20,28},{12,20},{4,12},{0,4},{9,1},{1... | collective-permute-start | bytes 294920 | tf_op jit(solution)/shard_map/ppermute | solution.py:481
  57.1 0.4 collective-permute-start.11
  57.5 2.5 %unpack_roots.1 = (bf16[1536,512]{1,0:T(8,128)(2,1)S(1)}, bf16[1536,512]{1,0:T(8,128)(2,1)S(1)}) custom-call(s32[1]{0:T(128)} %bitcast.me_ref, s32[8]{0:T(128)S(1)} %copy-done.4, bf16[192,640]{1,0:T(8,128)(2,1)S(1)} %copy-done.3, bf16[192,640]{1,0:T(8,128)(2,1)S(1)} %collective-permute-done.22.refs_1_, bf16[192,640]{1,0:T(8,128)(2,1)S(1)} %collective-permute-done.23.refs_2_, ...), custom_call_target="tpu_custom_call" | custom-call | tf_op jit(solution)/shard_map/unpack_roots/pallas_call | solution.py:294
  60.1 3.7 %begin.1 = (bf16[1536,512]{1,0:T(8,128)(2,1)}, bf16[1536,512]{1,0:T(8,128)(2,1)S(1)}, f32[2,512,512]{2,1,0:T(8,128)S(1)}) custom-call(s32[1]{0:T(128)} %bitcast.me_ref, bf16[192,512]{1,0:T(8,128)(2,1)S(1)} %add_own.1.refs_0_, bf16[96,512]{1,0:T(8,128)(2,1)S(1)} %collective-permute-done.8.refs_1_, bf16[96,512]{1,0:T(8,128)(2,1)S(1)} %collective-permute-done.16.refs_2_, ...), custom_call_target="tpu_custom_call" | custom-call | tf_op jit(solution)/shard_map/begin/pallas_call | solution.py:333
  63.9 2.8 %finish.1 = (bf16[1536,512]{1,0:T(8,128)(2,1)}, f32[192,512]{1,0:T(8,128)}, f32[192,512]{1,0:T(8,128)}) custom-call(s32[1]{0:T(128)} %bitcast.me_ref, s32[8]{0:T(128)S(1)} %copy-done.4, bf16[96,512]{1,0:T(8,128)(2,1)S(1)} %collective-permute-done.11.refs_0_, bf16[96,512]{1,0:T(8,128)(2,1)S(1)} %collective-permute-done.15.refs_1_, ...), custom_call_target="tpu_custom_call", output_to_operand_aliasing={{0}: (4, {})} | custom-call | tf_op jit(solution)/shard_map/finish/pallas_call | solution.py:432
  (36 shorter events, 0.2 us)
Async XLA Ops:
  0.6 8.8 %copy-start = (bf16[1,1536,512]{2,1,0:T(8,128)(2,1)S(1)}, bf16[1,1536,512]{2,1,0:T(8,128)(2,1)}, u32[]{:S(2)}) copy-start(bf16[1,1536,512]{2,1,0:T(8,128)(2,1)} %own_ref.13) | copy-start | bytes 4718596
  3.4 6.1 %collective-permute-start.4 = (bf16[96,512]{1,0:T(8,128)(2,1)}, bf16[96,512]{1,0:T(8,128)(2,1)S(1)}, u32[]{:S(2)}, u32[]{:S(2)}) collective-permute-start(bf16[96,512]{1,0:T(8,128)(2,1)} %get-tuple-element.12), channel_id=1, source_target_pairs={{8,0},{16,8},{24,16},{28,24},{20,28},{12,20},{4,12},{0,4},{9,1},{1... | collective-permute-start | bytes 294920 | tf_op jit(solution)/shard_map/ppermute | solution.py:481
  6.4 5.3 %copy-start.3 = (bf16[192,640]{1,0:T(8,128)(2,1)S(1)}, bf16[192,640]{1,0:T(8,128)(2,1)}, u32[]{:S(2)}) copy-start(bf16[192,640]{1,0:T(8,128)(2,1)} %get-tuple-element.13.refs_0_) | copy-start | bytes 737284
  6.4 4.9 %collective-permute-start = (bf16[96,512]{1,0:T(8,128)(2,1)}, bf16[96,512]{1,0:T(8,128)(2,1)S(1)}, u32[]{:S(2)}, u32[]{:S(2)}) collective-permute-start(bf16[96,512]{1,0:T(8,128)(2,1)} %get-tuple-element.11), channel_id=1, source_target_pairs={{0,8},{8,16},{16,24},{24,28},{28,20},{20,12},{12,4},{4,0},{1,9},{9... | collective-permute-start | bytes 294920 | tf_op jit(solution)/shard_map/ppermute | solution.py:478
  9.5 7.9 %collective-permute-start.5 = (bf16[192,512]{1,0:T(8,128)(2,1)S(1)}, bf16[192,512]{1,0:T(8,128)(2,1)S(1)}, u32[]{:S(2)}, u32[]{:S(2)}) collective-permute-start(bf16[192,512]{1,0:T(8,128)(2,1)S(1)} %add_send.9), channel_id=1, source_target_pairs={{8,0},{16,8},{24,16},{28,24},{20,28},{12,20},{4,12},{0,4},{9,1},{1... | collective-permute-start | bytes 589832 | tf_op jit(solution)/shard_map/ppermute | solution.py:481
  11.3 7.9 %collective-permute-start.1 = (bf16[192,512]{1,0:T(8,128)(2,1)S(1)}, bf16[192,512]{1,0:T(8,128)(2,1)S(1)}, u32[]{:S(2)}, u32[]{:S(2)}) collective-permute-start(bf16[192,512]{1,0:T(8,128)(2,1)S(1)} %add_send.6), channel_id=1, source_target_pairs={{0,8},{8,16},{16,24},{24,28},{28,20},{20,12},{12,4},{4,0},{1,9},{9... | collective-permute-start | bytes 589832 | tf_op jit(solution)/shard_map/ppermute | solution.py:478
  11.7 11.0 %collective-permute-start.23 = (bf16[192,640]{1,0:T(8,128)(2,1)S(1)}, bf16[192,640]{1,0:T(8,128)(2,1)S(1)}, u32[]{:S(2)}, u32[]{:S(2)}) collective-permute-start(bf16[192,640]{1,0:T(8,128)(2,1)S(1)} %copy-done.3), channel_id=1, source_target_pairs={{8,0},{16,8},{24,16},{28,24},{20,28},{12,20},{4,12},{0,4},{9,1},{1... | collective-permute-start | bytes 737288 | tf_op jit(solution)/shard_map/ppermute | solution.py:481
  13.4 11.1 %collective-permute-start.22 = (bf16[192,640]{1,0:T(8,128)(2,1)S(1)}, bf16[192,640]{1,0:T(8,128)(2,1)S(1)}, u32[]{:S(2)}, u32[]{:S(2)}) collective-permute-start(bf16[192,640]{1,0:T(8,128)(2,1)S(1)} %copy-done.3), channel_id=1, source_target_pairs={{0,8},{8,16},{16,24},{24,28},{28,20},{20,12},{12,4},{4,0},{1,9},{9... | collective-permute-start | bytes 737288 | tf_op jit(solution)/shard_map/ppermute | solution.py:478
  17.5 9.4 %collective-permute-start.6 = (bf16[192,512]{1,0:T(8,128)(2,1)S(1)}, bf16[192,512]{1,0:T(8,128)(2,1)S(1)}, u32[]{:S(2)}, u32[]{:S(2)}) collective-permute-start(bf16[192,512]{1,0:T(8,128)(2,1)S(1)} %add_send.10), channel_id=1, source_target_pairs={{8,0},{16,8},{24,16},{28,24},{20,28},{12,20},{4,12},{0,4},{9,1},{1... | collective-permute-start | bytes 589832 | tf_op jit(solution)/shard_map/ppermute | solution.py:481
  19.3 9.4 %collective-permute-start.2 = (bf16[192,512]{1,0:T(8,128)(2,1)S(1)}, bf16[192,512]{1,0:T(8,128)(2,1)S(1)}, u32[]{:S(2)}, u32[]{:S(2)}) collective-permute-start(bf16[192,512]{1,0:T(8,128)(2,1)S(1)} %add_send.7), channel_id=1, source_target_pairs={{0,8},{8,16},{16,24},{24,28},{28,20},{20,12},{12,4},{4,0},{1,9},{9... | collective-permute-start | bytes 589832 | tf_op jit(solution)/shard_map/ppermute | solution.py:478
  22.7 9.5 %collective-permute-start.25 = (bf16[192,640]{1,0:T(8,128)(2,1)S(1)}, bf16[192,640]{1,0:T(8,128)(2,1)S(1)}, u32[]{:S(2)}, u32[]{:S(2)}) collective-permute-start(bf16[192,640]{1,0:T(8,128)(2,1)S(1)} %collective-permute-done.23.refs_2_), channel_id=1, source_target_pairs={{8,0},{16,8},{24,16},{28,24},{20,28},{12,20},{4,12},{0,4},{9,1},{1... | collective-permute-start | bytes 737288 | tf_op jit(solution)/shard_map/ppermute | solution.py:481
  24.5 9.5 %collective-permute-start.24 = (bf16[192,640]{1,0:T(8,128)(2,1)S(1)}, bf16[192,640]{1,0:T(8,128)(2,1)S(1)}, u32[]{:S(2)}, u32[]{:S(2)}) collective-permute-start(bf16[192,640]{1,0:T(8,128)(2,1)S(1)} %collective-permute-done.22.refs_1_), channel_id=1, source_target_pairs={{0,8},{8,16},{16,24},{24,28},{28,20},{20,12},{12,4},{4,0},{1,9},{9... | collective-permute-start | bytes 737288 | tf_op jit(solution)/shard_map/ppermute | solution.py:478
  26.9 9.4 %collective-permute-start.7 = (bf16[192,512]{1,0:T(8,128)(2,1)S(1)}, bf16[192,512]{1,0:T(8,128)(2,1)S(1)}, u32[]{:S(2)}, u32[]{:S(2)}) collective-permute-start(bf16[192,512]{1,0:T(8,128)(2,1)S(1)} %add_send.11), channel_id=1, source_target_pairs={{8,0},{16,8},{24,16},{28,24},{20,28},{12,20},{4,12},{0,4},{9,1},{1... | collective-permute-start | bytes 589832 | tf_op jit(solution)/shard_map/ppermute | solution.py:481
  28.8 28.7 %copy-start.4 = (s32[8]{0:T(128)S(1)}, s32[8]{0:T(128)}, u32[]{:S(2)}) copy-start(s32[8]{0:T(128)} %owner_ref.5) | copy-start | bytes 100
  28.8 9.4 %collective-permute-start.3 = (bf16[192,512]{1,0:T(8,128)(2,1)S(1)}, bf16[192,512]{1,0:T(8,128)(2,1)S(1)}, u32[]{:S(2)}, u32[]{:S(2)}) collective-permute-start(bf16[192,512]{1,0:T(8,128)(2,1)S(1)} %add_send.8), channel_id=1, source_target_pairs={{0,8},{8,16},{16,24},{24,28},{28,20},{20,12},{12,4},{4,0},{1,9},{9... | collective-permute-start | bytes 589832 | tf_op jit(solution)/shard_map/ppermute | solution.py:478
  32.1 8.8 %collective-permute-start.27 = (bf16[192,640]{1,0:T(8,128)(2,1)S(1)}, bf16[192,640]{1,0:T(8,128)(2,1)S(1)}, u32[]{:S(2)}, u32[]{:S(2)}) collective-permute-start(bf16[192,640]{1,0:T(8,128)(2,1)S(1)} %collective-permute-done.25.refs_4_), channel_id=1, source_target_pairs={{8,0},{16,8},{24,16},{28,24},{20,28},{12,20},{4,12},{0,4},{9,1},{1... | collective-permute-start | bytes 737288 | tf_op jit(solution)/shard_map/ppermute | solution.py:481
  34.0 11.6 %collective-permute-start.26 = (bf16[192,640]{1,0:T(8,128)(2,1)S(1)}, bf16[192,640]{1,0:T(8,128)(2,1)S(1)}, u32[]{:S(2)}, u32[]{:S(2)}) collective-permute-start(bf16[192,640]{1,0:T(8,128)(2,1)S(1)} %collective-permute-done.24.refs_3_), channel_id=1, source_target_pairs={{0,8},{8,16},{16,24},{24,28},{28,20},{20,12},{12,4},{4,0},{1,9},{9... | collective-permute-start | bytes 737288 | tf_op jit(solution)/shard_map/ppermute | solution.py:478
  38.3 4.8 %collective-permute-start.12 = (bf16[96,512]{1,0:T(8,128)(2,1)S(1)}, bf16[96,512]{1,0:T(8,128)(2,1)S(1)}, u32[]{:S(2)}, u32[]{:S(2)}) collective-permute-start(bf16[96,512]{1,0:T(8,128)(2,1)S(1)} %get-tuple-element.19), channel_id=1, source_target_pairs={{8,0},{16,8},{24,16},{28,24},{20,28},{12,20},{4,12},{0,4},{9,1},{1... | collective-permute-start | bytes 294920 | tf_op jit(solution)/shard_map/ppermute | solution.py:481
  39.9 5.7 %collective-permute-start.8 = (bf16[96,512]{1,0:T(8,128)(2,1)S(1)}, bf16[96,512]{1,0:T(8,128)(2,1)S(1)}, u32[]{:S(2)}, u32[]{:S(2)}) collective-permute-start(bf16[96,512]{1,0:T(8,128)(2,1)S(1)} %get-tuple-element.20), channel_id=1, source_target_pairs={{0,8},{8,16},{16,24},{24,28},{28,20},{20,12},{12,4},{4,0},{1,9},{9... | collective-permute-start | bytes 294920 | tf_op jit(solution)/shard_map/ppermute | solution.py:478
  40.4 7.3 %collective-permute-start.17 = (bf16[96,512]{1,0:T(8,128)(2,1)S(1)}, bf16[96,512]{1,0:T(8,128)(2,1)S(1)}, u32[]{:S(2)}, u32[]{:S(2)}) collective-permute-start(bf16[96,512]{1,0:T(8,128)(2,1)S(1)} %get-tuple-element.19), channel_id=1, source_target_pairs={{0,8},{8,16},{16,24},{24,28},{28,20},{20,12},{12,4},{4,0},{1,9},{9... | collective-permute-start | bytes 294920 | tf_op jit(solution)/shard_map/ppermute | solution.py:478
  41.0 6.7 %collective-permute-start.16 = (bf16[96,512]{1,0:T(8,128)(2,1)S(1)}, bf16[96,512]{1,0:T(8,128)(2,1)S(1)}, u32[]{:S(2)}, u32[]{:S(2)}) collective-permute-start(bf16[96,512]{1,0:T(8,128)(2,1)S(1)} %get-tuple-element.20), channel_id=1, source_target_pairs={{8,0},{16,8},{24,16},{28,24},{20,28},{12,20},{4,12},{0,4},{9,1},{1... | collective-permute-start | bytes 294920 | tf_op jit(solution)/shard_map/ppermute | solution.py:481
  43.1 6.6 %collective-permute-start.13 = (bf16[96,512]{1,0:T(8,128)(2,1)S(1)}, bf16[96,512]{1,0:T(8,128)(2,1)S(1)}, u32[]{:S(2)}, u32[]{:S(2)}) collective-permute-start(bf16[96,512]{1,0:T(8,128)(2,1)S(1)} %collective-permute-done.12.refs_4_), channel_id=1, source_target_pairs={{8,0},{16,8},{24,16},{28,24},{20,28},{12,20},{4,12},{0,4},{9,1},{1... | collective-permute-start | bytes 294920 | tf_op jit(solution)/shard_map/ppermute | solution.py:481
  45.6 5.7 %collective-permute-start.9 = (bf16[96,512]{1,0:T(8,128)(2,1)S(1)}, bf16[96,512]{1,0:T(8,128)(2,1)S(1)}, u32[]{:S(2)}, u32[]{:S(2)}) collective-permute-start(bf16[96,512]{1,0:T(8,128)(2,1)S(1)} %collective-permute-done.8.refs_1_), channel_id=1, source_target_pairs={{0,8},{8,16},{16,24},{24,28},{28,20},{20,12},{12,4},{4,0},{1,9},{9... | collective-permute-start | bytes 294920 | tf_op jit(solution)/shard_map/ppermute | solution.py:478
  45.6 6.2 %collective-permute-start.29 = (bf16[96,640]{1,0:T(8,128)(2,1)S(1)}, bf16[96,640]{1,0:T(8,128)(2,1)S(1)}, u32[]{:S(2)}, u32[]{:S(2)}) collective-permute-start(bf16[96,640]{1,0:T(8,128)(2,1)S(1)} %slice.19), channel_id=1, source_target_pairs={{8,0},{16,8},{24,16},{28,24},{20,28},{12,20},{4,12},{0,4},{9,1},{1... | collective-permute-start | bytes 368648 | tf_op jit(solution)/shard_map/ppermute | solution.py:481
  47.7 5.7 %collective-permute-start.19 = (bf16[96,512]{1,0:T(8,128)(2,1)S(1)}, bf16[96,512]{1,0:T(8,128)(2,1)S(1)}, u32[]{:S(2)}, u32[]{:S(2)}) collective-permute-start(bf16[96,512]{1,0:T(8,128)(2,1)S(1)} %collective-permute-done.17.refs_3_), channel_id=1, source_target_pairs={{0,8},{8,16},{16,24},{24,28},{28,20},{20,12},{12,4},{4,0},{1,9},{9... | collective-permute-start | bytes 294920 | tf_op jit(solution)/shard_map/ppermute | solution.py:478
  47.7 6.6 %collective-permute-start.18 = (bf16[96,512]{1,0:T(8,128)(2,1)S(1)}, bf16[96,512]{1,0:T(8,128)(2,1)S(1)}, u32[]{:S(2)}, u32[]{:S(2)}) collective-permute-start(bf16[96,512]{1,0:T(8,128)(2,1)S(1)} %collective-permute-done.16.refs_2_), channel_id=1, source_target_pairs={{8,0},{16,8},{24,16},{28,24},{20,28},{12,20},{4,12},{0,4},{9,1},{1... | collective-permute-start | bytes 294920 | tf_op jit(solution)/shard_map/ppermute | solution.py:481
  49.7 5.7 %collective-permute-start.14 = (bf16[96,512]{1,0:T(8,128)(2,1)S(1)}, bf16[96,512]{1,0:T(8,128)(2,1)S(1)}, u32[]{:S(2)}, u32[]{:S(2)}) collective-permute-start(bf16[96,512]{1,0:T(8,128)(2,1)S(1)} %collective-permute-done.13.refs_8_), channel_id=1, source_target_pairs={{8,0},{16,8},{24,16},{28,24},{20,28},{12,20},{4,12},{0,4},{9,1},{1... | collective-permute-start | bytes 294920 | tf_op jit(solution)/shard_map/ppermute | solution.py:481
  51.3 5.8 %collective-permute-start.10 = (bf16[96,512]{1,0:T(8,128)(2,1)S(1)}, bf16[96,512]{1,0:T(8,128)(2,1)S(1)}, u32[]{:S(2)}, u32[]{:S(2)}) collective-permute-start(bf16[96,512]{1,0:T(8,128)(2,1)S(1)} %collective-permute-done.9.refs_5_), channel_id=1, source_target_pairs={{0,8},{8,16},{16,24},{24,28},{28,20},{20,12},{12,4},{4,0},{1,9},{9... | collective-permute-start | bytes 294920 | tf_op jit(solution)/shard_map/ppermute | solution.py:478
  51.8 5.7 %collective-permute-start.28 = (bf16[96,640]{1,0:T(8,128)(2,1)S(1)}, bf16[96,640]{1,0:T(8,128)(2,1)S(1)}, u32[]{:S(2)}, u32[]{:S(2)}) collective-permute-start(bf16[96,640]{1,0:T(8,128)(2,1)S(1)} %slice.18), channel_id=1, source_target_pairs={{0,8},{8,16},{16,24},{24,28},{28,20},{20,12},{12,4},{4,0},{1,9},{9... | collective-permute-start | bytes 368648 | tf_op jit(solution)/shard_map/ppermute | solution.py:478
  53.4 6.6 %collective-permute-start.21 = (bf16[96,512]{1,0:T(8,128)(2,1)S(1)}, bf16[96,512]{1,0:T(8,128)(2,1)S(1)}, u32[]{:S(2)}, u32[]{:S(2)}) collective-permute-start(bf16[96,512]{1,0:T(8,128)(2,1)S(1)} %collective-permute-done.19.refs_7_), channel_id=1, source_target_pairs={{0,8},{8,16},{16,24},{24,28},{28,20},{20,12},{12,4},{4,0},{1,9},{9... | collective-permute-start | bytes 294920 | tf_op jit(solution)/shard_map/ppermute | solution.py:478
  54.3 5.7 %collective-permute-start.20 = (bf16[96,512]{1,0:T(8,128)(2,1)S(1)}, bf16[96,512]{1,0:T(8,128)(2,1)S(1)}, u32[]{:S(2)}, u32[]{:S(2)}) collective-permute-start(bf16[96,512]{1,0:T(8,128)(2,1)S(1)} %collective-permute-done.18.refs_6_), channel_id=1, source_target_pairs={{8,0},{16,8},{24,16},{28,24},{20,28},{12,20},{4,12},{0,4},{9,1},{1... | collective-permute-start | bytes 294920 | tf_op jit(solution)/shard_map/ppermute | solution.py:481
  55.5 8.4 %collective-permute-start.15 = (bf16[96,512]{1,0:T(8,128)(2,1)S(1)}, bf16[96,512]{1,0:T(8,128)(2,1)S(1)}, u32[]{:S(2)}, u32[]{:S(2)}) collective-permute-start(bf16[96,512]{1,0:T(8,128)(2,1)S(1)} %collective-permute-done.14.refs_12_), channel_id=1, source_target_pairs={{8,0},{16,8},{24,16},{28,24},{20,28},{12,20},{4,12},{0,4},{9,1},{1... | collective-permute-start | bytes 294920 | tf_op jit(solution)/shard_map/ppermute | solution.py:481
  57.1 6.7 %collective-permute-start.11 = (bf16[96,512]{1,0:T(8,128)(2,1)S(1)}, bf16[96,512]{1,0:T(8,128)(2,1)S(1)}, u32[]{:S(2)}, u32[]{:S(2)}) collective-permute-start(bf16[96,512]{1,0:T(8,128)(2,1)S(1)} %collective-permute-done.10.refs_9_), channel_id=1, source_target_pairs={{0,8},{8,16},{16,24},{24,28},{28,20},{20,12},{12,4},{4,0},{1,9},{9... | collective-permute-start | bytes 294920 | tf_op jit(solution)/shard_map/ppermute | solution.py:478
  60.1 3.8 %copy-start.1 = (f32[192,512]{1,0:T(8,128)S(1)}, f32[192,512]{1,0:T(8,128)}, u32[]{:S(2)}) copy-start(f32[192,512]{1,0:T(8,128)} %refs_7_.1) | copy-start | bytes 1179652
  60.1 3.8 %copy-start.2 = (f32[192,512]{1,0:T(8,128)S(1)}, f32[192,512]{1,0:T(8,128)}, u32[]{:S(2)}) copy-start(f32[192,512]{1,0:T(8,128)} %refs_8_.1) | copy-start | bytes 1179652

commit v3 on v2

--- a/solution.py
+++ b/solution.py
@@ -16,7 +16,6 @@
 NT = (((1,), (1,)), ((), ()))
 TN = (((0,), (0,)), ((), ()))
 VMEM_LIMIT = 40 * 1024 * 1024
-OPEN_LIMIT = 62 * 1024 * 1024
 
 
 def against(band_rows, whole_rows, select):
@@ -108,64 +107,6 @@
     return pltpu.CompilerParams(vmem_limit_bytes=limit)
 
 
-def add_send(me, partial, arrived, distance, n, first, *after):
-    band, breadth = partial.shape[1] // n, partial.shape[2]
-    rows = arrived.shape[0]
-
-    def kernel(me_ref, own_ref, a_ref, *refs):
-        out_ref = refs[-1]
-        if rows == band:
-            out_ref[...] = (own_ref[0].astype(F32) + a_ref[...].astype(F32)).astype(BF16)
-        else:
-            got, other = slice(first, first + rows), slice(rows - first, band - first)
-            out_ref[got] = (own_ref[0, got].astype(F32) + a_ref[...].astype(F32)).astype(BF16)
-            out_ref[other] = own_ref[0, other]
-
-    return pl.pallas_call(
-        kernel,
-        out_shape=jax.ShapeDtypeStruct((band, breadth), BF16),
-        grid_spec=pltpu.PrefetchScalarGridSpec(
-            num_scalar_prefetch=1,
-            grid=(1,),
-            in_specs=[
-                pl.BlockSpec((1, band, breadth), lambda i, m: (0, away(m[0], distance, n), 0)),
-                whole(rows, breadth),
-            ]
-            + [pl.BlockSpec(memory_space=pl.ANY)] * len(after),
-            out_specs=whole(band, breadth),
-        ),
-        compiler_params=params(),
-        name="add_send",
-    )(me, partial, arrived, *after)
-
-
-def add_own(me, partial, right, left, n, *after):
-    band, breadth = partial.shape[1] // n, partial.shape[2]
-
-    def kernel(me_ref, own_ref, r_ref, l_ref, *refs):
-        out_ref = refs[-1]
-        total = own_ref[0].astype(F32) + r_ref[...].astype(F32) + l_ref[...].astype(F32)
-        out_ref[...] = total.astype(BF16)
-
-    return pl.pallas_call(
-        kernel,
-        out_shape=jax.ShapeDtypeStruct((band, breadth), BF16),
-        grid_spec=pltpu.PrefetchScalarGridSpec(
-            num_scalar_prefetch=1,
-            grid=(1,),
-            in_specs=[
-                pl.BlockSpec((1, band, breadth), lambda i, m: (0, m[0], 0)),
-                whole(band, breadth),
-                whole(band, breadth),
-            ]
-            + [pl.BlockSpec(memory_space=pl.ANY)] * len(after),
-            out_specs=whole(band, breadth),
-        ),
-        compiler_params=params(),
-        name="add_own",
-    )(me, partial, right, left, *after)
-
-
 PAIR = 2 * TILE
 
 
@@ -185,33 +126,43 @@
     return pl.ds(pl.multiple_of((pair & (breadth // PAIR - 1)) * PAIR, PAIR), PAIR)
 
 
-def open_ring(me, owner, partial, left_root, right_root, n):
+def first_sends(me, partial, n):
+    breadth = partial.shape[2]
+    band = partial.shape[1] // n
+    half = band // 2
+
+    def kernel(me_ref, far_ref, right_ref, left_ref):
+        right_ref[...] = far_ref[0, :half]
+        left_ref[...] = far_ref[0, half:]
+
+    sent = jax.ShapeDtypeStruct((half, breadth), BF16)
+    return pl.pallas_call(
+        kernel,
+        out_shape=(sent, sent),
+        grid_spec=pltpu.PrefetchScalarGridSpec(
+            num_scalar_prefetch=1,
+            grid=(1,),
+            in_specs=[
+                pl.BlockSpec((1, band, breadth), lambda i, m: (0, away(m[0], n // 2, n), 0)),
+            ],
+            out_specs=(whole(half, breadth), whole(half, breadth)),
+        ),
+        compiler_params=params(),
+        name="first_sends",
+    )(me, partial)
+
+
+def pack_roots(me, owner, left_root, right_root, n):
     band, breadth = left_root.shape
-    half = band // 2
     tiles = breadth // TILE
     whole_pairs = tiles // 4
     width = kept(breadth)
 
-    def kernel(me_ref, owner_ref, p_ref, lr_ref, rr_ref, right_ref, left_ref, out_ref, l_ref, r_ref, sems):
-        start = away(me_ref[0], n // 2, n) * band
-        copies = [
-            pltpu.make_async_copy(lr_ref, l_ref, sems.at[0]),
-            pltpu.make_async_copy(rr_ref, r_ref, sems.at[1]),
-            pltpu.make_async_copy(
-                p_ref.at[0, pl.ds(pl.multiple_of(start, half), half)], right_ref, sems.at[2]
-            ),
-            pltpu.make_async_copy(
-                p_ref.at[0, pl.ds(pl.multiple_of(start + half, half), half)], left_ref, sems.at[3]
-            ),
-        ]
-        for copy in copies:
-            copy.start()
-        k = band_of(owner_ref, me_ref[0], n)
+    def kernel(me_ref, owner_ref, l_ref, r_ref, out_ref):
+        number = band_of(owner_ref, me_ref[0], n)
         low = lax.broadcasted_iota(jnp.int32, (TILE, PAIR), 1) < TILE
-        copies[0].wait()
-        copies[1].wait()
         for row in range(0, band, TILE):
-            tile = (k * (band // TILE) + row // TILE) & (tiles - 1)
+            tile = (number * (band // TILE) + row // TILE) & (tiles - 1)
             first, half_pair, even = pairs_of(tile, breadth)
             rows = slice(row, row + TILE)
             for i in range(whole_pairs):
@@ -222,23 +173,77 @@
             right = pltpu.roll(r_ref[rows, lanes(half_pair, breadth)].astype(F32), TILE, 1)
             mine = jnp.where(low == even, left, right)
             out_ref[rows, 2 * whole_pairs * PAIR :] = mine.astype(BF16)
-        copies[2].wait()
-        copies[3].wait()
-
-    sent = jax.ShapeDtypeStruct((half, breadth), BF16)
-    return pl.pallas_call(
-        kernel,
-        out_shape=(sent, sent, jax.ShapeDtypeStruct((band, 2 * width), BF16)),
+
+    return pl.pallas_call(
+        kernel,
+        out_shape=jax.ShapeDtypeStruct((band, 2 * width), BF16),
         grid_spec=pltpu.PrefetchScalarGridSpec(
             num_scalar_prefetch=2,
             grid=(1,),
-            in_specs=[pl.BlockSpec(memory_space=pltpu.HBM)] * 3,
-            out_specs=(whole(half, breadth), whole(half, breadth), whole(band, 2 * width)),
-            scratch_shapes=[pltpu.VMEM((band, breadth), BF16)] * 2 + [pltpu.SemaphoreType.DMA((4,))],
-        ),
-        compiler_params=params(OPEN_LIMIT),
-        name="open_ring",
-    )(me, owner, partial, left_root, right_root)
+            in_specs=[whole(band, breadth), whole(band, breadth)],
+            out_specs=whole(band, 2 * width),
+        ),
+        compiler_params=params(),
+        name="pack_roots",
+    )(me, owner, left_root, right_root)
+
+
+def add_send(me, partial, arrived, distance, n, first, *after):
+    band, breadth = partial.shape[1] // n, partial.shape[2]
+    rows = arrived.shape[0]
+
+    def kernel(me_ref, own_ref, a_ref, *refs):
+        out_ref = refs[-1]
+        if rows == band:
+            out_ref[...] = (own_ref[0].astype(F32) + a_ref[...].astype(F32)).astype(BF16)
+        else:
+            got, other = slice(first, first + rows), slice(rows - first, band - first)
+            out_ref[got] = (own_ref[0, got].astype(F32) + a_ref[...].astype(F32)).astype(BF16)
+            out_ref[other] = own_ref[0, other]
+
+    return pl.pallas_call(
+        kernel,
+        out_shape=jax.ShapeDtypeStruct((band, breadth), BF16),
+        grid_spec=pltpu.PrefetchScalarGridSpec(
+            num_scalar_prefetch=1,
+            grid=(1,),
+            in_specs=[
+                pl.BlockSpec((1, band, breadth), lambda i, m: (0, away(m[0], distance, n), 0)),
+                whole(rows, breadth),
+            ]
+            + [pl.BlockSpec(memory_space=pl.ANY)] * len(after),
+            out_specs=whole(band, breadth),
+        ),
+        compiler_params=params(),
+        name="add_send",
+    )(me, partial, arrived, *after)
+
+
+def add_own(me, partial, right, left, n, *after):
+    band, breadth = partial.shape[1] // n, partial.shape[2]
+
+    def kernel(me_ref, own_ref, r_ref, l_ref, *refs):
+        out_ref = refs[-1]
+        total = own_ref[0].astype(F32) + r_ref[...].astype(F32) + l_ref[...].astype(F32)
+        out_ref[...] = total.astype(BF16)
+
+    return pl.pallas_call(
+        kernel,
+        out_shape=jax.ShapeDtypeStruct((band, breadth), BF16),
+        grid_spec=pltpu.PrefetchScalarGridSpec(
+            num_scalar_prefetch=1,
+            grid=(1,),
+            in_specs=[
+                pl.BlockSpec((1, band, breadth), lambda i, m: (0, m[0], 0)),
+                whole(band, breadth),
+                whole(band, breadth),
+            ]
+            + [pl.BlockSpec(memory_space=pl.ANY)] * len(after),
+            out_specs=whole(band, breadth),
+        ),
+        compiler_params=params(),
+        name="add_own",
+    )(me, partial, right, left, *after)
 
 
 def unpack_roots(me, owner, pieces, stacked, breadth, n):
@@ -248,19 +253,26 @@
     nblocks = stacked // breadth
 
     def kernel(me_ref, owner_ref, *refs):
-        refs, (left_ref, right_ref, half_l, half_r) = refs[: len(pieces)], refs[len(pieces) :]
+        refs, (left_ref, right_ref, half_l, half_r, table, sem) = refs[: len(pieces)], refs[len(pieces) :]
+        copy = pltpu.make_async_copy(owner_ref, table, sem)
+        copy.start()
         lower = lax.broadcasted_iota(jnp.int32, (TILE, PAIR), 1) < TILE
         nothing = jnp.zeros((TILE, PAIR), BF16)
-        bands = {}
+        shift = TILE.bit_length() - 1
+        down = lax.broadcasted_iota(jnp.int32, (breadth, breadth), 0) >> shift
+        over = lax.broadcasted_iota(jnp.int32, (breadth, breadth), 1) >> shift
+        apart = over - down + jnp.where(over < down, tiles, 0)
+        mirrored = (apart > 0) & (apart < tiles // 2)
+        copy.wait()
+        numbers = {o: band_of(table, away(me_ref[0], o, n), n) for o in {p[0] for p in pieces}}
         for (offset, first, _), ref in zip(pieces, refs):
-            if offset not in bands:
-                bands[offset] = band_of(owner_ref, away(me_ref[0], offset, n), n)
+            number = numbers[offset]
             edges = sorted({first, first + ref.shape[0], *range(0, band + 1, TILE)})
             edges = [x for x in edges if first <= x <= first + ref.shape[0]]
             for row, end in zip(edges[:-1], edges[1:]):
-                tile = (bands[offset] * (band // TILE) + row // TILE) & (tiles - 1)
+                tile = (number * (band // TILE) + row // TILE) & (tiles - 1)
                 start, half_pair, even = pairs_of(tile, breadth)
-                at = pl.ds(pl.multiple_of(bands[offset] * band + row, CHUNK), end - row)
+                at = pl.ds(pl.multiple_of(number * band + row, CHUNK), end - row)
                 rows = slice(row - first, end - first)
                 low = lower[: end - row]
                 zeros = nothing[: end - row]
@@ -279,11 +291,6 @@
                         half_r[at, pair] = zeros
                 half_l[at, lanes(half_pair, breadth)] = left
                 half_r[at, lanes(half_pair, breadth)] = right
-        shift = TILE.bit_length() - 1
-        down = lax.broadcasted_iota(jnp.int32, (breadth, breadth), 0) >> shift
-        over = lax.broadcasted_iota(jnp.int32, (breadth, breadth), 1) >> shift
-        apart = over - down + jnp.where(over < down, tiles, 0)
-        mirrored = (apart > 0) & (apart < tiles // 2)
         for half, out in ((half_r, right_ref), (half_l, left_ref)):
             for b in range(nblocks):
                 rows = slice(b * breadth, (b + 1) * breadth)
@@ -295,11 +302,12 @@
         kernel,
         out_shape=(out, out),
         grid_spec=pltpu.PrefetchScalarGridSpec(
-            num_scalar_prefetch=2,
-            grid=(1,),
-            in_specs=[whole(*x.shape) for _, _, x in pieces],
+            num_scalar_prefetch=1,
+            grid=(1,),
+            in_specs=[pl.BlockSpec(memory_space=pl.ANY)] + [whole(*x.shape) for _, _, x in pieces],
             out_specs=(whole(stacked, breadth), whole(stacked, breadth)),
-            scratch_shapes=[pltpu.VMEM((stacked, breadth), BF16)] * 2,
+            scratch_shapes=[pltpu.VMEM((stacked, breadth), BF16)] * 2
+            + [pltpu.SMEM((n,), jnp.int32), pltpu.SemaphoreType.DMA],
         ),
         compiler_params=params(),
         name="unpack_roots",
@@ -355,11 +363,14 @@
 def finish(me, owner, pieces, directions, grad, rest, left_root, right_root, left_factor, right_factor, n):
     stacked, breadth = left_root.shape
     band = stacked // n
+    nblocks = stacked // breadth
 
     def kernel(me_ref, owner_ref, *refs):
         parts, refs = refs[: len(pieces)], refs[len(pieces) :]
-        _, grad_ref, rest_ref, lroot, rroot, lfac, rfac, *refs = refs
-        dir_ref, lout_ref, rout_ref, late, block, lout, rout, sems = refs
+        part_ref, grad_ref, rest_ref, lroot, rroot, lfac, rfac, *refs = refs
+        dir_ref, lout_ref, rout_ref, late, block, lout, rout, table, sems = refs
+        lookup = pltpu.make_async_copy(owner_ref, table, sems.at[4 + nblocks])
+        lookup.start()
         far = away(me_ref[0], n // 2, n) * band
         for (_, first, _), ref in zip(pieces, parts):
             late[first : first + ref.shape[0]] = ref[...]
@@ -375,6 +386,16 @@
         def copy(slot, number):
             return pltpu.make_async_copy(block.at[slot], dir_ref.at[span(number)], sems.at[slot])
 
+        def keep(b):
+            rows = slice(b * breadth, (b + 1) * breadth)
+            return pltpu.make_async_copy(part_ref.at[rows], dir_ref.at[rows], sems.at[4 + b])
+
+        for b in range(nblocks):
+
+            @pl.when((first_block != b) & (last_block != b))
+            def _():
+                keep(b).start()
+
         def complete(slot, number):
             some = jnp.where(row == number, late[...].astype(F32), 0.0).astype(BF16)
             mixed = jnp.dot(some, rroot[span(number), :], preferred_element_type=F32).astype(BF16)
@@ -388,7 +409,8 @@
         def _():
             complete(1, last_block)
 
-        start = band_of(owner_ref, me_ref[0], n) * band
+        lookup.wait()
+        start = band_of(table, me_ref[0], n) * band
         grad_ref[there, :] = late[...]
         mine = grad_ref[pl.ds(pl.multiple_of(start, CHUNK), band), :]
         own_first = start >> shift
@@ -425,6 +447,12 @@
         def _():
             copy(1, last_block).wait()
 
+        for b in range(nblocks):
+
+            @pl.when((first_block != b) & (last_block != b))
+            def _():
+                keep(b).wait()
+
         for out in outs:
             out.wait()
 
@@ -433,10 +461,12 @@
         kernel,
         out_shape=(jax.ShapeDtypeStruct((stacked, breadth), BF16), own, own),
         grid_spec=pltpu.PrefetchScalarGridSpec(
-            num_scalar_prefetch=2,
-            grid=(1,),
-            in_specs=[whole(*x.shape) for _, _, x in pieces]
-            + [pl.BlockSpec(memory_space=pl.ANY), whole(stacked, breadth), whole(2, breadth, breadth)]
+            num_scalar_prefetch=1,
+            grid=(1,),
+            in_specs=[pl.BlockSpec(memory_space=pl.ANY)]
+            + [whole(*x.shape) for _, _, x in pieces]
+            + [whole(stacked, breadth)] * 2
+            + [whole(2, breadth, breadth)]
             + [whole(stacked, breadth)] * 2
             + [whole(band, breadth)] * 2,
             out_specs=[pl.BlockSpec(memory_space=pl.ANY)] * 3,
@@ -445,10 +475,10 @@
                 pltpu.VMEM((2, breadth, breadth), BF16),
                 pltpu.VMEM((band, breadth), F32),
                 pltpu.VMEM((band, breadth), F32),
-                pltpu.SemaphoreType.DMA((4,)),
+                pltpu.SMEM((n,), jnp.int32),
+                pltpu.SemaphoreType.DMA((5 + nblocks,)),
             ],
         ),
-        input_output_aliases={2 + len(pieces): 0},
         compiler_params=params(),
         name="finish",
     )(
@@ -504,7 +534,8 @@
             right, left = send_right(ways[0]), send_left(ways[3])
         return pieces + [(n // 2, 0, right), (n // 2, rows, left)]
 
-    right, left, packed = open_ring(me, band_owner, partial_grads, left_root, right_root, n)
+    right, left = first_sends(me, partial_grads, n)
+    packed = pack_roots(me, band_owner, left_root, right_root, n)
     right, left = send_right(right), send_left(left)
     root_pieces = gather(packed, 1)
     for distance in range(n // 2 - 1, 0, -1):

time: 66.8 us -> 63.4 us (0.949)
  Pallas kernels: 12.1 us -> 8.28 us
  local copies, waits for them, and re-layouts: 0.07 us -> 1.47 us
  waiting for transfers between devices: 20.3 us -> 19.4 us
    pallas_call x1 -> x2, Pallas kernels: 2.73 us -> 0.69 us  [the longest x1 0.68 us: pack_roots(): pl.pallas_call(kernel, out_shape=jax.ShapeDtypeStruct((band, 2 * width),...]
    unnamed x10 -> x14, local copies, waits for them, and re-layouts: 0.03 us -> 1.43 us
    pallas_call x1, Pallas kernels: 3.74 us -> 2.59 us  [begin(): pl.pallas_call(kernel, out_shape=(jax.ShapeDtypeStruct((stacked, breadth)...]
    ppermute x15, starting transfers between devices: 27.9 us -> 26.9 us  [send_left(): return lax.ppermute(x, 'dp', backward)]
    ppermute x15, starting transfers between devices: 5.46 us -> 6.32 us  [send_right(): return lax.ppermute(x, 'dp', onward)]
    ppermute x15, waiting for transfers between devices: 17.6 us -> 16.7 us  [send_left(): return lax.ppermute(x, 'dp', backward)]
where the time goes in v3:
time: 63.4 us; the launch traced here: 63.2 us
  starting transfers between devices  33.3 us (53%)
  waiting for transfers between devices  19.4 us (31%)
  Pallas kernels  8.28 us (13%)
  local copies, waits for them, and re-layouts  1.47 us (2%)
  between operations  0.84 us (1%)
    ppermute x15, starting transfers between devices, send_left(): return lax.ppermute(x, 'dp', backward)  26.9 us
    ppermute x15, waiting for transfers between devices, send_left(): return lax.ppermute(x, 'dp', backward)  16.7 us
    ppermute x15, starting transfers between devices, send_right(): return lax.ppermute(x, 'dp', onward)  6.32 us
    ppermute x15, waiting for transfers between devices, send_right(): return lax.ppermute(x, 'dp', onward)  2.66 us
    pallas_call x1, Pallas kernels, begin(): pl.pallas_call(kernel, out_shape=(jax.ShapeDtypeStruct((stacked, breadth)...  2.59 us
    pallas_call x1, Pallas kernels, unpack_roots(): pl.pallas_call(kernel, out_shape=(out, out), grid_spec=pltpu.PrefetchScal...  2.38 us
    pallas_call x1, Pallas kernels, finish(): pl.pallas_call(kernel, out_shape=(jax.ShapeDtypeStruct((stacked, breadth)...  2.25 us
    unnamed x14, local copies, waits for them, and re-layouts  1.43 us
  transfers between devices with their start and end apart: 30, of which 12 were waited for; matrix products, arithmetic and copies ran while one was open for 0% of the time, Pallas kernels for 10%

profile of v3, /device:TPU:0, one launch (start us, length us, event | category | flops | bytes accessed | tf_op | source)
XLA Modules:
  0.0 63.2 jit_solution(13499421939409047904)
XLA Ops:
  0.6 1.4 %copy-done = bf16[1,1536,512]{2,1,0:T(8,128)(2,1)S(1)} copy-done((bf16[1,1536,512]{2,1,0:T(8,128)(2,1)S(1)}, bf16[1,1536,512]{2,1,0:T(8,128)(2,1)}, u32[]{:S(2)}) %copy-start) | copy-done | bytes 1572888
  2.1 3.0 %collective-permute-start.4 = (bf16[96,512]{1,0:T(8,128)(2,1)S(1)}, bf16[96,512]{1,0:T(8,128)(2,1)S(1)}, u32[]{:S(2)}, u32[]{:S(2)}) collective-permute-start(bf16[96,512]{1,0:T(8,128)(2,1)S(1)} %get-tuple-element.11), channel_id=1, source_target_pairs={{8,0},{16,8},{24,16},{28,24},{20,28},{12,20},{4,12},{0,4},{9,1},{1... | collective-permute-start | bytes 294920 | tf_op jit(solution)/shard_map/ppermute | solution.py:511
  5.1 0.2 collective-permute-start
  5.2 2.7 %collective-permute-done.4.a_ref = bf16[96,512]{1,0:T(8,128)(2,1)S(1)} collective-permute-done((bf16[96,512]{1,0:T(8,128)(2,1)S(1)}, bf16[96,512]{1,0:T(8,128)(2,1)S(1)}, u32[]{:S(2)}, u32[]{:S(2)}) %collective-permute-start.4) | collective-permute-done | bytes 98336 | tf_op jit(solution)/shard_map/ppermute | solution.py:511
  8.0 1.8 %collective-permute-start.5 = (bf16[192,512]{1,0:T(8,128)(2,1)S(1)}, bf16[192,512]{1,0:T(8,128)(2,1)S(1)}, u32[]{:S(2)}, u32[]{:S(2)}) collective-permute-start(bf16[192,512]{1,0:T(8,128)(2,1)S(1)} %add_send.9), channel_id=1, source_target_pairs={{8,0},{16,8},{24,16},{28,24},{20,28},{12,20},{4,12},{0,4},{9,1},{1... | collective-permute-start | bytes 589832 | tf_op jit(solution)/shard_map/ppermute | solution.py:511
  9.8 0.3 collective-permute-start.1
  10.2 0.7 %pack_roots.1.refs_0_ = bf16[192,640]{1,0:T(8,128)(2,1)S(1)} custom-call(s32[1]{0:T(128)} %bitcast.me_ref, s32[8]{0:T(128)S(1)} %copy-done.6, bf16[192,512]{1,0:T(8,128)(2,1)S(1)} %copy-done.4, bf16[192,512]{1,0:T(8,128)(2,1)S(1)} %copy-done.5), custom_call_target="tpu_custom_call" | custom-call | tf_op jit(solution)/shard_map/pack_roots/pallas_call | solution.py:177
  10.8 1.8 %collective-permute-start.23 = (bf16[192,640]{1,0:T(8,128)(2,1)S(1)}, bf16[192,640]{1,0:T(8,128)(2,1)S(1)}, u32[]{:S(2)}, u32[]{:S(2)}) collective-permute-start(bf16[192,640]{1,0:T(8,128)(2,1)S(1)} %pack_roots.1.refs_0_), channel_id=1, source_target_pairs={{8,0},{16,8},{24,16},{28,24},{20,28},{12,20},{4,12},{0,4},{9,1},{1... | collective-permute-start | bytes 737288 | tf_op jit(solution)/shard_map/ppermute | solution.py:511
  12.6 0.3 collective-permute-start.22
  12.9 3.0 %collective-permute-done.5.a_ref = bf16[192,512]{1,0:T(8,128)(2,1)S(1)} collective-permute-done((bf16[192,512]{1,0:T(8,128)(2,1)S(1)}, bf16[192,512]{1,0:T(8,128)(2,1)S(1)}, u32[]{:S(2)}, u32[]{:S(2)}) %collective-permute-start.5) | collective-permute-done | bytes 196640 | tf_op jit(solution)/shard_map/ppermute | solution.py:511
  15.9 1.7 %collective-permute-start.6 = (bf16[192,512]{1,0:T(8,128)(2,1)S(1)}, bf16[192,512]{1,0:T(8,128)(2,1)S(1)}, u32[]{:S(2)}, u32[]{:S(2)}) collective-permute-start(bf16[192,512]{1,0:T(8,128)(2,1)S(1)} %add_send.10), channel_id=1, source_target_pairs={{8,0},{16,8},{24,16},{28,24},{20,28},{12,20},{4,12},{0,4},{9,1},{1... | collective-permute-start | bytes 589832 | tf_op jit(solution)/shard_map/ppermute | solution.py:511
  17.7 0.1 add_send.7
  17.7 0.4 collective-permute-start.2
  18.1 3.0 %collective-permute-done.23.refs_2_ = bf16[192,640]{1,0:T(8,128)(2,1)S(1)} collective-permute-done((bf16[192,640]{1,0:T(8,128)(2,1)S(1)}, bf16[192,640]{1,0:T(8,128)(2,1)S(1)}, u32[]{:S(2)}, u32[]{:S(2)}) %collective-permute-start.23) | collective-permute-done | bytes 245792 | tf_op jit(solution)/shard_map/ppermute | solution.py:511
  21.1 1.7 %collective-permute-start.25 = (bf16[192,640]{1,0:T(8,128)(2,1)S(1)}, bf16[192,640]{1,0:T(8,128)(2,1)S(1)}, u32[]{:S(2)}, u32[]{:S(2)}) collective-permute-start(bf16[192,640]{1,0:T(8,128)(2,1)S(1)} %collective-permute-done.23.refs_2_), channel_id=1, source_target_pairs={{8,0},{16,8},{24,16},{28,24},{20,28},{12,20},{4,12},{0,4},{9,1},{1... | collective-permute-start | bytes 737288 | tf_op jit(solution)/shard_map/ppermute | solution.py:511
  22.8 0.4 collective-permute-start.24
  23.2 2.1 %collective-permute-done.6.a_ref = bf16[192,512]{1,0:T(8,128)(2,1)S(1)} collective-permute-done((bf16[192,512]{1,0:T(8,128)(2,1)S(1)}, bf16[192,512]{1,0:T(8,128)(2,1)S(1)}, u32[]{:S(2)}, u32[]{:S(2)}) %collective-permute-start.6) | collective-permute-done | bytes 196640 | tf_op jit(solution)/shard_map/ppermute | solution.py:511
  25.3 0.1 add_send.11
  25.4 1.7 %collective-permute-start.7 = (bf16[192,512]{1,0:T(8,128)(2,1)S(1)}, bf16[192,512]{1,0:T(8,128)(2,1)S(1)}, u32[]{:S(2)}, u32[]{:S(2)}) collective-permute-start(bf16[192,512]{1,0:T(8,128)(2,1)S(1)} %add_send.11), channel_id=1, source_target_pairs={{8,0},{16,8},{24,16},{28,24},{20,28},{12,20},{4,12},{0,4},{9,1},{1... | collective-permute-start | bytes 589832 | tf_op jit(solution)/shard_map/ppermute | solution.py:511
  27.2 0.4 collective-permute-start.3
  27.6 3.0 %collective-permute-done.25.refs_4_ = bf16[192,640]{1,0:T(8,128)(2,1)S(1)} collective-permute-done((bf16[192,640]{1,0:T(8,128)(2,1)S(1)}, bf16[192,640]{1,0:T(8,128)(2,1)S(1)}, u32[]{:S(2)}, u32[]{:S(2)}) %collective-permute-start.25) | collective-permute-done | bytes 245792 | tf_op jit(solution)/shard_map/ppermute | solution.py:511
  30.6 1.7 %collective-permute-start.27 = (bf16[192,640]{1,0:T(8,128)(2,1)S(1)}, bf16[192,640]{1,0:T(8,128)(2,1)S(1)}, u32[]{:S(2)}, u32[]{:S(2)}) collective-permute-start(bf16[192,640]{1,0:T(8,128)(2,1)S(1)} %collective-permute-done.25.refs_4_), channel_id=1, source_target_pairs={{8,0},{16,8},{24,16},{28,24},{20,28},{12,20},{4,12},{0,4},{9,1},{1... | collective-permute-start | bytes 737288 | tf_op jit(solution)/shard_map/ppermute | solution.py:511
  32.3 0.4 collective-permute-start.26
  32.7 2.1 %collective-permute-done.7.l_ref = bf16[192,512]{1,0:T(8,128)(2,1)S(1)} collective-permute-done((bf16[192,512]{1,0:T(8,128)(2,1)S(1)}, bf16[192,512]{1,0:T(8,128)(2,1)S(1)}, u32[]{:S(2)}, u32[]{:S(2)}) %collective-permute-start.7) | collective-permute-done | bytes 196640 | tf_op jit(solution)/shard_map/ppermute | solution.py:511
  34.8 1.7 %collective-permute-done.3.r_ref = bf16[192,512]{1,0:T(8,128)(2,1)S(1)} collective-permute-done((bf16[192,512]{1,0:T(8,128)(2,1)S(1)}, bf16[192,512]{1,0:T(8,128)(2,1)S(1)}, u32[]{:S(2)}, u32[]{:S(2)}) %collective-permute-start.3) | collective-permute-done | bytes 196640 | tf_op jit(solution)/shard_map/ppermute | solution.py:508
  36.5 0.1 add_own.1.refs_0_
  36.6 1.7 %collective-permute-start.12 = (bf16[96,512]{1,0:T(8,128)(2,1)S(1)}, bf16[96,512]{1,0:T(8,128)(2,1)S(1)}, u32[]{:S(2)}, u32[]{:S(2)}) collective-permute-start(bf16[96,512]{1,0:T(8,128)(2,1)S(1)} %get-tuple-element.17), channel_id=1, source_target_pairs={{8,0},{16,8},{24,16},{28,24},{20,28},{12,20},{4,12},{0,4},{9,1},{1... | collective-permute-start | bytes 294920 | tf_op jit(solution)/shard_map/ppermute | solution.py:511
  38.3 0.4 collective-permute-start.8
  38.7 0.4 collective-permute-start.17
  39.1 0.3 collective-permute-done.27.refs_6_
  39.4 1.7 %collective-permute-start.16 = (bf16[96,512]{1,0:T(8,128)(2,1)S(1)}, bf16[96,512]{1,0:T(8,128)(2,1)S(1)}, u32[]{:S(2)}, u32[]{:S(2)}) collective-permute-start(bf16[96,512]{1,0:T(8,128)(2,1)S(1)} %get-tuple-element.18), channel_id=1, source_target_pairs={{8,0},{16,8},{24,16},{28,24},{20,28},{12,20},{4,12},{0,4},{9,1},{1... | collective-permute-start | bytes 294920 | tf_op jit(solution)/shard_map/ppermute | solution.py:511
  41.1 0.5 collective-permute-done.12.refs_4_
  41.6 2.0 %collective-permute-start.13 = (bf16[96,512]{1,0:T(8,128)(2,1)S(1)}, bf16[96,512]{1,0:T(8,128)(2,1)S(1)}, u32[]{:S(2)}, u32[]{:S(2)}) collective-permute-start(bf16[96,512]{1,0:T(8,128)(2,1)S(1)} %collective-permute-done.12.refs_4_), channel_id=1, source_target_pairs={{8,0},{16,8},{24,16},{28,24},{20,28},{12,20},{4,12},{0,4},{9,1},{1... | collective-permute-start | bytes 294920 | tf_op jit(solution)/shard_map/ppermute | solution.py:511
  43.6 0.2 collective-permute-done.8.refs_1_
  43.8 2.1 %collective-permute-start.29 = (bf16[96,640]{1,0:T(8,128)(2,1)S(1)}, bf16[96,640]{1,0:T(8,128)(2,1)S(1)}, u32[]{:S(2)}, u32[]{:S(2)}) collective-permute-start(bf16[96,640]{1,0:T(8,128)(2,1)S(1)} %slice.19), channel_id=1, source_target_pairs={{8,0},{16,8},{24,16},{28,24},{20,28},{12,20},{4,12},{0,4},{9,1},{1... | collective-permute-start | bytes 368648 | tf_op jit(solution)/shard_map/ppermute | solution.py:511
  45.9 2.0 %collective-permute-start.18 = (bf16[96,512]{1,0:T(8,128)(2,1)S(1)}, bf16[96,512]{1,0:T(8,128)(2,1)S(1)}, u32[]{:S(2)}, u32[]{:S(2)}) collective-permute-start(bf16[96,512]{1,0:T(8,128)(2,1)S(1)} %collective-permute-done.16.refs_2_), channel_id=1, source_target_pairs={{8,0},{16,8},{24,16},{28,24},{20,28},{12,20},{4,12},{0,4},{9,1},{1... | collective-permute-start | bytes 294920 | tf_op jit(solution)/shard_map/ppermute | solution.py:511
  47.9 1.6 %collective-permute-start.14 = (bf16[96,512]{1,0:T(8,128)(2,1)S(1)}, bf16[96,512]{1,0:T(8,128)(2,1)S(1)}, u32[]{:S(2)}, u32[]{:S(2)}) collective-permute-start(bf16[96,512]{1,0:T(8,128)(2,1)S(1)} %collective-permute-done.13.refs_8_), channel_id=1, source_target_pairs={{8,0},{16,8},{24,16},{28,24},{20,28},{12,20},{4,12},{0,4},{9,1},{1... | collective-permute-start | bytes 294920 | tf_op jit(solution)/shard_map/ppermute | solution.py:511
  49.5 0.5 collective-permute-start.10
  50.0 1.1 %collective-permute-start.28 = (bf16[96,640]{1,0:T(8,128)(2,1)S(1)}, bf16[96,640]{1,0:T(8,128)(2,1)S(1)}, u32[]{:S(2)}, u32[]{:S(2)}) collective-permute-start(bf16[96,640]{1,0:T(8,128)(2,1)S(1)} %slice.18), channel_id=1, source_target_pairs={{0,8},{8,16},{16,24},{24,28},{28,20},{20,12},{12,4},{4,0},{1,9},{9... | collective-permute-start | bytes 368648 | tf_op jit(solution)/shard_map/ppermute | solution.py:508
  51.0 0.6 collective-permute-done.19.refs_7_
  51.6 1.0 %collective-permute-start.21 = (bf16[96,512]{1,0:T(8,128)(2,1)S(1)}, bf16[96,512]{1,0:T(8,128)(2,1)S(1)}, u32[]{:S(2)}, u32[]{:S(2)}) collective-permute-start(bf16[96,512]{1,0:T(8,128)(2,1)S(1)} %collective-permute-done.19.refs_7_), channel_id=1, source_target_pairs={{0,8},{8,16},{16,24},{24,28},{28,20},{20,12},{12,4},{4,0},{1,9},{9... | collective-permute-start | bytes 294920 | tf_op jit(solution)/shard_map/ppermute | solution.py:508
  52.6 1.0 %collective-permute-start.20 = (bf16[96,512]{1,0:T(8,128)(2,1)S(1)}, bf16[96,512]{1,0:T(8,128)(2,1)S(1)}, u32[]{:S(2)}, u32[]{:S(2)}) collective-permute-start(bf16[96,512]{1,0:T(8,128)(2,1)S(1)} %collective-permute-done.18.refs_6_), channel_id=1, source_target_pairs={{8,0},{16,8},{24,16},{28,24},{20,28},{12,20},{4,12},{0,4},{9,1},{1... | collective-permute-start | bytes 294920 | tf_op jit(solution)/shard_map/ppermute | solution.py:511
  53.6 1.6 %collective-permute-start.15 = (bf16[96,512]{1,0:T(8,128)(2,1)S(1)}, bf16[96,512]{1,0:T(8,128)(2,1)S(1)}, u32[]{:S(2)}, u32[]{:S(2)}) collective-permute-start(bf16[96,512]{1,0:T(8,128)(2,1)S(1)} %collective-permute-done.14.refs_12_), channel_id=1, source_target_pairs={{8,0},{16,8},{24,16},{28,24},{20,28},{12,20},{4,12},{0,4},{9,1},{1... | collective-permute-start | bytes 294920 | tf_op jit(solution)/shard_map/ppermute | solution.py:511
  55.2 0.5 collective-permute-start.11
  55.7 0.2 collective-permute-done.28.refs_7_
  55.9 2.4 %unpack_roots.1 = (bf16[1536,512]{1,0:T(8,128)(2,1)S(1)}, bf16[1536,512]{1,0:T(8,128)(2,1)S(1)}) custom-call(s32[1]{0:T(128)} %bitcast.me_ref, s32[8]{0:T(128)S(1)} %copy-done.6, bf16[192,640]{1,0:T(8,128)(2,1)S(1)} %pack_roots.1.refs_0_, bf16[192,640]{1,0:T(8,128)(2,1)S(1)} %collective-permute-done.22.refs_1_, ...), custom_call_target="tpu_custom_call" | custom-call | tf_op jit(solution)/shard_map/unpack_roots/pallas_call | solution.py:301
  58.3 2.6 %begin.1 = (bf16[1536,512]{1,0:T(8,128)(2,1)S(1)}, bf16[1536,512]{1,0:T(8,128)(2,1)S(1)}, f32[2,512,512]{2,1,0:T(8,128)S(1)}) custom-call(s32[1]{0:T(128)} %bitcast.me_ref, bf16[192,512]{1,0:T(8,128)(2,1)S(1)} %add_own.1.refs_0_, bf16[96,512]{1,0:T(8,128)(2,1)S(1)} %collective-permute-done.8.refs_1_, bf16[96,512]{1,0:T(8,128)(2,1)S(1)} %collective-permute-done.16.refs_2_, ...), custom_call_target="tpu_custom_call" | custom-call | tf_op jit(solution)/shard_map/begin/pallas_call | solution.py:341
  60.9 2.3 %finish.1 = (bf16[1536,512]{1,0:T(8,128)(2,1)}, f32[192,512]{1,0:T(8,128)}, f32[192,512]{1,0:T(8,128)}) custom-call(s32[1]{0:T(128)} %bitcast.me_ref, s32[8]{0:T(128)S(1)} %copy-done.6, bf16[96,512]{1,0:T(8,128)(2,1)S(1)} %collective-permute-done.11.refs_0_, bf16[96,512]{1,0:T(8,128)(2,1)S(1)} %collective-permute-done.15.refs_1_, ...), custom_call_target="tpu_custom_call" | custom-call | tf_op jit(solution)/shard_map/finish/pallas_call | solution.py:460
  (41 shorter events, 0.3 us)
Async XLA Ops:
  0.6 1.4 %copy-start = (bf16[1,1536,512]{2,1,0:T(8,128)(2,1)S(1)}, bf16[1,1536,512]{2,1,0:T(8,128)(2,1)}, u32[]{:S(2)}) copy-start(bf16[1,1536,512]{2,1,0:T(8,128)(2,1)} %own_ref.13) | copy-start | bytes 4718596
  2.1 5.9 %collective-permute-start.4 = (bf16[96,512]{1,0:T(8,128)(2,1)S(1)}, bf16[96,512]{1,0:T(8,128)(2,1)S(1)}, u32[]{:S(2)}, u32[]{:S(2)}) collective-permute-start(bf16[96,512]{1,0:T(8,128)(2,1)S(1)} %get-tuple-element.11), channel_id=1, source_target_pairs={{8,0},{16,8},{24,16},{28,24},{20,28},{12,20},{4,12},{0,4},{9,1},{1... | collective-permute-start | bytes 294920 | tf_op jit(solution)/shard_map/ppermute | solution.py:511
  5.1 5.1 %copy-start.4 = (bf16[192,512]{1,0:T(8,128)(2,1)S(1)}, bf16[192,512]{1,0:T(8,128)(2,1)}, u32[]{:S(2)}) copy-start(bf16[192,512]{1,0:T(8,128)(2,1)} %l_ref.1) | copy-start | bytes 589828
  5.1 5.1 %copy-start.5 = (bf16[192,512]{1,0:T(8,128)(2,1)S(1)}, bf16[192,512]{1,0:T(8,128)(2,1)}, u32[]{:S(2)}) copy-start(bf16[192,512]{1,0:T(8,128)(2,1)} %r_ref.1) | copy-start | bytes 589828
  5.1 5.1 %copy-start.6 = (s32[8]{0:T(128)S(1)}, s32[8]{0:T(128)}, u32[]{:S(2)}) copy-start(s32[8]{0:T(128)} %owner_ref.5) | copy-start | bytes 100
  5.1 4.7 %collective-permute-start = (bf16[96,512]{1,0:T(8,128)(2,1)S(1)}, bf16[96,512]{1,0:T(8,128)(2,1)S(1)}, u32[]{:S(2)}, u32[]{:S(2)}) collective-permute-start(bf16[96,512]{1,0:T(8,128)(2,1)S(1)} %get-tuple-element.10), channel_id=1, source_target_pairs={{0,8},{8,16},{16,24},{24,28},{28,20},{20,12},{12,4},{4,0},{1,9},{9... | collective-permute-start | bytes 294920 | tf_op jit(solution)/shard_map/ppermute | solution.py:508
  8.0 7.9 %copy-start.1 = (bf16[1,1536,512]{2,1,0:T(8,128)(2,1)S(1)}, bf16[1,1536,512]{2,1,0:T(8,128)(2,1)}, u32[]{:S(2)}) copy-start(bf16[1,1536,512]{2,1,0:T(8,128)(2,1)} %own_ref.13) | copy-start | bytes 4718596
  8.0 7.9 %collective-permute-start.5 = (bf16[192,512]{1,0:T(8,128)(2,1)S(1)}, bf16[192,512]{1,0:T(8,128)(2,1)S(1)}, u32[]{:S(2)}, u32[]{:S(2)}) collective-permute-start(bf16[192,512]{1,0:T(8,128)(2,1)S(1)} %add_send.9), channel_id=1, source_target_pairs={{8,0},{16,8},{24,16},{28,24},{20,28},{12,20},{4,12},{0,4},{9,1},{1... | collective-permute-start | bytes 589832 | tf_op jit(solution)/shard_map/ppermute | solution.py:511
  9.8 7.8 %collective-permute-start.1 = (bf16[192,512]{1,0:T(8,128)(2,1)S(1)}, bf16[192,512]{1,0:T(8,128)(2,1)S(1)}, u32[]{:S(2)}, u32[]{:S(2)}) collective-permute-start(bf16[192,512]{1,0:T(8,128)(2,1)S(1)} %add_send.6), channel_id=1, source_target_pairs={{0,8},{8,16},{16,24},{24,28},{28,20},{20,12},{12,4},{4,0},{1,9},{9... | collective-permute-start | bytes 589832 | tf_op jit(solution)/shard_map/ppermute | solution.py:508
  10.8 10.3 %collective-permute-start.23 = (bf16[192,640]{1,0:T(8,128)(2,1)S(1)}, bf16[192,640]{1,0:T(8,128)(2,1)S(1)}, u32[]{:S(2)}, u32[]{:S(2)}) collective-permute-start(bf16[192,640]{1,0:T(8,128)(2,1)S(1)} %pack_roots.1.refs_0_), channel_id=1, source_target_pairs={{8,0},{16,8},{24,16},{28,24},{20,28},{12,20},{4,12},{0,4},{9,1},{1... | collective-permute-start | bytes 737288 | tf_op jit(solution)/shard_map/ppermute | solution.py:511
  12.6 10.2 %collective-permute-start.22 = (bf16[192,640]{1,0:T(8,128)(2,1)S(1)}, bf16[192,640]{1,0:T(8,128)(2,1)S(1)}, u32[]{:S(2)}, u32[]{:S(2)}) collective-permute-start(bf16[192,640]{1,0:T(8,128)(2,1)S(1)} %pack_roots.1.refs_0_), channel_id=1, source_target_pairs={{0,8},{8,16},{16,24},{24,28},{28,20},{20,12},{12,4},{4,0},{1,9},{9... | collective-permute-start | bytes 737288 | tf_op jit(solution)/shard_map/ppermute | solution.py:508
  15.9 9.4 %collective-permute-start.6 = (bf16[192,512]{1,0:T(8,128)(2,1)S(1)}, bf16[192,512]{1,0:T(8,128)(2,1)S(1)}, u32[]{:S(2)}, u32[]{:S(2)}) collective-permute-start(bf16[192,512]{1,0:T(8,128)(2,1)S(1)} %add_send.10), channel_id=1, source_target_pairs={{8,0},{16,8},{24,16},{28,24},{20,28},{12,20},{4,12},{0,4},{9,1},{1... | collective-permute-start | bytes 589832 | tf_op jit(solution)/shard_map/ppermute | solution.py:511
  17.7 9.4 %collective-permute-start.2 = (bf16[192,512]{1,0:T(8,128)(2,1)S(1)}, bf16[192,512]{1,0:T(8,128)(2,1)S(1)}, u32[]{:S(2)}, u32[]{:S(2)}) collective-permute-start(bf16[192,512]{1,0:T(8,128)(2,1)S(1)} %add_send.7), channel_id=1, source_target_pairs={{0,8},{8,16},{16,24},{24,28},{28,20},{20,12},{12,4},{4,0},{1,9},{9... | collective-permute-start | bytes 589832 | tf_op jit(solution)/shard_map/ppermute | solution.py:508
  21.1 9.5 %collective-permute-start.25 = (bf16[192,640]{1,0:T(8,128)(2,1)S(1)}, bf16[192,640]{1,0:T(8,128)(2,1)S(1)}, u32[]{:S(2)}, u32[]{:S(2)}) collective-permute-start(bf16[192,640]{1,0:T(8,128)(2,1)S(1)} %collective-permute-done.23.refs_2_), channel_id=1, source_target_pairs={{8,0},{16,8},{24,16},{28,24},{20,28},{12,20},{4,12},{0,4},{9,1},{1... | collective-permute-start | bytes 737288 | tf_op jit(solution)/shard_map/ppermute | solution.py:511
  22.8 9.5 %collective-permute-start.24 = (bf16[192,640]{1,0:T(8,128)(2,1)S(1)}, bf16[192,640]{1,0:T(8,128)(2,1)S(1)}, u32[]{:S(2)}, u32[]{:S(2)}) collective-permute-start(bf16[192,640]{1,0:T(8,128)(2,1)S(1)} %collective-permute-done.22.refs_1_), channel_id=1, source_target_pairs={{0,8},{8,16},{16,24},{24,28},{28,20},{20,12},{12,4},{4,0},{1,9},{9... | collective-permute-start | bytes 737288 | tf_op jit(solution)/shard_map/ppermute | solution.py:508
  25.4 9.4 %collective-permute-start.7 = (bf16[192,512]{1,0:T(8,128)(2,1)S(1)}, bf16[192,512]{1,0:T(8,128)(2,1)S(1)}, u32[]{:S(2)}, u32[]{:S(2)}) collective-permute-start(bf16[192,512]{1,0:T(8,128)(2,1)S(1)} %add_send.11), channel_id=1, source_target_pairs={{8,0},{16,8},{24,16},{28,24},{20,28},{12,20},{4,12},{0,4},{9,1},{1... | collective-permute-start | bytes 589832 | tf_op jit(solution)/shard_map/ppermute | solution.py:511
  27.2 9.3 %collective-permute-start.3 = (bf16[192,512]{1,0:T(8,128)(2,1)S(1)}, bf16[192,512]{1,0:T(8,128)(2,1)S(1)}, u32[]{:S(2)}, u32[]{:S(2)}) collective-permute-start(bf16[192,512]{1,0:T(8,128)(2,1)S(1)} %add_send.8), channel_id=1, source_target_pairs={{0,8},{8,16},{16,24},{24,28},{28,20},{20,12},{12,4},{4,0},{1,9},{9... | collective-permute-start | bytes 589832 | tf_op jit(solution)/shard_map/ppermute | solution.py:508
  30.6 8.8 %collective-permute-start.27 = (bf16[192,640]{1,0:T(8,128)(2,1)S(1)}, bf16[192,640]{1,0:T(8,128)(2,1)S(1)}, u32[]{:S(2)}, u32[]{:S(2)}) collective-permute-start(bf16[192,640]{1,0:T(8,128)(2,1)S(1)} %collective-permute-done.25.refs_4_), channel_id=1, source_target_pairs={{8,0},{16,8},{24,16},{28,24},{20,28},{12,20},{4,12},{0,4},{9,1},{1... | collective-permute-start | bytes 737288 | tf_op jit(solution)/shard_map/ppermute | solution.py:511
  32.3 11.5 %collective-permute-start.26 = (bf16[192,640]{1,0:T(8,128)(2,1)S(1)}, bf16[192,640]{1,0:T(8,128)(2,1)S(1)}, u32[]{:S(2)}, u32[]{:S(2)}) collective-permute-start(bf16[192,640]{1,0:T(8,128)(2,1)S(1)} %collective-permute-done.24.refs_3_), channel_id=1, source_target_pairs={{0,8},{8,16},{16,24},{24,28},{28,20},{20,12},{12,4},{4,0},{1,9},{9... | collective-permute-start | bytes 737288 | tf_op jit(solution)/shard_map/ppermute | solution.py:508
  36.6 5.0 %collective-permute-start.12 = (bf16[96,512]{1,0:T(8,128)(2,1)S(1)}, bf16[96,512]{1,0:T(8,128)(2,1)S(1)}, u32[]{:S(2)}, u32[]{:S(2)}) collective-permute-start(bf16[96,512]{1,0:T(8,128)(2,1)S(1)} %get-tuple-element.17), channel_id=1, source_target_pairs={{8,0},{16,8},{24,16},{28,24},{20,28},{12,20},{4,12},{0,4},{9,1},{1... | collective-permute-start | bytes 294920 | tf_op jit(solution)/shard_map/ppermute | solution.py:511
  38.3 5.5 %collective-permute-start.8 = (bf16[96,512]{1,0:T(8,128)(2,1)S(1)}, bf16[96,512]{1,0:T(8,128)(2,1)S(1)}, u32[]{:S(2)}, u32[]{:S(2)}) collective-permute-start(bf16[96,512]{1,0:T(8,128)(2,1)S(1)} %get-tuple-element.18), channel_id=1, source_target_pairs={{0,8},{8,16},{16,24},{24,28},{28,20},{20,12},{12,4},{4,0},{1,9},{9... | collective-permute-start | bytes 294920 | tf_op jit(solution)/shard_map/ppermute | solution.py:508
  38.7 7.2 %collective-permute-start.17 = (bf16[96,512]{1,0:T(8,128)(2,1)S(1)}, bf16[96,512]{1,0:T(8,128)(2,1)S(1)}, u32[]{:S(2)}, u32[]{:S(2)}) collective-permute-start(bf16[96,512]{1,0:T(8,128)(2,1)S(1)} %get-tuple-element.17), channel_id=1, source_target_pairs={{0,8},{8,16},{16,24},{24,28},{28,20},{20,12},{12,4},{4,0},{1,9},{9... | collective-permute-start | bytes 294920 | tf_op jit(solution)/shard_map/ppermute | solution.py:508
  39.4 6.5 %collective-permute-start.16 = (bf16[96,512]{1,0:T(8,128)(2,1)S(1)}, bf16[96,512]{1,0:T(8,128)(2,1)S(1)}, u32[]{:S(2)}, u32[]{:S(2)}) collective-permute-start(bf16[96,512]{1,0:T(8,128)(2,1)S(1)} %get-tuple-element.18), channel_id=1, source_target_pairs={{8,0},{16,8},{24,16},{28,24},{20,28},{12,20},{4,12},{0,4},{9,1},{1... | collective-permute-start | bytes 294920 | tf_op jit(solution)/shard_map/ppermute | solution.py:511
  41.6 6.3 %collective-permute-start.13 = (bf16[96,512]{1,0:T(8,128)(2,1)S(1)}, bf16[96,512]{1,0:T(8,128)(2,1)S(1)}, u32[]{:S(2)}, u32[]{:S(2)}) collective-permute-start(bf16[96,512]{1,0:T(8,128)(2,1)S(1)} %collective-permute-done.12.refs_4_), channel_id=1, source_target_pairs={{8,0},{16,8},{24,16},{28,24},{20,28},{12,20},{4,12},{0,4},{9,1},{1... | collective-permute-start | bytes 294920 | tf_op jit(solution)/shard_map/ppermute | solution.py:511
  43.8 5.7 %collective-permute-start.9 = (bf16[96,512]{1,0:T(8,128)(2,1)S(1)}, bf16[96,512]{1,0:T(8,128)(2,1)S(1)}, u32[]{:S(2)}, u32[]{:S(2)}) collective-permute-start(bf16[96,512]{1,0:T(8,128)(2,1)S(1)} %collective-permute-done.8.refs_1_), channel_id=1, source_target_pairs={{0,8},{8,16},{16,24},{24,28},{28,20},{20,12},{12,4},{4,0},{1,9},{9... | collective-permute-start | bytes 294920 | tf_op jit(solution)/shard_map/ppermute | solution.py:508
  43.8 6.2 %collective-permute-start.29 = (bf16[96,640]{1,0:T(8,128)(2,1)S(1)}, bf16[96,640]{1,0:T(8,128)(2,1)S(1)}, u32[]{:S(2)}, u32[]{:S(2)}) collective-permute-start(bf16[96,640]{1,0:T(8,128)(2,1)S(1)} %slice.19), channel_id=1, source_target_pairs={{8,0},{16,8},{24,16},{28,24},{20,28},{12,20},{4,12},{0,4},{9,1},{1... | collective-permute-start | bytes 368648 | tf_op jit(solution)/shard_map/ppermute | solution.py:511
  45.9 5.7 %collective-permute-start.19 = (bf16[96,512]{1,0:T(8,128)(2,1)S(1)}, bf16[96,512]{1,0:T(8,128)(2,1)S(1)}, u32[]{:S(2)}, u32[]{:S(2)}) collective-permute-start(bf16[96,512]{1,0:T(8,128)(2,1)S(1)} %collective-permute-done.17.refs_3_), channel_id=1, source_target_pairs={{0,8},{8,16},{16,24},{24,28},{28,20},{20,12},{12,4},{4,0},{1,9},{9... | collective-permute-start | bytes 294920 | tf_op jit(solution)/shard_map/ppermute | solution.py:508
  45.9 6.7 %collective-permute-start.18 = (bf16[96,512]{1,0:T(8,128)(2,1)S(1)}, bf16[96,512]{1,0:T(8,128)(2,1)S(1)}, u32[]{:S(2)}, u32[]{:S(2)}) collective-permute-start(bf16[96,512]{1,0:T(8,128)(2,1)S(1)} %collective-permute-done.16.refs_2_), channel_id=1, source_target_pairs={{8,0},{16,8},{24,16},{28,24},{20,28},{12,20},{4,12},{0,4},{9,1},{1... | collective-permute-start | bytes 294920 | tf_op jit(solution)/shard_map/ppermute | solution.py:511
  47.9 5.7 %collective-permute-start.14 = (bf16[96,512]{1,0:T(8,128)(2,1)S(1)}, bf16[96,512]{1,0:T(8,128)(2,1)S(1)}, u32[]{:S(2)}, u32[]{:S(2)}) collective-permute-start(bf16[96,512]{1,0:T(8,128)(2,1)S(1)} %collective-permute-done.13.refs_8_), channel_id=1, source_target_pairs={{8,0},{16,8},{24,16},{28,24},{20,28},{12,20},{4,12},{0,4},{9,1},{1... | collective-permute-start | bytes 294920 | tf_op jit(solution)/shard_map/ppermute | solution.py:511
  49.5 5.7 %collective-permute-start.10 = (bf16[96,512]{1,0:T(8,128)(2,1)S(1)}, bf16[96,512]{1,0:T(8,128)(2,1)S(1)}, u32[]{:S(2)}, u32[]{:S(2)}) collective-permute-start(bf16[96,512]{1,0:T(8,128)(2,1)S(1)} %collective-permute-done.9.refs_5_), channel_id=1, source_target_pairs={{0,8},{8,16},{16,24},{24,28},{28,20},{20,12},{12,4},{4,0},{1,9},{9... | collective-permute-start | bytes 294920 | tf_op jit(solution)/shard_map/ppermute | solution.py:508
  50.0 5.9 %collective-permute-start.28 = (bf16[96,640]{1,0:T(8,128)(2,1)S(1)}, bf16[96,640]{1,0:T(8,128)(2,1)S(1)}, u32[]{:S(2)}, u32[]{:S(2)}) collective-permute-start(bf16[96,640]{1,0:T(8,128)(2,1)S(1)} %slice.18), channel_id=1, source_target_pairs={{0,8},{8,16},{16,24},{24,28},{28,20},{20,12},{12,4},{4,0},{1,9},{9... | collective-permute-start | bytes 368648 | tf_op jit(solution)/shard_map/ppermute | solution.py:508
  51.6 6.7 %collective-permute-start.21 = (bf16[96,512]{1,0:T(8,128)(2,1)S(1)}, bf16[96,512]{1,0:T(8,128)(2,1)S(1)}, u32[]{:S(2)}, u32[]{:S(2)}) collective-permute-start(bf16[96,512]{1,0:T(8,128)(2,1)S(1)} %collective-permute-done.19.refs_7_), channel_id=1, source_target_pairs={{0,8},{8,16},{16,24},{24,28},{28,20},{20,12},{12,4},{4,0},{1,9},{9... | collective-permute-start | bytes 294920 | tf_op jit(solution)/shard_map/ppermute | solution.py:508
  52.6 5.6 %collective-permute-start.20 = (bf16[96,512]{1,0:T(8,128)(2,1)S(1)}, bf16[96,512]{1,0:T(8,128)(2,1)S(1)}, u32[]{:S(2)}, u32[]{:S(2)}) collective-permute-start(bf16[96,512]{1,0:T(8,128)(2,1)S(1)} %collective-permute-done.18.refs_6_), channel_id=1, source_target_pairs={{8,0},{16,8},{24,16},{28,24},{20,28},{12,20},{4,12},{0,4},{9,1},{1... | collective-permute-start | bytes 294920 | tf_op jit(solution)/shard_map/ppermute | solution.py:511
  53.6 7.3 %collective-permute-start.15 = (bf16[96,512]{1,0:T(8,128)(2,1)S(1)}, bf16[96,512]{1,0:T(8,128)(2,1)S(1)}, u32[]{:S(2)}, u32[]{:S(2)}) collective-permute-start(bf16[96,512]{1,0:T(8,128)(2,1)S(1)} %collective-permute-done.14.refs_12_), channel_id=1, source_target_pairs={{8,0},{16,8},{24,16},{28,24},{20,28},{12,20},{4,12},{0,4},{9,1},{1... | collective-permute-start | bytes 294920 | tf_op jit(solution)/shard_map/ppermute | solution.py:511
  55.2 5.7 %collective-permute-start.11 = (bf16[96,512]{1,0:T(8,128)(2,1)S(1)}, bf16[96,512]{1,0:T(8,128)(2,1)S(1)}, u32[]{:S(2)}, u32[]{:S(2)}) collective-permute-start(bf16[96,512]{1,0:T(8,128)(2,1)S(1)} %collective-permute-done.10.refs_9_), channel_id=1, source_target_pairs={{0,8},{8,16},{16,24},{24,28},{28,20},{20,12},{12,4},{4,0},{1,9},{9... | collective-permute-start | bytes 294920 | tf_op jit(solution)/shard_map/ppermute | solution.py:508
  58.3 2.6 %copy-start.2 = (f32[192,512]{1,0:T(8,128)S(1)}, f32[192,512]{1,0:T(8,128)}, u32[]{:S(2)}) copy-start(f32[192,512]{1,0:T(8,128)} %refs_7_.1) | copy-start | bytes 1179652
  58.3 2.6 %copy-start.3 = (f32[192,512]{1,0:T(8,128)S(1)}, f32[192,512]{1,0:T(8,128)}, u32[]{:S(2)}) copy-start(f32[192,512]{1,0:T(8,128)} %refs_8_.1) | copy-start | bytes 1179652

commit v4 on v3

--- a/solution.py
+++ b/solution.py
@@ -110,20 +110,26 @@
 PAIR = 2 * TILE
 
 
-def kept(breadth):
-    return breadth // 2 + TILE
-
-
-def pairs_of(tile, breadth):
-    pairs = breadth // PAIR
-    odd = tile & 1
-    whole_pair = (tile + odd) >> 1
-    half_pair = whole_pair + pairs // 2 + (pairs // 2 - 1) * odd
-    return whole_pair, half_pair, odd == 0
+def meets(tile, tiles):
+    half, quarter = tiles // 2, tiles // 4
+    return ((tile < half) & (tile != quarter)) | (tile == half + quarter)
+
+
+def slots_of(n, band, tiles):
+    rows = band // TILE
+    return max(sum(meets((k * rows + t) % tiles, tiles) for t in range(rows)) for k in range(n))
 
 
 def lanes(pair, breadth):
     return pl.ds(pl.multiple_of((pair & (breadth // PAIR - 1)) * PAIR, PAIR), PAIR)
+
+
+def lower_half(rows):
+    return lax.broadcasted_iota(jnp.int32, (rows, PAIR), 1) < TILE
+
+
+def swapped(x):
+    return pltpu.roll(x, TILE, 1)
 
 
 def first_sends(me, partial, n):
@@ -155,37 +161,100 @@
 def pack_roots(me, owner, left_root, right_root, n):
     band, breadth = left_root.shape
     tiles = breadth // TILE
-    whole_pairs = tiles // 4
-    width = kept(breadth)
+    quarter = tiles // 4
+    more = slots_of(n, band, tiles) * TILE * PAIR // breadth
 
     def kernel(me_ref, owner_ref, l_ref, r_ref, out_ref):
         number = band_of(owner_ref, me_ref[0], n)
-        low = lax.broadcasted_iota(jnp.int32, (TILE, PAIR), 1) < TILE
+        low = lower_half(TILE)
+        out_ref[band:] = jnp.zeros((more, breadth), BF16)
+        slot = jnp.int32(0)
         for row in range(0, band, TILE):
             tile = (number * (band // TILE) + row // TILE) & (tiles - 1)
-            first, half_pair, even = pairs_of(tile, breadth)
+            odd, pair = tile & 1, tile >> 1
             rows = slice(row, row + TILE)
-            for i in range(whole_pairs):
-                pair = lanes(first + i, breadth)
-                out_ref[rows, i * PAIR : (i + 1) * PAIR] = l_ref[rows, pair]
-                out_ref[rows, (whole_pairs + i) * PAIR : (whole_pairs + i + 1) * PAIR] = r_ref[rows, pair]
-            left = l_ref[rows, lanes(half_pair, breadth)].astype(F32)
-            right = pltpu.roll(r_ref[rows, lanes(half_pair, breadth)].astype(F32), TILE, 1)
-            mine = jnp.where(low == even, left, right)
-            out_ref[rows, 2 * whole_pairs * PAIR :] = mine.astype(BF16)
+            last = lanes(pair + quarter, breadth)
+            for at, ref in ((0, l_ref), (quarter, r_ref)):
+                start = ref[rows, lanes(pair, breadth)].astype(F32)
+                end = ref[rows, last].astype(F32)
+                mixed = jnp.where(low & (odd == 1), end, start).astype(BF16)
+                out_ref[rows, at * PAIR : (at + 1) * PAIR] = mixed
+                for i in range(1, quarter):
+                    out_ref[rows, (at + i) * PAIR : (at + i + 1) * PAIR] = ref[rows, lanes(pair + i, breadth)]
+            here = meets(tile, tiles)
+
+            @pl.when(here)
+            def _():
+                left, right = l_ref[rows, last].astype(F32), r_ref[rows, last].astype(F32)
+                left = jnp.where(odd == 1, swapped(left), left)
+                right = jnp.where(odd == 1, right, swapped(right))
+                both = jnp.where(low, left, right).astype(BF16)
+                for i in range(TILE // more):
+                    place = lanes(slot * (TILE // more) + i, breadth)
+                    out_ref[band : band + more, place] = both[i * more : (i + 1) * more]
+
+            slot = slot + here.astype(jnp.int32)
 
     return pl.pallas_call(
         kernel,
-        out_shape=jax.ShapeDtypeStruct((band, 2 * width), BF16),
+        out_shape=jax.ShapeDtypeStruct((band + more, breadth), BF16),
         grid_spec=pltpu.PrefetchScalarGridSpec(
             num_scalar_prefetch=2,
             grid=(1,),
             in_specs=[whole(band, breadth), whole(band, breadth)],
-            out_specs=whole(band, 2 * width),
+            out_specs=whole(band + more, breadth),
         ),
         compiler_params=params(),
         name="pack_roots",
     )(me, owner, left_root, right_root)
+
+
+def place_packed(pieces, refs, numbers, half_l, half_r, band, breadth):
+    tiles = breadth // TILE
+    quarter = tiles // 4
+    low = lower_half(TILE)
+    zeros = jnp.zeros((TILE, PAIR), BF16)
+    for offset, number in numbers.items():
+        parts = [(first, ref) for (place, first, _), ref in zip(pieces, refs) if place == offset]
+        more = max(first + ref.shape[0] for first, ref in parts) - band
+
+        def rows_at(row, end, pairs):
+            found = []
+            for first, ref in parts:
+                top, bottom = max(row, first), min(end, first + ref.shape[0])
+                if top < bottom:
+                    found.append(ref[top - first : bottom - first, pairs].astype(F32))
+            return jnp.concatenate(found, 0) if len(found) > 1 else found[0]
+
+        slot = jnp.int32(0)
+        for row in range(0, band, TILE):
+            tile = (number * (band // TILE) + row // TILE) & (tiles - 1)
+            odd, pair = tile & 1, tile >> 1
+            at = pl.ds(pl.multiple_of(number * band + row, TILE), TILE)
+            here = meets(tile, tiles)
+            both = jnp.concatenate(
+                [
+                    rows_at(band, band + more, lanes(slot * (TILE // more) + i, breadth))
+                    for i in range(TILE // more)
+                ],
+                0,
+            )
+            slot = slot + here.astype(jnp.int32)
+            other = swapped(both)
+            late = low & (odd == 1)
+            mine = (low == (odd == 0)) & here
+            for start, half, value in (
+                (0, half_l, jnp.where(odd == 1, other, both)),
+                (quarter, half_r, jnp.where(odd == 1, both, other)),
+            ):
+                mixed = rows_at(row, row + TILE, slice(start * PAIR, (start + 1) * PAIR))
+                half[at, lanes(pair, breadth)] = jnp.where(late, 0.0, mixed).astype(BF16)
+                end = jnp.where(mine, value, jnp.where(late, mixed, 0.0))
+                half[at, lanes(pair + quarter, breadth)] = end.astype(BF16)
+                for i in range(1, quarter):
+                    some = rows_at(row, row + TILE, slice((start + i) * PAIR, (start + i + 1) * PAIR))
+                    half[at, lanes(pair + i, breadth)] = some.astype(BF16)
+                    half[at, lanes(pair + quarter + i, breadth)] = zeros
 
 
 def add_send(me, partial, arrived, distance, n, first, *after):
@@ -249,48 +318,20 @@
 def unpack_roots(me, owner, pieces, stacked, breadth, n):
     band = stacked // n
     tiles = breadth // TILE
-    whole_pairs = tiles // 4
     nblocks = stacked // breadth
 
     def kernel(me_ref, owner_ref, *refs):
         refs, (left_ref, right_ref, half_l, half_r, table, sem) = refs[: len(pieces)], refs[len(pieces) :]
         copy = pltpu.make_async_copy(owner_ref, table, sem)
         copy.start()
-        lower = lax.broadcasted_iota(jnp.int32, (TILE, PAIR), 1) < TILE
-        nothing = jnp.zeros((TILE, PAIR), BF16)
         shift = TILE.bit_length() - 1
         down = lax.broadcasted_iota(jnp.int32, (breadth, breadth), 0) >> shift
         over = lax.broadcasted_iota(jnp.int32, (breadth, breadth), 1) >> shift
         apart = over - down + jnp.where(over < down, tiles, 0)
-        mirrored = (apart > 0) & (apart < tiles // 2)
+        mirrored = (apart > 0) & (apart <= tiles // 2)
         copy.wait()
-        numbers = {o: band_of(table, away(me_ref[0], o, n), n) for o in {p[0] for p in pieces}}
-        for (offset, first, _), ref in zip(pieces, refs):
-            number = numbers[offset]
-            edges = sorted({first, first + ref.shape[0], *range(0, band + 1, TILE)})
-            edges = [x for x in edges if first <= x <= first + ref.shape[0]]
-            for row, end in zip(edges[:-1], edges[1:]):
-                tile = (number * (band // TILE) + row // TILE) & (tiles - 1)
-                start, half_pair, even = pairs_of(tile, breadth)
-                at = pl.ds(pl.multiple_of(number * band + row, CHUNK), end - row)
-                rows = slice(row - first, end - first)
-                low = lower[: end - row]
-                zeros = nothing[: end - row]
-                shared = ref[rows, 2 * whole_pairs * PAIR :].astype(F32)
-                left = jnp.where(low == even, shared, 0.0).astype(BF16)
-                right = jnp.where(low == even, pltpu.roll(shared, TILE, 1), 0.0).astype(BF16)
-                for i in range(2 * whole_pairs):
-                    pair = lanes(start + i, breadth)
-                    if i < whole_pairs:
-                        half_l[at, pair] = ref[rows, i * PAIR : (i + 1) * PAIR]
-                        half_r[at, pair] = ref[
-                            rows, (whole_pairs + i) * PAIR : (whole_pairs + i + 1) * PAIR
-                        ]
-                    else:
-                        half_l[at, pair] = zeros
-                        half_r[at, pair] = zeros
-                half_l[at, lanes(half_pair, breadth)] = left
-                half_r[at, lanes(half_pair, breadth)] = right
+        numbers = {o: band_of(table, away(me_ref[0], o, n), n) for o in sorted({p[0] for p in pieces})}
+        place_packed(pieces, refs, numbers, half_l, half_r, band, breadth)
         for half, out in ((half_r, right_ref), (half_l, left_ref)):
             for b in range(nblocks):
                 rows = slice(b * breadth, (b + 1) * breadth)
@@ -524,11 +565,11 @@
             ways = [upper, upper, lower, lower]
             for hop in range(1, n // 2):
                 ways = [
+                    send_left(ways[3]),
+                    send_right(ways[2]),
+                    send_left(ways[1]),
                     send_right(ways[0]),
-                    send_left(ways[1]),
-                    send_right(ways[2]),
-                    send_left(ways[3]),
-                ]
+                ][::-1]
                 pieces += [(-hop, 0, ways[0]), (hop, 0, ways[1])]
                 pieces += [(-hop, rows, ways[2]), (hop, rows, ways[3])]
             right, left = send_right(ways[0]), send_left(ways[3])
@@ -553,6 +594,9 @@
     stacked, breadth = partial_grads.shape[1:]
     band = stacked // n
     fits = band % TILE == 0 and breadth % (4 * TILE) == 0 and breadth & (breadth - 1) == 0
+    if fits:
+        more = slots_of(n, band, breadth // TILE) * TILE * PAIR // breadth
+        fits = more > 0 and TILE % more == 0 and (band + more) % 32 == 0
     if 4 <= n <= 16 and n % 2 == 0 and fits:
         return ring(n, partial_grads, *rest)
     return general(partial_grads, *rest)

time: 63.4 us -> 62.7 us (0.989)
  starting transfers between devices: 33.3 us -> 32.1 us
    ppermute x15, starting transfers between devices: 6.32 us -> 4.96 us  [send_right(): return lax.ppermute(x, 'dp', onward)]
    ppermute x15, waiting for transfers between devices: 2.66 us -> 3.73 us  [send_right(): return lax.ppermute(x, 'dp', onward)]
  transfers between devices with their start and end apart: 30 -> 30, of which waited for: 12 -> 14; matrix products, arithmetic and copies ran while one was open for 0% -> 0% of each run, Pallas kernels for 10% -> 10%
where the time goes in v4:
time: 62.7 us; the launch traced here: 62.6 us
  starting transfers between devices  32.1 us (51%)
  waiting for transfers between devices  19.9 us (32%)
  Pallas kernels  8.34 us (13%)
  local copies, waits for them, and re-layouts  1.47 us (2%)
  between operations  0.84 us (1%)
    ppermute x15, starting transfers between devices, send_left(): return lax.ppermute(x, 'dp', backward)  27.1 us
    ppermute x15, waiting for transfers between devices, send_left(): return lax.ppermute(x, 'dp', backward)  16.1 us
    ppermute x15, starting transfers between devices, send_right(): return lax.ppermute(x, 'dp', onward)  4.96 us
    ppermute x15, waiting for transfers between devices, send_right(): return lax.ppermute(x, 'dp', onward)  3.73 us
    pallas_call x1, Pallas kernels, begin(): pl.pallas_call(kernel, out_shape=(jax.ShapeDtypeStruct((stacked, breadth)...  2.6 us
    pallas_call x1, Pallas kernels, unpack_roots(): pl.pallas_call(kernel, out_shape=(out, out), grid_spec=pltpu.PrefetchScal...  2.42 us
    pallas_call x1, Pallas kernels, finish(): pl.pallas_call(kernel, out_shape=(jax.ShapeDtypeStruct((stacked, breadth)...  2.25 us
    unnamed x14, local copies, waits for them, and re-layouts  1.43 us
  transfers between devices with their start and end apart: 30, of which 14 were waited for; matrix products, arithmetic and copies ran while one was open for 0% of the time, Pallas kernels for 10%

profile of v4, /device:TPU:0, one launch (start us, length us, event | category | flops | bytes accessed | tf_op | source)
XLA Modules:
  0.0 62.6 jit_solution(15229263697789342935)
XLA Ops:
  0.6 1.4 %copy-done = bf16[1,1536,512]{2,1,0:T(8,128)(2,1)S(1)} copy-done((bf16[1,1536,512]{2,1,0:T(8,128)(2,1)S(1)}, bf16[1,1536,512]{2,1,0:T(8,128)(2,1)}, u32[]{:S(2)}) %copy-start) | copy-done | bytes 1572888
  2.1 3.0 %collective-permute-start.4 = (bf16[96,512]{1,0:T(8,128)(2,1)S(1)}, bf16[96,512]{1,0:T(8,128)(2,1)S(1)}, u32[]{:S(2)}, u32[]{:S(2)}) collective-permute-start(bf16[96,512]{1,0:T(8,128)(2,1)S(1)} %get-tuple-element.11), channel_id=1, source_target_pairs={{8,0},{16,8},{24,16},{28,24},{20,28},{12,20},{4,12},{0,4},{9,1},{1... | collective-permute-start | bytes 294920 | tf_op jit(solution)/shard_map/ppermute | solution.py:552
  5.1 0.2 collective-permute-start
  5.2 2.7 %collective-permute-done.4.a_ref = bf16[96,512]{1,0:T(8,128)(2,1)S(1)} collective-permute-done((bf16[96,512]{1,0:T(8,128)(2,1)S(1)}, bf16[96,512]{1,0:T(8,128)(2,1)S(1)}, u32[]{:S(2)}, u32[]{:S(2)}) %collective-permute-start.4) | collective-permute-done | bytes 98336 | tf_op jit(solution)/shard_map/ppermute | solution.py:552
  8.0 1.8 %collective-permute-start.5 = (bf16[192,512]{1,0:T(8,128)(2,1)S(1)}, bf16[192,512]{1,0:T(8,128)(2,1)S(1)}, u32[]{:S(2)}, u32[]{:S(2)}) collective-permute-start(bf16[192,512]{1,0:T(8,128)(2,1)S(1)} %add_send.9), channel_id=1, source_target_pairs={{8,0},{16,8},{24,16},{28,24},{20,28},{12,20},{4,12},{0,4},{9,1},{1... | collective-permute-start | bytes 589832 | tf_op jit(solution)/shard_map/ppermute | solution.py:552
  9.8 0.3 collective-permute-start.1
  10.2 0.7 %pack_roots.1.refs_0_ = bf16[224,512]{1,0:T(8,128)(2,1)S(1)} custom-call(s32[1]{0:T(128)} %bitcast.me_ref, s32[8]{0:T(128)S(1)} %copy-done.6, bf16[192,512]{1,0:T(8,128)(2,1)S(1)} %copy-done.4, bf16[192,512]{1,0:T(8,128)(2,1)S(1)} %copy-done.5), custom_call_target="tpu_custom_call" | custom-call | tf_op jit(solution)/shard_map/pack_roots/pallas_call | solution.py:198
  10.9 1.9 %collective-permute-start.23 = (bf16[224,512]{1,0:T(8,128)(2,1)S(1)}, bf16[224,512]{1,0:T(8,128)(2,1)S(1)}, u32[]{:S(2)}, u32[]{:S(2)}) collective-permute-start(bf16[224,512]{1,0:T(8,128)(2,1)S(1)} %pack_roots.1.refs_0_), channel_id=1, source_target_pairs={{8,0},{16,8},{24,16},{28,24},{20,28},{12,20},{4,12},{0,4},{9,1},{1... | collective-permute-start | bytes 688136 | tf_op jit(solution)/shard_map/ppermute | solution.py:552
  12.7 0.2 collective-permute-start.22
  12.9 2.9 %collective-permute-done.5.a_ref = bf16[192,512]{1,0:T(8,128)(2,1)S(1)} collective-permute-done((bf16[192,512]{1,0:T(8,128)(2,1)S(1)}, bf16[192,512]{1,0:T(8,128)(2,1)S(1)}, u32[]{:S(2)}, u32[]{:S(2)}) %collective-permute-start.5) | collective-permute-done | bytes 196640 | tf_op jit(solution)/shard_map/ppermute | solution.py:552
  15.9 1.6 %collective-permute-start.6 = (bf16[192,512]{1,0:T(8,128)(2,1)S(1)}, bf16[192,512]{1,0:T(8,128)(2,1)S(1)}, u32[]{:S(2)}, u32[]{:S(2)}) collective-permute-start(bf16[192,512]{1,0:T(8,128)(2,1)S(1)} %add_send.10), channel_id=1, source_target_pairs={{8,0},{16,8},{24,16},{28,24},{20,28},{12,20},{4,12},{0,4},{9,1},{1... | collective-permute-start | bytes 589832 | tf_op jit(solution)/shard_map/ppermute | solution.py:552
  17.5 0.1 collective-permute-done.1.a_ref
  17.7 0.4 collective-permute-start.2
  18.1 2.7 %collective-permute-done.23.refs_2_ = bf16[224,512]{1,0:T(8,128)(2,1)S(1)} collective-permute-done((bf16[224,512]{1,0:T(8,128)(2,1)S(1)}, bf16[224,512]{1,0:T(8,128)(2,1)S(1)}, u32[]{:S(2)}, u32[]{:S(2)}) %collective-permute-start.23) | collective-permute-done | bytes 229408 | tf_op jit(solution)/shard_map/ppermute | solution.py:552
  20.8 1.6 %collective-permute-start.25 = (bf16[224,512]{1,0:T(8,128)(2,1)S(1)}, bf16[224,512]{1,0:T(8,128)(2,1)S(1)}, u32[]{:S(2)}, u32[]{:S(2)}) collective-permute-start(bf16[224,512]{1,0:T(8,128)(2,1)S(1)} %collective-permute-done.23.refs_2_), channel_id=1, source_target_pairs={{8,0},{16,8},{24,16},{28,24},{20,28},{12,20},{4,12},{0,4},{9,1},{1... | collective-permute-start | bytes 688136 | tf_op jit(solution)/shard_map/ppermute | solution.py:552
  22.3 0.2 collective-permute-done.22.refs_1_
  22.5 0.3 collective-permute-start.24
  22.9 2.1 %collective-permute-done.6.a_ref = bf16[192,512]{1,0:T(8,128)(2,1)S(1)} collective-permute-done((bf16[192,512]{1,0:T(8,128)(2,1)S(1)}, bf16[192,512]{1,0:T(8,128)(2,1)S(1)}, u32[]{:S(2)}, u32[]{:S(2)}) %collective-permute-start.6) | collective-permute-done | bytes 196640 | tf_op jit(solution)/shard_map/ppermute | solution.py:552
  25.1 1.6 %collective-permute-start.7 = (bf16[192,512]{1,0:T(8,128)(2,1)S(1)}, bf16[192,512]{1,0:T(8,128)(2,1)S(1)}, u32[]{:S(2)}, u32[]{:S(2)}) collective-permute-start(bf16[192,512]{1,0:T(8,128)(2,1)S(1)} %add_send.11), channel_id=1, source_target_pairs={{8,0},{16,8},{24,16},{28,24},{20,28},{12,20},{4,12},{0,4},{9,1},{1... | collective-permute-start | bytes 589832 | tf_op jit(solution)/shard_map/ppermute | solution.py:552
  26.7 0.1 collective-permute-done.2.a_ref
  26.8 0.4 collective-permute-start.3
  27.3 2.7 %collective-permute-done.25.refs_4_ = bf16[224,512]{1,0:T(8,128)(2,1)S(1)} collective-permute-done((bf16[224,512]{1,0:T(8,128)(2,1)S(1)}, bf16[224,512]{1,0:T(8,128)(2,1)S(1)}, u32[]{:S(2)}, u32[]{:S(2)}) %collective-permute-start.25) | collective-permute-done | bytes 229408 | tf_op jit(solution)/shard_map/ppermute | solution.py:552
  29.9 1.6 %collective-permute-start.27 = (bf16[224,512]{1,0:T(8,128)(2,1)S(1)}, bf16[224,512]{1,0:T(8,128)(2,1)S(1)}, u32[]{:S(2)}, u32[]{:S(2)}) collective-permute-start(bf16[224,512]{1,0:T(8,128)(2,1)S(1)} %collective-permute-done.25.refs_4_), channel_id=1, source_target_pairs={{8,0},{16,8},{24,16},{28,24},{20,28},{12,20},{4,12},{0,4},{9,1},{1... | collective-permute-start | bytes 688136 | tf_op jit(solution)/shard_map/ppermute | solution.py:552
  31.5 0.2 collective-permute-done.24.refs_3_
  31.7 0.3 collective-permute-start.26
  32.0 2.1 %collective-permute-done.7.l_ref = bf16[192,512]{1,0:T(8,128)(2,1)S(1)} collective-permute-done((bf16[192,512]{1,0:T(8,128)(2,1)S(1)}, bf16[192,512]{1,0:T(8,128)(2,1)S(1)}, u32[]{:S(2)}, u32[]{:S(2)}) %collective-permute-start.7) | collective-permute-done | bytes 196640 | tf_op jit(solution)/shard_map/ppermute | solution.py:552
  34.1 1.8 %collective-permute-done.3.r_ref = bf16[192,512]{1,0:T(8,128)(2,1)S(1)} collective-permute-done((bf16[192,512]{1,0:T(8,128)(2,1)S(1)}, bf16[192,512]{1,0:T(8,128)(2,1)S(1)}, u32[]{:S(2)}, u32[]{:S(2)}) %collective-permute-start.3) | collective-permute-done | bytes 196640 | tf_op jit(solution)/shard_map/ppermute | solution.py:549
  35.9 0.1 add_own.1.refs_0_
  36.0 1.6 %collective-permute-start.12 = (bf16[96,512]{1,0:T(8,128)(2,1)S(1)}, bf16[96,512]{1,0:T(8,128)(2,1)S(1)}, u32[]{:S(2)}, u32[]{:S(2)}) collective-permute-start(bf16[96,512]{1,0:T(8,128)(2,1)S(1)} %get-tuple-element.17), channel_id=1, source_target_pairs={{8,0},{16,8},{24,16},{28,24},{20,28},{12,20},{4,12},{0,4},{9,1},{1... | collective-permute-start | bytes 294920 | tf_op jit(solution)/shard_map/ppermute | solution.py:552
  37.6 0.4 collective-permute-start.8
  38.1 0.3 collective-permute-start.17
  38.4 1.7 %collective-permute-start.16 = (bf16[96,512]{1,0:T(8,128)(2,1)S(1)}, bf16[96,512]{1,0:T(8,128)(2,1)S(1)}, u32[]{:S(2)}, u32[]{:S(2)}) collective-permute-start(bf16[96,512]{1,0:T(8,128)(2,1)S(1)} %get-tuple-element.18), channel_id=1, source_target_pairs={{8,0},{16,8},{24,16},{28,24},{20,28},{12,20},{4,12},{0,4},{9,1},{1... | collective-permute-start | bytes 294920 | tf_op jit(solution)/shard_map/ppermute | solution.py:552
  40.1 0.9 %collective-permute-done.12.refs_4_ = bf16[96,512]{1,0:T(8,128)(2,1)S(1)} collective-permute-done((bf16[96,512]{1,0:T(8,128)(2,1)S(1)}, bf16[96,512]{1,0:T(8,128)(2,1)S(1)}, u32[]{:S(2)}, u32[]{:S(2)}) %collective-permute-start.12) | collective-permute-done | bytes 98336 | tf_op jit(solution)/shard_map/ppermute | solution.py:552
  41.0 2.1 %collective-permute-start.13 = (bf16[96,512]{1,0:T(8,128)(2,1)S(1)}, bf16[96,512]{1,0:T(8,128)(2,1)S(1)}, u32[]{:S(2)}, u32[]{:S(2)}) collective-permute-start(bf16[96,512]{1,0:T(8,128)(2,1)S(1)} %collective-permute-done.12.refs_4_), channel_id=1, source_target_pairs={{8,0},{16,8},{24,16},{28,24},{20,28},{12,20},{4,12},{0,4},{9,1},{1... | collective-permute-start | bytes 294920 | tf_op jit(solution)/shard_map/ppermute | solution.py:552
  43.1 0.2 collective-permute-done.8.refs_1_
  43.4 2.0 %collective-permute-start.29 = (bf16[112,512]{1,0:T(8,128)(2,1)S(1)}, bf16[112,512]{1,0:T(8,128)(2,1)S(1)}, u32[]{:S(2)}, u32[]{:S(2)}) collective-permute-start(bf16[112,512]{1,0:T(8,128)(2,1)S(1)} %slice.19), channel_id=1, source_target_pairs={{8,0},{16,8},{24,16},{28,24},{20,28},{12,20},{4,12},{0,4},{9,1},{1... | collective-permute-start | bytes 344072 | tf_op jit(solution)/shard_map/ppermute | solution.py:552
  45.5 2.0 %collective-permute-start.18 = (bf16[96,512]{1,0:T(8,128)(2,1)S(1)}, bf16[96,512]{1,0:T(8,128)(2,1)S(1)}, u32[]{:S(2)}, u32[]{:S(2)}) collective-permute-start(bf16[96,512]{1,0:T(8,128)(2,1)S(1)} %collective-permute-done.16.refs_2_), channel_id=1, source_target_pairs={{8,0},{16,8},{24,16},{28,24},{20,28},{12,20},{4,12},{0,4},{9,1},{1... | collective-permute-start | bytes 294920 | tf_op jit(solution)/shard_map/ppermute | solution.py:552
  47.4 1.6 %collective-permute-start.14 = (bf16[96,512]{1,0:T(8,128)(2,1)S(1)}, bf16[96,512]{1,0:T(8,128)(2,1)S(1)}, u32[]{:S(2)}, u32[]{:S(2)}) collective-permute-start(bf16[96,512]{1,0:T(8,128)(2,1)S(1)} %collective-permute-done.13.refs_8_), channel_id=1, source_target_pairs={{8,0},{16,8},{24,16},{28,24},{20,28},{12,20},{4,12},{0,4},{9,1},{1... | collective-permute-start | bytes 294920 | tf_op jit(solution)/shard_map/ppermute | solution.py:552
  49.0 0.5 collective-permute-start.10
  49.5 0.5 collective-permute-start.28
  50.0 1.1 %collective-permute-done.19.refs_7_ = bf16[96,512]{1,0:T(8,128)(2,1)S(1)} collective-permute-done((bf16[96,512]{1,0:T(8,128)(2,1)S(1)}, bf16[96,512]{1,0:T(8,128)(2,1)S(1)}, u32[]{:S(2)}, u32[]{:S(2)}) %collective-permute-start.19) | collective-permute-done | bytes 98336 | tf_op jit(solution)/shard_map/ppermute | solution.py:549
  51.1 0.4 collective-permute-start.21
  51.6 1.6 %collective-permute-start.20 = (bf16[96,512]{1,0:T(8,128)(2,1)S(1)}, bf16[96,512]{1,0:T(8,128)(2,1)S(1)}, u32[]{:S(2)}, u32[]{:S(2)}) collective-permute-start(bf16[96,512]{1,0:T(8,128)(2,1)S(1)} %collective-permute-done.18.refs_6_), channel_id=1, source_target_pairs={{8,0},{16,8},{24,16},{28,24},{20,28},{12,20},{4,12},{0,4},{9,1},{1... | collective-permute-start | bytes 294920 | tf_op jit(solution)/shard_map/ppermute | solution.py:552
  53.2 1.5 %collective-permute-start.15 = (bf16[96,512]{1,0:T(8,128)(2,1)S(1)}, bf16[96,512]{1,0:T(8,128)(2,1)S(1)}, u32[]{:S(2)}, u32[]{:S(2)}) collective-permute-start(bf16[96,512]{1,0:T(8,128)(2,1)S(1)} %collective-permute-done.14.refs_12_), channel_id=1, source_target_pairs={{8,0},{16,8},{24,16},{28,24},{20,28},{12,20},{4,12},{0,4},{9,1},{1... | collective-permute-start | bytes 294920 | tf_op jit(solution)/shard_map/ppermute | solution.py:552
  54.7 0.5 collective-permute-start.11
  55.2 2.4 %unpack_roots.1 = (bf16[1536,512]{1,0:T(8,128)(2,1)S(1)}, bf16[1536,512]{1,0:T(8,128)(2,1)S(1)}) custom-call(s32[1]{0:T(128)} %bitcast.me_ref, s32[8]{0:T(128)S(1)} %copy-done.6, bf16[224,512]{1,0:T(8,128)(2,1)S(1)} %pack_roots.1.refs_0_, bf16[224,512]{1,0:T(8,128)(2,1)S(1)} %collective-permute-done.22.refs_1_, ...), custom_call_target="tpu_custom_call" | custom-call | tf_op jit(solution)/shard_map/unpack_roots/pallas_call | solution.py:342
  57.7 2.6 %begin.1 = (bf16[1536,512]{1,0:T(8,128)(2,1)S(1)}, bf16[1536,512]{1,0:T(8,128)(2,1)S(1)}, f32[2,512,512]{2,1,0:T(8,128)S(1)}) custom-call(s32[1]{0:T(128)} %bitcast.me_ref, bf16[192,512]{1,0:T(8,128)(2,1)S(1)} %add_own.1.refs_0_, bf16[96,512]{1,0:T(8,128)(2,1)S(1)} %collective-permute-done.8.refs_1_, bf16[96,512]{1,0:T(8,128)(2,1)S(1)} %collective-permute-done.16.refs_2_, ...), custom_call_target="tpu_custom_call" | custom-call | tf_op jit(solution)/shard_map/begin/pallas_call | solution.py:382
  60.3 2.3 %finish.1 = (bf16[1536,512]{1,0:T(8,128)(2,1)}, f32[192,512]{1,0:T(8,128)}, f32[192,512]{1,0:T(8,128)}) custom-call(s32[1]{0:T(128)} %bitcast.me_ref, s32[8]{0:T(128)S(1)} %copy-done.6, bf16[96,512]{1,0:T(8,128)(2,1)S(1)} %collective-permute-done.11.refs_0_, bf16[96,512]{1,0:T(8,128)(2,1)S(1)} %collective-permute-done.15.refs_1_, ...), custom_call_target="tpu_custom_call" | custom-call | tf_op jit(solution)/shard_map/finish/pallas_call | solution.py:501
  (41 shorter events, 0.5 us)
Async XLA Ops:
  0.6 1.4 %copy-start = (bf16[1,1536,512]{2,1,0:T(8,128)(2,1)S(1)}, bf16[1,1536,512]{2,1,0:T(8,128)(2,1)}, u32[]{:S(2)}) copy-start(bf16[1,1536,512]{2,1,0:T(8,128)(2,1)} %own_ref.13) | copy-start | bytes 4718596
  2.1 5.9 %collective-permute-start.4 = (bf16[96,512]{1,0:T(8,128)(2,1)S(1)}, bf16[96,512]{1,0:T(8,128)(2,1)S(1)}, u32[]{:S(2)}, u32[]{:S(2)}) collective-permute-start(bf16[96,512]{1,0:T(8,128)(2,1)S(1)} %get-tuple-element.11), channel_id=1, source_target_pairs={{8,0},{16,8},{24,16},{28,24},{20,28},{12,20},{4,12},{0,4},{9,1},{1... | collective-permute-start | bytes 294920 | tf_op jit(solution)/shard_map/ppermute | solution.py:552
  5.1 5.1 %copy-start.4 = (bf16[192,512]{1,0:T(8,128)(2,1)S(1)}, bf16[192,512]{1,0:T(8,128)(2,1)}, u32[]{:S(2)}) copy-start(bf16[192,512]{1,0:T(8,128)(2,1)} %l_ref.1) | copy-start | bytes 589828
  5.1 5.1 %copy-start.5 = (bf16[192,512]{1,0:T(8,128)(2,1)S(1)}, bf16[192,512]{1,0:T(8,128)(2,1)}, u32[]{:S(2)}) copy-start(bf16[192,512]{1,0:T(8,128)(2,1)} %r_ref.1) | copy-start | bytes 589828
  5.1 5.1 %copy-start.6 = (s32[8]{0:T(128)S(1)}, s32[8]{0:T(128)}, u32[]{:S(2)}) copy-start(s32[8]{0:T(128)} %owner_ref.5) | copy-start | bytes 100
  5.1 4.7 %collective-permute-start = (bf16[96,512]{1,0:T(8,128)(2,1)S(1)}, bf16[96,512]{1,0:T(8,128)(2,1)S(1)}, u32[]{:S(2)}, u32[]{:S(2)}) collective-permute-start(bf16[96,512]{1,0:T(8,128)(2,1)S(1)} %get-tuple-element.10), channel_id=1, source_target_pairs={{0,8},{8,16},{16,24},{24,28},{28,20},{20,12},{12,4},{4,0},{1,9},{9... | collective-permute-start | bytes 294920 | tf_op jit(solution)/shard_map/ppermute | solution.py:549
  8.0 7.9 %copy-start.1 = (bf16[1,1536,512]{2,1,0:T(8,128)(2,1)S(1)}, bf16[1,1536,512]{2,1,0:T(8,128)(2,1)}, u32[]{:S(2)}) copy-start(bf16[1,1536,512]{2,1,0:T(8,128)(2,1)} %own_ref.13) | copy-start | bytes 4718596
  8.0 7.9 %collective-permute-start.5 = (bf16[192,512]{1,0:T(8,128)(2,1)S(1)}, bf16[192,512]{1,0:T(8,128)(2,1)S(1)}, u32[]{:S(2)}, u32[]{:S(2)}) collective-permute-start(bf16[192,512]{1,0:T(8,128)(2,1)S(1)} %add_send.9), channel_id=1, source_target_pairs={{8,0},{16,8},{24,16},{28,24},{20,28},{12,20},{4,12},{0,4},{9,1},{1... | collective-permute-start | bytes 589832 | tf_op jit(solution)/shard_map/ppermute | solution.py:552
  9.8 7.8 %collective-permute-start.1 = (bf16[192,512]{1,0:T(8,128)(2,1)S(1)}, bf16[192,512]{1,0:T(8,128)(2,1)S(1)}, u32[]{:S(2)}, u32[]{:S(2)}) collective-permute-start(bf16[192,512]{1,0:T(8,128)(2,1)S(1)} %add_send.6), channel_id=1, source_target_pairs={{0,8},{8,16},{16,24},{24,28},{28,20},{20,12},{12,4},{4,0},{1,9},{9... | collective-permute-start | bytes 589832 | tf_op jit(solution)/shard_map/ppermute | solution.py:549
  10.9 9.9 %collective-permute-start.23 = (bf16[224,512]{1,0:T(8,128)(2,1)S(1)}, bf16[224,512]{1,0:T(8,128)(2,1)S(1)}, u32[]{:S(2)}, u32[]{:S(2)}) collective-permute-start(bf16[224,512]{1,0:T(8,128)(2,1)S(1)} %pack_roots.1.refs_0_), channel_id=1, source_target_pairs={{8,0},{16,8},{24,16},{28,24},{20,28},{12,20},{4,12},{0,4},{9,1},{1... | collective-permute-start | bytes 688136 | tf_op jit(solution)/shard_map/ppermute | solution.py:552
  12.7 9.8 %collective-permute-start.22 = (bf16[224,512]{1,0:T(8,128)(2,1)S(1)}, bf16[224,512]{1,0:T(8,128)(2,1)S(1)}, u32[]{:S(2)}, u32[]{:S(2)}) collective-permute-start(bf16[224,512]{1,0:T(8,128)(2,1)S(1)} %pack_roots.1.refs_0_), channel_id=1, source_target_pairs={{0,8},{8,16},{16,24},{24,28},{28,20},{20,12},{12,4},{4,0},{1,9},{9... | collective-permute-start | bytes 688136 | tf_op jit(solution)/shard_map/ppermute | solution.py:549
  15.9 9.1 %collective-permute-start.6 = (bf16[192,512]{1,0:T(8,128)(2,1)S(1)}, bf16[192,512]{1,0:T(8,128)(2,1)S(1)}, u32[]{:S(2)}, u32[]{:S(2)}) collective-permute-start(bf16[192,512]{1,0:T(8,128)(2,1)S(1)} %add_send.10), channel_id=1, source_target_pairs={{8,0},{16,8},{24,16},{28,24},{20,28},{12,20},{4,12},{0,4},{9,1},{1... | collective-permute-start | bytes 589832 | tf_op jit(solution)/shard_map/ppermute | solution.py:552
  17.7 9.1 %collective-permute-start.2 = (bf16[192,512]{1,0:T(8,128)(2,1)S(1)}, bf16[192,512]{1,0:T(8,128)(2,1)S(1)}, u32[]{:S(2)}, u32[]{:S(2)}) collective-permute-start(bf16[192,512]{1,0:T(8,128)(2,1)S(1)} %add_send.7), channel_id=1, source_target_pairs={{0,8},{8,16},{16,24},{24,28},{28,20},{20,12},{12,4},{4,0},{1,9},{9... | collective-permute-start | bytes 589832 | tf_op jit(solution)/shard_map/ppermute | solution.py:549
  20.8 9.1 %collective-permute-start.25 = (bf16[224,512]{1,0:T(8,128)(2,1)S(1)}, bf16[224,512]{1,0:T(8,128)(2,1)S(1)}, u32[]{:S(2)}, u32[]{:S(2)}) collective-permute-start(bf16[224,512]{1,0:T(8,128)(2,1)S(1)} %collective-permute-done.23.refs_2_), channel_id=1, source_target_pairs={{8,0},{16,8},{24,16},{28,24},{20,28},{12,20},{4,12},{0,4},{9,1},{1... | collective-permute-start | bytes 688136 | tf_op jit(solution)/shard_map/ppermute | solution.py:552
  22.5 9.1 %collective-permute-start.24 = (bf16[224,512]{1,0:T(8,128)(2,1)S(1)}, bf16[224,512]{1,0:T(8,128)(2,1)S(1)}, u32[]{:S(2)}, u32[]{:S(2)}) collective-permute-start(bf16[224,512]{1,0:T(8,128)(2,1)S(1)} %collective-permute-done.22.refs_1_), channel_id=1, source_target_pairs={{0,8},{8,16},{16,24},{24,28},{28,20},{20,12},{12,4},{4,0},{1,9},{9... | collective-permute-start | bytes 688136 | tf_op jit(solution)/shard_map/ppermute | solution.py:549
  25.1 9.1 %collective-permute-start.7 = (bf16[192,512]{1,0:T(8,128)(2,1)S(1)}, bf16[192,512]{1,0:T(8,128)(2,1)S(1)}, u32[]{:S(2)}, u32[]{:S(2)}) collective-permute-start(bf16[192,512]{1,0:T(8,128)(2,1)S(1)} %add_send.11), channel_id=1, source_target_pairs={{8,0},{16,8},{24,16},{28,24},{20,28},{12,20},{4,12},{0,4},{9,1},{1... | collective-permute-start | bytes 589832 | tf_op jit(solution)/shard_map/ppermute | solution.py:552
  26.8 9.1 %collective-permute-start.3 = (bf16[192,512]{1,0:T(8,128)(2,1)S(1)}, bf16[192,512]{1,0:T(8,128)(2,1)S(1)}, u32[]{:S(2)}, u32[]{:S(2)}) collective-permute-start(bf16[192,512]{1,0:T(8,128)(2,1)S(1)} %add_send.8), channel_id=1, source_target_pairs={{0,8},{8,16},{16,24},{24,28},{28,20},{20,12},{12,4},{4,0},{1,9},{9... | collective-permute-start | bytes 589832 | tf_op jit(solution)/shard_map/ppermute | solution.py:549
  29.9 8.5 %collective-permute-start.27 = (bf16[224,512]{1,0:T(8,128)(2,1)S(1)}, bf16[224,512]{1,0:T(8,128)(2,1)S(1)}, u32[]{:S(2)}, u32[]{:S(2)}) collective-permute-start(bf16[224,512]{1,0:T(8,128)(2,1)S(1)} %collective-permute-done.25.refs_4_), channel_id=1, source_target_pairs={{8,0},{16,8},{24,16},{28,24},{20,28},{12,20},{4,12},{0,4},{9,1},{1... | collective-permute-start | bytes 688136 | tf_op jit(solution)/shard_map/ppermute | solution.py:552
  31.7 11.7 %collective-permute-start.26 = (bf16[224,512]{1,0:T(8,128)(2,1)S(1)}, bf16[224,512]{1,0:T(8,128)(2,1)S(1)}, u32[]{:S(2)}, u32[]{:S(2)}) collective-permute-start(bf16[224,512]{1,0:T(8,128)(2,1)S(1)} %collective-permute-done.24.refs_3_), channel_id=1, source_target_pairs={{0,8},{8,16},{16,24},{24,28},{28,20},{20,12},{12,4},{4,0},{1,9},{9... | collective-permute-start | bytes 688136 | tf_op jit(solution)/shard_map/ppermute | solution.py:549
  36.0 5.0 %collective-permute-start.12 = (bf16[96,512]{1,0:T(8,128)(2,1)S(1)}, bf16[96,512]{1,0:T(8,128)(2,1)S(1)}, u32[]{:S(2)}, u32[]{:S(2)}) collective-permute-start(bf16[96,512]{1,0:T(8,128)(2,1)S(1)} %get-tuple-element.17), channel_id=1, source_target_pairs={{8,0},{16,8},{24,16},{28,24},{20,28},{12,20},{4,12},{0,4},{9,1},{1... | collective-permute-start | bytes 294920 | tf_op jit(solution)/shard_map/ppermute | solution.py:552
  37.6 5.7 %collective-permute-start.8 = (bf16[96,512]{1,0:T(8,128)(2,1)S(1)}, bf16[96,512]{1,0:T(8,128)(2,1)S(1)}, u32[]{:S(2)}, u32[]{:S(2)}) collective-permute-start(bf16[96,512]{1,0:T(8,128)(2,1)S(1)} %get-tuple-element.18), channel_id=1, source_target_pairs={{0,8},{8,16},{16,24},{24,28},{28,20},{20,12},{12,4},{4,0},{1,9},{9... | collective-permute-start | bytes 294920 | tf_op jit(solution)/shard_map/ppermute | solution.py:549
  38.1 7.3 %collective-permute-start.17 = (bf16[96,512]{1,0:T(8,128)(2,1)S(1)}, bf16[96,512]{1,0:T(8,128)(2,1)S(1)}, u32[]{:S(2)}, u32[]{:S(2)}) collective-permute-start(bf16[96,512]{1,0:T(8,128)(2,1)S(1)} %get-tuple-element.17), channel_id=1, source_target_pairs={{0,8},{8,16},{16,24},{24,28},{28,20},{20,12},{12,4},{4,0},{1,9},{9... | collective-permute-start | bytes 294920 | tf_op jit(solution)/shard_map/ppermute | solution.py:549
  38.4 7.1 %collective-permute-start.16 = (bf16[96,512]{1,0:T(8,128)(2,1)S(1)}, bf16[96,512]{1,0:T(8,128)(2,1)S(1)}, u32[]{:S(2)}, u32[]{:S(2)}) collective-permute-start(bf16[96,512]{1,0:T(8,128)(2,1)S(1)} %get-tuple-element.18), channel_id=1, source_target_pairs={{8,0},{16,8},{24,16},{28,24},{20,28},{12,20},{4,12},{0,4},{9,1},{1... | collective-permute-start | bytes 294920 | tf_op jit(solution)/shard_map/ppermute | solution.py:552
  41.0 6.4 %collective-permute-start.13 = (bf16[96,512]{1,0:T(8,128)(2,1)S(1)}, bf16[96,512]{1,0:T(8,128)(2,1)S(1)}, u32[]{:S(2)}, u32[]{:S(2)}) collective-permute-start(bf16[96,512]{1,0:T(8,128)(2,1)S(1)} %collective-permute-done.12.refs_4_), channel_id=1, source_target_pairs={{8,0},{16,8},{24,16},{28,24},{20,28},{12,20},{4,12},{0,4},{9,1},{1... | collective-permute-start | bytes 294920 | tf_op jit(solution)/shard_map/ppermute | solution.py:552
  43.3 5.7 %collective-permute-start.9 = (bf16[96,512]{1,0:T(8,128)(2,1)S(1)}, bf16[96,512]{1,0:T(8,128)(2,1)S(1)}, u32[]{:S(2)}, u32[]{:S(2)}) collective-permute-start(bf16[96,512]{1,0:T(8,128)(2,1)S(1)} %collective-permute-done.8.refs_1_), channel_id=1, source_target_pairs={{0,8},{8,16},{16,24},{24,28},{28,20},{20,12},{12,4},{4,0},{1,9},{9... | collective-permute-start | bytes 294920 | tf_op jit(solution)/shard_map/ppermute | solution.py:549
  43.4 6.1 %collective-permute-start.29 = (bf16[112,512]{1,0:T(8,128)(2,1)S(1)}, bf16[112,512]{1,0:T(8,128)(2,1)S(1)}, u32[]{:S(2)}, u32[]{:S(2)}) collective-permute-start(bf16[112,512]{1,0:T(8,128)(2,1)S(1)} %slice.19), channel_id=1, source_target_pairs={{8,0},{16,8},{24,16},{28,24},{20,28},{12,20},{4,12},{0,4},{9,1},{1... | collective-permute-start | bytes 344072 | tf_op jit(solution)/shard_map/ppermute | solution.py:552
  45.4 5.7 %collective-permute-start.19 = (bf16[96,512]{1,0:T(8,128)(2,1)S(1)}, bf16[96,512]{1,0:T(8,128)(2,1)S(1)}, u32[]{:S(2)}, u32[]{:S(2)}) collective-permute-start(bf16[96,512]{1,0:T(8,128)(2,1)S(1)} %collective-permute-done.17.refs_3_), channel_id=1, source_target_pairs={{0,8},{8,16},{16,24},{24,28},{28,20},{20,12},{12,4},{4,0},{1,9},{9... | collective-permute-start | bytes 294920 | tf_op jit(solution)/shard_map/ppermute | solution.py:549
  45.5 6.1 %collective-permute-start.18 = (bf16[96,512]{1,0:T(8,128)(2,1)S(1)}, bf16[96,512]{1,0:T(8,128)(2,1)S(1)}, u32[]{:S(2)}, u32[]{:S(2)}) collective-permute-start(bf16[96,512]{1,0:T(8,128)(2,1)S(1)} %collective-permute-done.16.refs_2_), channel_id=1, source_target_pairs={{8,0},{16,8},{24,16},{28,24},{20,28},{12,20},{4,12},{0,4},{9,1},{1... | collective-permute-start | bytes 294920 | tf_op jit(solution)/shard_map/ppermute | solution.py:552
  47.4 5.7 %collective-permute-start.14 = (bf16[96,512]{1,0:T(8,128)(2,1)S(1)}, bf16[96,512]{1,0:T(8,128)(2,1)S(1)}, u32[]{:S(2)}, u32[]{:S(2)}) collective-permute-start(bf16[96,512]{1,0:T(8,128)(2,1)S(1)} %collective-permute-done.13.refs_8_), channel_id=1, source_target_pairs={{8,0},{16,8},{24,16},{28,24},{20,28},{12,20},{4,12},{0,4},{9,1},{1... | collective-permute-start | bytes 294920 | tf_op jit(solution)/shard_map/ppermute | solution.py:552
  49.0 5.7 %collective-permute-start.10 = (bf16[96,512]{1,0:T(8,128)(2,1)S(1)}, bf16[96,512]{1,0:T(8,128)(2,1)S(1)}, u32[]{:S(2)}, u32[]{:S(2)}) collective-permute-start(bf16[96,512]{1,0:T(8,128)(2,1)S(1)} %collective-permute-done.9.refs_5_), channel_id=1, source_target_pairs={{0,8},{8,16},{16,24},{24,28},{28,20},{20,12},{12,4},{4,0},{1,9},{9... | collective-permute-start | bytes 294920 | tf_op jit(solution)/shard_map/ppermute | solution.py:549
  49.5 5.7 %collective-permute-start.28 = (bf16[112,512]{1,0:T(8,128)(2,1)S(1)}, bf16[112,512]{1,0:T(8,128)(2,1)S(1)}, u32[]{:S(2)}, u32[]{:S(2)}) collective-permute-start(bf16[112,512]{1,0:T(8,128)(2,1)S(1)} %slice.18), channel_id=1, source_target_pairs={{0,8},{8,16},{16,24},{24,28},{28,20},{20,12},{12,4},{4,0},{1,9},{9... | collective-permute-start | bytes 344072 | tf_op jit(solution)/shard_map/ppermute | solution.py:549
  51.1 6.5 %collective-permute-start.21 = (bf16[96,512]{1,0:T(8,128)(2,1)S(1)}, bf16[96,512]{1,0:T(8,128)(2,1)S(1)}, u32[]{:S(2)}, u32[]{:S(2)}) collective-permute-start(bf16[96,512]{1,0:T(8,128)(2,1)S(1)} %collective-permute-done.19.refs_7_), channel_id=1, source_target_pairs={{0,8},{8,16},{16,24},{24,28},{28,20},{20,12},{12,4},{4,0},{1,9},{9... | collective-permute-start | bytes 294920 | tf_op jit(solution)/shard_map/ppermute | solution.py:549
  51.6 6.1 %collective-permute-start.20 = (bf16[96,512]{1,0:T(8,128)(2,1)S(1)}, bf16[96,512]{1,0:T(8,128)(2,1)S(1)}, u32[]{:S(2)}, u32[]{:S(2)}) collective-permute-start(bf16[96,512]{1,0:T(8,128)(2,1)S(1)} %collective-permute-done.18.refs_6_), channel_id=1, source_target_pairs={{8,0},{16,8},{24,16},{28,24},{20,28},{12,20},{4,12},{0,4},{9,1},{1... | collective-permute-start | bytes 294920 | tf_op jit(solution)/shard_map/ppermute | solution.py:552
  53.2 7.1 %collective-permute-start.15 = (bf16[96,512]{1,0:T(8,128)(2,1)S(1)}, bf16[96,512]{1,0:T(8,128)(2,1)S(1)}, u32[]{:S(2)}, u32[]{:S(2)}) collective-permute-start(bf16[96,512]{1,0:T(8,128)(2,1)S(1)} %collective-permute-done.14.refs_12_), channel_id=1, source_target_pairs={{8,0},{16,8},{24,16},{28,24},{20,28},{12,20},{4,12},{0,4},{9,1},{1... | collective-permute-start | bytes 294920 | tf_op jit(solution)/shard_map/ppermute | solution.py:552
  54.7 5.6 %collective-permute-start.11 = (bf16[96,512]{1,0:T(8,128)(2,1)S(1)}, bf16[96,512]{1,0:T(8,128)(2,1)S(1)}, u32[]{:S(2)}, u32[]{:S(2)}) collective-permute-start(bf16[96,512]{1,0:T(8,128)(2,1)S(1)} %collective-permute-done.10.refs_9_), channel_id=1, source_target_pairs={{0,8},{8,16},{16,24},{24,28},{28,20},{20,12},{12,4},{4,0},{1,9},{9... | collective-permute-start | bytes 294920 | tf_op jit(solution)/shard_map/ppermute | solution.py:549
  57.6 2.7 %copy-start.2 = (f32[192,512]{1,0:T(8,128)S(1)}, f32[192,512]{1,0:T(8,128)}, u32[]{:S(2)}) copy-start(f32[192,512]{1,0:T(8,128)} %refs_7_.1) | copy-start | bytes 1179652
  57.7 2.6 %copy-start.3 = (f32[192,512]{1,0:T(8,128)S(1)}, f32[192,512]{1,0:T(8,128)}, u32[]{:S(2)}) copy-start(f32[192,512]{1,0:T(8,128)} %refs_8_.1) | copy-start | bytes 1179652

commit v5 on v4

--- a/solution.py
+++ b/solution.py
@@ -93,10 +93,9 @@
 
 
 def band_of(owner_ref, device, n):
-    band = jnp.int32(0)
-    for k in range(n):
-        band = band + jnp.where(owner_ref[k] == device, k, 0)
-    return band
+    order = lax.broadcasted_iota(jnp.int32, (1, n), 1)
+    hit = owner_ref[...] == device
+    return jnp.sum(jnp.where(hit, order, 0).astype(F32)).astype(jnp.int32)
 
 
 def whole(*shape):
@@ -199,9 +198,9 @@
         kernel,
         out_shape=jax.ShapeDtypeStruct((band + more, breadth), BF16),
         grid_spec=pltpu.PrefetchScalarGridSpec(
-            num_scalar_prefetch=2,
+            num_scalar_prefetch=1,
             grid=(1,),
-            in_specs=[whole(band, breadth), whole(band, breadth)],
+            in_specs=[whole(1, n), whole(band, breadth), whole(band, breadth)],
             out_specs=whole(band + more, breadth),
         ),
         compiler_params=params(),
@@ -213,7 +212,6 @@
     tiles = breadth // TILE
     quarter = tiles // 4
     low = lower_half(TILE)
-    zeros = jnp.zeros((TILE, PAIR), BF16)
     for offset, number in numbers.items():
         parts = [(first, ref) for (place, first, _), ref in zip(pieces, refs) if place == offset]
         more = max(first + ref.shape[0] for first, ref in parts) - band
@@ -254,7 +252,6 @@
                 for i in range(1, quarter):
                     some = rows_at(row, row + TILE, slice((start + i) * PAIR, (start + i + 1) * PAIR))
                     half[at, lanes(pair + i, breadth)] = some.astype(BF16)
-                    half[at, lanes(pair + quarter + i, breadth)] = zeros
 
 
 def add_send(me, partial, arrived, distance, n, first, *after):
@@ -321,22 +318,34 @@
     nblocks = stacked // breadth
 
     def kernel(me_ref, owner_ref, *refs):
-        refs, (left_ref, right_ref, half_l, half_r, table, sem) = refs[: len(pieces)], refs[len(pieces) :]
-        copy = pltpu.make_async_copy(owner_ref, table, sem)
-        copy.start()
-        shift = TILE.bit_length() - 1
-        down = lax.broadcasted_iota(jnp.int32, (breadth, breadth), 0) >> shift
-        over = lax.broadcasted_iota(jnp.int32, (breadth, breadth), 1) >> shift
-        apart = over - down + jnp.where(over < down, tiles, 0)
-        mirrored = (apart > 0) & (apart <= tiles // 2)
-        copy.wait()
-        numbers = {o: band_of(table, away(me_ref[0], o, n), n) for o in sorted({p[0] for p in pieces})}
+        refs, (left_ref, right_ref, half_l, half_r) = refs[: len(pieces)], refs[len(pieces) :]
+        upper = lax.broadcasted_iota(jnp.int32, (PAIR, PAIR), 0) < TILE
+        aside = upper & (lax.broadcasted_iota(jnp.int32, (PAIR, PAIR), 1) >= TILE)
+        numbers = {}
+        for offset in sorted({p[0] for p in pieces}):
+            numbers[offset] = band_of(owner_ref, away(me_ref[0], offset, n), n)
         place_packed(pieces, refs, numbers, half_l, half_r, band, breadth)
+        pairs = tiles // 2
         for half, out in ((half_r, right_ref), (half_l, left_ref)):
             for b in range(nblocks):
-                rows = slice(b * breadth, (b + 1) * breadth)
-                upper = half[rows]
-                out[rows] = upper + jnp.where(mirrored, upper, jnp.zeros_like(upper)).T
+
+                def square(i, j):
+                    top = b * breadth + i * PAIR
+                    return slice(top, top + PAIR), slice(j * PAIR, (j + 1) * PAIR)
+
+                for i in range(pairs):
+                    for j in range(pairs):
+                        apart = (i - j) % pairs
+                        if apart == 0:
+                            here = half[square(i, i)]
+                            value = here + jnp.where(aside, here, jnp.zeros_like(here)).T
+                        elif apart < pairs // 2:
+                            value = half[square(j, i)].T
+                        elif apart == pairs // 2:
+                            value = half[square(i, j)] + half[square(j, i)].T
+                        else:
+                            value = half[square(i, j)]
+                        out[square(i, j)] = value
 
     out = jax.ShapeDtypeStruct((stacked, breadth), BF16)
     return pl.pallas_call(
@@ -345,10 +354,9 @@
         grid_spec=pltpu.PrefetchScalarGridSpec(
             num_scalar_prefetch=1,
             grid=(1,),
-            in_specs=[pl.BlockSpec(memory_space=pl.ANY)] + [whole(*x.shape) for _, _, x in pieces],
+            in_specs=[whole(1, n)] + [whole(*x.shape) for _, _, x in pieces],
             out_specs=(whole(stacked, breadth), whole(stacked, breadth)),
-            scratch_shapes=[pltpu.VMEM((stacked, breadth), BF16)] * 2
-            + [pltpu.SMEM((n,), jnp.int32), pltpu.SemaphoreType.DMA],
+            scratch_shapes=[pltpu.VMEM((stacked, breadth), BF16)] * 2,
         ),
         compiler_params=params(),
         name="unpack_roots",
@@ -373,18 +381,14 @@
             mixed = jnp.dot(grad[rows], rroot[rows], preferred_element_type=F32).astype(BF16)
             block = jnp.dot(lroot[rows], mixed, preferred_element_type=F32)
             dir_ref[rows] = block.astype(BF16)
-            for slot, at in enumerate((start, start + band - 1)):
-
-                @pl.when(at >> (breadth.bit_length() - 1) == b)
-                def _():
-                    rest_ref[slot] = block
+            rest_ref[b] = block
 
     return pl.pallas_call(
         kernel,
         out_shape=(
             jax.ShapeDtypeStruct((stacked, breadth), BF16),
             jax.ShapeDtypeStruct((stacked, breadth), BF16),
-            jax.ShapeDtypeStruct((2, breadth, breadth), F32),
+            jax.ShapeDtypeStruct((nblocks, breadth, breadth), F32),
         ),
         grid_spec=pltpu.PrefetchScalarGridSpec(
             num_scalar_prefetch=1,
@@ -393,7 +397,7 @@
             out_specs=(
                 whole(stacked, breadth),
                 whole(stacked, breadth),
-                whole(2, breadth, breadth),
+                whole(nblocks, breadth, breadth),
             ),
         ),
         compiler_params=params(),
@@ -409,9 +413,7 @@
     def kernel(me_ref, owner_ref, *refs):
         parts, refs = refs[: len(pieces)], refs[len(pieces) :]
         part_ref, grad_ref, rest_ref, lroot, rroot, lfac, rfac, *refs = refs
-        dir_ref, lout_ref, rout_ref, late, block, lout, rout, table, sems = refs
-        lookup = pltpu.make_async_copy(owner_ref, table, sems.at[4 + nblocks])
-        lookup.start()
+        dir_ref, lout_ref, rout_ref, late, block, lout, rout, sems = refs
         far = away(me_ref[0], n // 2, n) * band
         for (_, first, _), ref in zip(pieces, parts):
             late[first : first + ref.shape[0]] = ref[...]
@@ -441,17 +443,9 @@
             some = jnp.where(row == number, late[...].astype(F32), 0.0).astype(BF16)
             mixed = jnp.dot(some, rroot[span(number), :], preferred_element_type=F32).astype(BF16)
             more = lax.dot_general(lroot[there, :], mixed, TN, preferred_element_type=F32)
-            block[slot] = (rest_ref[slot] + more).astype(BF16)
-            copy(slot, number).start()
-
-        complete(0, first_block)
-
-        @pl.when(last_block != first_block)
-        def _():
-            complete(1, last_block)
-
-        lookup.wait()
-        start = band_of(table, me_ref[0], n) * band
+            block[slot] = (rest_ref[number] + more).astype(BF16)
+
+        start = band_of(owner_ref, me_ref[0], n) * band
         grad_ref[there, :] = late[...]
         mine = grad_ref[pl.ds(pl.multiple_of(start, CHUNK), band), :]
         own_first = start >> shift
@@ -459,27 +453,32 @@
         own_row = start + lax.broadcasted_iota(jnp.int32, (band, breadth), 0)
         column = lax.broadcasted_iota(jnp.int32, (band, breadth), 1)
 
-        def left_term(number):
-            return lax.dot_general(mine, grad_ref[span(number), :], NT, preferred_element_type=F32)
-
-        def right_term(number):
+        def renewed(number):
             g = grad_ref[span(number), :]
+            left = lax.dot_general(mine, g, NT, preferred_element_type=F32)
             pick = (own_row - number * breadth == column).astype(BF16)
             turned = lax.dot_general(pick, g, NT, preferred_element_type=F32).astype(BF16)
-            return jnp.dot(turned, g, preferred_element_type=F32)
-
-        later = own_row >= own_last * breadth
+            right = jnp.dot(turned, g, preferred_element_type=F32)
+            return BETA * lfac[...] + (1.0 - BETA) * left, BETA * rfac[...] + (1.0 - BETA) * right
+
+        complete(0, first_block)
+        lout[...], rout[...] = renewed(own_first)
+        copy(0, first_block).start()
+
+        @pl.when(last_block != first_block)
+        def _():
+            complete(1, last_block)
+            copy(1, last_block).start()
+
+        @pl.when(own_last != own_first)
+        def _():
+            later = own_row >= own_last * breadth
+            left, right = renewed(own_last)
+            lout[...] = jnp.where(later, left, lout[...])
+            rout[...] = jnp.where(later, right, rout[...])
+
         outs = []
-        for slot, (term, fac, out, ref) in enumerate(
-            ((left_term, lfac, lout, lout_ref), (right_term, rfac, rout, rout_ref))
-        ):
-            out[...] = BETA * fac[...] + (1.0 - BETA) * term(own_first)
-
-            @pl.when(own_last != own_first)
-            def _():
-                new = BETA * fac[...] + (1.0 - BETA) * term(own_last)
-                out[...] = jnp.where(later, new, out[...])
-
+        for slot, (out, ref) in enumerate(((lout, lout_ref), (rout, rout_ref))):
             outs.append(pltpu.make_async_copy(out, ref, sems.at[2 + slot]))
             outs[-1].start()
         copy(0, first_block).wait()
@@ -504,10 +503,10 @@
         grid_spec=pltpu.PrefetchScalarGridSpec(
             num_scalar_prefetch=1,
             grid=(1,),
-            in_specs=[pl.BlockSpec(memory_space=pl.ANY)]
+            in_specs=[whole(1, n)]
             + [whole(*x.shape) for _, _, x in pieces]
             + [whole(stacked, breadth)] * 2
-            + [whole(2, breadth, breadth)]
+            + [whole(nblocks, breadth, breadth)]
             + [whole(stacked, breadth)] * 2
             + [whole(band, breadth)] * 2,
             out_specs=[pl.BlockSpec(memory_space=pl.ANY)] * 3,
@@ -516,8 +515,7 @@
                 pltpu.VMEM((2, breadth, breadth), BF16),
                 pltpu.VMEM((band, breadth), F32),
                 pltpu.VMEM((band, breadth), F32),
-                pltpu.SMEM((n,), jnp.int32),
-                pltpu.SemaphoreType.DMA((5 + nblocks,)),
+                pltpu.SemaphoreType.DMA((4 + nblocks,)),
             ],
         ),
         compiler_params=params(),
@@ -541,6 +539,7 @@
     band = stacked // n
     half = band // 2
     me = lax.axis_index("dp").astype(jnp.int32).reshape(1)
+    owner = band_owner.reshape(1, n)
     order = [2 * q for q in range(n // 2)] + [2 * (n - 1 - q) + 1 for q in range(n // 2, n)]
     onward = [(order[q], order[(q + 1) % n]) for q in range(n)]
     backward = [(b, a) for a, b in onward]
@@ -576,18 +575,18 @@
         return pieces + [(n // 2, 0, right), (n // 2, rows, left)]
 
     right, left = first_sends(me, partial_grads, n)
-    packed = pack_roots(me, band_owner, left_root, right_root, n)
+    packed = pack_roots(me, owner, left_root, right_root, n)
     right, left = send_right(right), send_left(left)
     root_pieces = gather(packed, 1)
     for distance in range(n // 2 - 1, 0, -1):
         right = add_send(me, partial_grads, right, distance, n, 0)
         left = add_send(me, partial_grads, left, -distance, n, half if left.shape[0] == half else 0)
         right, left = send_right(right), send_left(left)
-    roots = unpack_roots(me, band_owner, root_pieces, stacked, breadth, n)
+    roots = unpack_roots(me, owner, root_pieces, stacked, breadth, n)
     own = add_own(me, partial_grads, right, left, n)
     pieces = gather(own, GRAD_PARTS)
     begun = begin(me, pieces[:-2], *roots, n)
-    return finish(me, band_owner, pieces[-2:], *begun, *roots, left_factor, right_factor, n)
+    return finish(me, owner, pieces[-2:], *begun, *roots, left_factor, right_factor, n)
 
 
 def shards(n, partial_grads, *rest):

time: 62.7 us -> 62 us (0.989)
  Pallas kernels: 8.34 us -> 6.88 us
  starting transfers between devices: 32.1 us -> 32.9 us
    pallas_call x1, Pallas kernels: 2.42 us -> 1.78 us  [unpack_roots(): pl.pallas_call(kernel, out_shape=(out, out), grid_spec=pltpu.PrefetchScal...]
  transfers between devices with their start and end apart: 30 -> 30, of which waited for: 14 -> 12; matrix products, arithmetic and copies ran while one was open for 0% -> 0% of each run, Pallas kernels for 10% -> 7%
where the time goes in v5:
time: 62 us; the launch traced here: 61.8 us
  starting transfers between devices  32.9 us (53%)
  waiting for transfers between devices  19.7 us (32%)
  Pallas kernels  6.88 us (11%)
  local copies, waits for them, and re-layouts  1.47 us (2%)
  between operations  0.82 us (1%)
    ppermute x15, starting transfers between devices, send_left(): return lax.ppermute(x, 'dp', backward)  27.4 us
    ppermute x15, waiting for transfers between devices, send_left(): return lax.ppermute(x, 'dp', backward)  16.5 us
    ppermute x15, starting transfers between devices, send_right(): return lax.ppermute(x, 'dp', onward)  5.5 us
    ppermute x15, waiting for transfers between devices, send_right(): return lax.ppermute(x, 'dp', onward)  3.14 us
    pallas_call x1, Pallas kernels, finish(): pl.pallas_call(kernel, out_shape=(jax.ShapeDtypeStruct((stacked, breadth)...  2.35 us
    pallas_call x1, Pallas kernels, begin(): pl.pallas_call(kernel, out_shape=(jax.ShapeDtypeStruct((stacked, breadth)...  2.1 us
    pallas_call x1, Pallas kernels, unpack_roots(): pl.pallas_call(kernel, out_shape=(out, out), grid_spec=pltpu.PrefetchScal...  1.78 us
    unnamed x14, local copies, waits for them, and re-layouts  1.43 us
  transfers between devices with their start and end apart: 30, of which 12 were waited for; matrix products, arithmetic and copies ran while one was open for 0% of the time, Pallas kernels for 7%

profile of v5, /device:TPU:0, one launch (start us, length us, event | category | flops | bytes accessed | tf_op | source)
XLA Modules:
  0.0 61.8 jit_solution(12813842483458718668)
XLA Ops:
  0.6 1.4 %copy-done = bf16[1,1536,512]{2,1,0:T(8,128)(2,1)S(1)} copy-done((bf16[1,1536,512]{2,1,0:T(8,128)(2,1)S(1)}, bf16[1,1536,512]{2,1,0:T(8,128)(2,1)}, u32[]{:S(2)}) %copy-start) | copy-done | bytes 1572888
  2.1 3.0 %collective-permute-start.4 = (bf16[96,512]{1,0:T(8,128)(2,1)S(1)}, bf16[96,512]{1,0:T(8,128)(2,1)S(1)}, u32[]{:S(2)}, u32[]{:S(2)}) collective-permute-start(bf16[96,512]{1,0:T(8,128)(2,1)S(1)} %get-tuple-element.11), channel_id=1, source_target_pairs={{8,0},{16,8},{24,16},{28,24},{20,28},{12,20},{4,12},{0,4},{9,1},{1... | collective-permute-start | bytes 294920 | tf_op jit(solution)/shard_map/ppermute | solution.py:551
  5.1 0.2 collective-permute-start
  5.2 2.7 %collective-permute-done.4.a_ref = bf16[96,512]{1,0:T(8,128)(2,1)S(1)} collective-permute-done((bf16[96,512]{1,0:T(8,128)(2,1)S(1)}, bf16[96,512]{1,0:T(8,128)(2,1)S(1)}, u32[]{:S(2)}, u32[]{:S(2)}) %collective-permute-start.4) | collective-permute-done | bytes 98336 | tf_op jit(solution)/shard_map/ppermute | solution.py:551
  8.0 1.8 %collective-permute-start.5 = (bf16[192,512]{1,0:T(8,128)(2,1)S(1)}, bf16[192,512]{1,0:T(8,128)(2,1)S(1)}, u32[]{:S(2)}, u32[]{:S(2)}) collective-permute-start(bf16[192,512]{1,0:T(8,128)(2,1)S(1)} %add_send.9), channel_id=1, source_target_pairs={{8,0},{16,8},{24,16},{28,24},{20,28},{12,20},{4,12},{0,4},{9,1},{1... | collective-permute-start | bytes 589832 | tf_op jit(solution)/shard_map/ppermute | solution.py:551
  9.8 0.3 collective-permute-start.1
  10.2 0.3 pack_roots.1.refs_0_
  10.4 1.9 %collective-permute-start.23 = (bf16[224,512]{1,0:T(8,128)(2,1)S(1)}, bf16[224,512]{1,0:T(8,128)(2,1)S(1)}, u32[]{:S(2)}, u32[]{:S(2)}) collective-permute-start(bf16[224,512]{1,0:T(8,128)(2,1)S(1)} %pack_roots.1.refs_0_), channel_id=1, source_target_pairs={{8,0},{16,8},{24,16},{28,24},{20,28},{12,20},{4,12},{0,4},{9,1},{1... | collective-permute-start | bytes 688136 | tf_op jit(solution)/shard_map/ppermute | solution.py:551
  12.3 0.2 collective-permute-start.22
  12.5 3.4 %collective-permute-done.5.a_ref = bf16[192,512]{1,0:T(8,128)(2,1)S(1)} collective-permute-done((bf16[192,512]{1,0:T(8,128)(2,1)S(1)}, bf16[192,512]{1,0:T(8,128)(2,1)S(1)}, u32[]{:S(2)}, u32[]{:S(2)}) %collective-permute-start.5) | collective-permute-done | bytes 196640 | tf_op jit(solution)/shard_map/ppermute | solution.py:551
  15.9 1.8 %collective-permute-start.6 = (bf16[192,512]{1,0:T(8,128)(2,1)S(1)}, bf16[192,512]{1,0:T(8,128)(2,1)S(1)}, u32[]{:S(2)}, u32[]{:S(2)}) collective-permute-start(bf16[192,512]{1,0:T(8,128)(2,1)S(1)} %add_send.10), channel_id=1, source_target_pairs={{8,0},{16,8},{24,16},{28,24},{20,28},{12,20},{4,12},{0,4},{9,1},{1... | collective-permute-start | bytes 589832 | tf_op jit(solution)/shard_map/ppermute | solution.py:551
  17.8 0.3 collective-permute-start.2
  18.1 2.7 %collective-permute-done.23.refs_2_ = bf16[224,512]{1,0:T(8,128)(2,1)S(1)} collective-permute-done((bf16[224,512]{1,0:T(8,128)(2,1)S(1)}, bf16[224,512]{1,0:T(8,128)(2,1)S(1)}, u32[]{:S(2)}, u32[]{:S(2)}) %collective-permute-start.23) | collective-permute-done | bytes 229408 | tf_op jit(solution)/shard_map/ppermute | solution.py:551
  20.8 1.7 %collective-permute-start.25 = (bf16[224,512]{1,0:T(8,128)(2,1)S(1)}, bf16[224,512]{1,0:T(8,128)(2,1)S(1)}, u32[]{:S(2)}, u32[]{:S(2)}) collective-permute-start(bf16[224,512]{1,0:T(8,128)(2,1)S(1)} %collective-permute-done.23.refs_2_), channel_id=1, source_target_pairs={{8,0},{16,8},{24,16},{28,24},{20,28},{12,20},{4,12},{0,4},{9,1},{1... | collective-permute-start | bytes 688136 | tf_op jit(solution)/shard_map/ppermute | solution.py:551
  22.5 0.1 collective-permute-done.22.refs_1_
  22.6 0.3 collective-permute-start.24
  22.9 2.1 %collective-permute-done.6.a_ref = bf16[192,512]{1,0:T(8,128)(2,1)S(1)} collective-permute-done((bf16[192,512]{1,0:T(8,128)(2,1)S(1)}, bf16[192,512]{1,0:T(8,128)(2,1)S(1)}, u32[]{:S(2)}, u32[]{:S(2)}) %collective-permute-start.6) | collective-permute-done | bytes 196640 | tf_op jit(solution)/shard_map/ppermute | solution.py:551
  25.1 1.8 %collective-permute-start.7 = (bf16[192,512]{1,0:T(8,128)(2,1)S(1)}, bf16[192,512]{1,0:T(8,128)(2,1)S(1)}, u32[]{:S(2)}, u32[]{:S(2)}) collective-permute-start(bf16[192,512]{1,0:T(8,128)(2,1)S(1)} %add_send.11), channel_id=1, source_target_pairs={{8,0},{16,8},{24,16},{28,24},{20,28},{12,20},{4,12},{0,4},{9,1},{1... | collective-permute-start | bytes 589832 | tf_op jit(solution)/shard_map/ppermute | solution.py:551
  26.9 0.3 collective-permute-start.3
  27.3 2.7 %collective-permute-done.25.refs_4_ = bf16[224,512]{1,0:T(8,128)(2,1)S(1)} collective-permute-done((bf16[224,512]{1,0:T(8,128)(2,1)S(1)}, bf16[224,512]{1,0:T(8,128)(2,1)S(1)}, u32[]{:S(2)}, u32[]{:S(2)}) %collective-permute-start.25) | collective-permute-done | bytes 229408 | tf_op jit(solution)/shard_map/ppermute | solution.py:551
  29.9 1.7 %collective-permute-start.27 = (bf16[224,512]{1,0:T(8,128)(2,1)S(1)}, bf16[224,512]{1,0:T(8,128)(2,1)S(1)}, u32[]{:S(2)}, u32[]{:S(2)}) collective-permute-start(bf16[224,512]{1,0:T(8,128)(2,1)S(1)} %collective-permute-done.25.refs_4_), channel_id=1, source_target_pairs={{8,0},{16,8},{24,16},{28,24},{20,28},{12,20},{4,12},{0,4},{9,1},{1... | collective-permute-start | bytes 688136 | tf_op jit(solution)/shard_map/ppermute | solution.py:551
  31.7 0.1 collective-permute-done.24.refs_3_
  31.7 0.3 collective-permute-start.26
  32.0 2.1 %collective-permute-done.7.l_ref = bf16[192,512]{1,0:T(8,128)(2,1)S(1)} collective-permute-done((bf16[192,512]{1,0:T(8,128)(2,1)S(1)}, bf16[192,512]{1,0:T(8,128)(2,1)S(1)}, u32[]{:S(2)}, u32[]{:S(2)}) %collective-permute-start.7) | collective-permute-done | bytes 196640 | tf_op jit(solution)/shard_map/ppermute | solution.py:551
  34.1 1.8 %collective-permute-done.3.r_ref = bf16[192,512]{1,0:T(8,128)(2,1)S(1)} collective-permute-done((bf16[192,512]{1,0:T(8,128)(2,1)S(1)}, bf16[192,512]{1,0:T(8,128)(2,1)S(1)}, u32[]{:S(2)}, u32[]{:S(2)}) %collective-permute-start.3) | collective-permute-done | bytes 196640 | tf_op jit(solution)/shard_map/ppermute | solution.py:548
  36.0 0.1 add_own.1.refs_0_
  36.1 1.6 %collective-permute-start.12 = (bf16[96,512]{1,0:T(8,128)(2,1)S(1)}, bf16[96,512]{1,0:T(8,128)(2,1)S(1)}, u32[]{:S(2)}, u32[]{:S(2)}) collective-permute-start(bf16[96,512]{1,0:T(8,128)(2,1)S(1)} %get-tuple-element.17), channel_id=1, source_target_pairs={{8,0},{16,8},{24,16},{28,24},{20,28},{12,20},{4,12},{0,4},{9,1},{1... | collective-permute-start | bytes 294920 | tf_op jit(solution)/shard_map/ppermute | solution.py:551
  37.7 0.4 collective-permute-start.8
  38.1 0.3 collective-permute-start.17
  38.4 1.7 %collective-permute-start.16 = (bf16[96,512]{1,0:T(8,128)(2,1)S(1)}, bf16[96,512]{1,0:T(8,128)(2,1)S(1)}, u32[]{:S(2)}, u32[]{:S(2)}) collective-permute-start(bf16[96,512]{1,0:T(8,128)(2,1)S(1)} %get-tuple-element.18), channel_id=1, source_target_pairs={{8,0},{16,8},{24,16},{28,24},{20,28},{12,20},{4,12},{0,4},{9,1},{1... | collective-permute-start | bytes 294920 | tf_op jit(solution)/shard_map/ppermute | solution.py:551
  40.2 1.0 %collective-permute-done.12.refs_4_ = bf16[96,512]{1,0:T(8,128)(2,1)S(1)} collective-permute-done((bf16[96,512]{1,0:T(8,128)(2,1)S(1)}, bf16[96,512]{1,0:T(8,128)(2,1)S(1)}, u32[]{:S(2)}, u32[]{:S(2)}) %collective-permute-start.12) | collective-permute-done | bytes 98336 | tf_op jit(solution)/shard_map/ppermute | solution.py:551
  41.2 2.1 %collective-permute-start.13 = (bf16[96,512]{1,0:T(8,128)(2,1)S(1)}, bf16[96,512]{1,0:T(8,128)(2,1)S(1)}, u32[]{:S(2)}, u32[]{:S(2)}) collective-permute-start(bf16[96,512]{1,0:T(8,128)(2,1)S(1)} %collective-permute-done.12.refs_4_), channel_id=1, source_target_pairs={{8,0},{16,8},{24,16},{28,24},{20,28},{12,20},{4,12},{0,4},{9,1},{1... | collective-permute-start | bytes 294920 | tf_op jit(solution)/shard_map/ppermute | solution.py:551
  43.3 0.2 collective-permute-start.9
  43.5 1.8 %collective-permute-start.29 = (bf16[112,512]{1,0:T(8,128)(2,1)S(1)}, bf16[112,512]{1,0:T(8,128)(2,1)S(1)}, u32[]{:S(2)}, u32[]{:S(2)}) collective-permute-start(bf16[112,512]{1,0:T(8,128)(2,1)S(1)} %slice.19), channel_id=1, source_target_pairs={{8,0},{16,8},{24,16},{28,24},{20,28},{12,20},{4,12},{0,4},{9,1},{1... | collective-permute-start | bytes 344072 | tf_op jit(solution)/shard_map/ppermute | solution.py:551
  45.4 0.2 collective-permute-start.19
  45.6 1.8 %collective-permute-start.18 = (bf16[96,512]{1,0:T(8,128)(2,1)S(1)}, bf16[96,512]{1,0:T(8,128)(2,1)S(1)}, u32[]{:S(2)}, u32[]{:S(2)}) collective-permute-start(bf16[96,512]{1,0:T(8,128)(2,1)S(1)} %collective-permute-done.16.refs_2_), channel_id=1, source_target_pairs={{8,0},{16,8},{24,16},{28,24},{20,28},{12,20},{4,12},{0,4},{9,1},{1... | collective-permute-start | bytes 294920 | tf_op jit(solution)/shard_map/ppermute | solution.py:551
  47.4 1.6 %collective-permute-start.14 = (bf16[96,512]{1,0:T(8,128)(2,1)S(1)}, bf16[96,512]{1,0:T(8,128)(2,1)S(1)}, u32[]{:S(2)}, u32[]{:S(2)}) collective-permute-start(bf16[96,512]{1,0:T(8,128)(2,1)S(1)} %collective-permute-done.13.refs_8_), channel_id=1, source_target_pairs={{8,0},{16,8},{24,16},{28,24},{20,28},{12,20},{4,12},{0,4},{9,1},{1... | collective-permute-start | bytes 294920 | tf_op jit(solution)/shard_map/ppermute | solution.py:551
  49.0 0.5 collective-permute-start.10
  49.5 0.7 %collective-permute-start.28 = (bf16[112,512]{1,0:T(8,128)(2,1)S(1)}, bf16[112,512]{1,0:T(8,128)(2,1)S(1)}, u32[]{:S(2)}, u32[]{:S(2)}) collective-permute-start(bf16[112,512]{1,0:T(8,128)(2,1)S(1)} %slice.18), channel_id=1, source_target_pairs={{0,8},{8,16},{16,24},{24,28},{28,20},{20,12},{12,4},{4,0},{1,9},{9... | collective-permute-start | bytes 344072 | tf_op jit(solution)/shard_map/ppermute | solution.py:548
  50.2 0.9 %collective-permute-done.19.refs_7_ = bf16[96,512]{1,0:T(8,128)(2,1)S(1)} collective-permute-done((bf16[96,512]{1,0:T(8,128)(2,1)S(1)}, bf16[96,512]{1,0:T(8,128)(2,1)S(1)}, u32[]{:S(2)}, u32[]{:S(2)}) %collective-permute-start.19) | collective-permute-done | bytes 98336 | tf_op jit(solution)/shard_map/ppermute | solution.py:548
  51.1 0.6 %collective-permute-start.21 = (bf16[96,512]{1,0:T(8,128)(2,1)S(1)}, bf16[96,512]{1,0:T(8,128)(2,1)S(1)}, u32[]{:S(2)}, u32[]{:S(2)}) collective-permute-start(bf16[96,512]{1,0:T(8,128)(2,1)S(1)} %collective-permute-done.19.refs_7_), channel_id=1, source_target_pairs={{0,8},{8,16},{16,24},{24,28},{28,20},{20,12},{12,4},{4,0},{1,9},{9... | collective-permute-start | bytes 294920 | tf_op jit(solution)/shard_map/ppermute | solution.py:548
  51.8 1.5 %collective-permute-start.20 = (bf16[96,512]{1,0:T(8,128)(2,1)S(1)}, bf16[96,512]{1,0:T(8,128)(2,1)S(1)}, u32[]{:S(2)}, u32[]{:S(2)}) collective-permute-start(bf16[96,512]{1,0:T(8,128)(2,1)S(1)} %collective-permute-done.18.refs_6_), channel_id=1, source_target_pairs={{8,0},{16,8},{24,16},{28,24},{20,28},{12,20},{4,12},{0,4},{9,1},{1... | collective-permute-start | bytes 294920 | tf_op jit(solution)/shard_map/ppermute | solution.py:551
  53.3 1.5 %collective-permute-start.15 = (bf16[96,512]{1,0:T(8,128)(2,1)S(1)}, bf16[96,512]{1,0:T(8,128)(2,1)S(1)}, u32[]{:S(2)}, u32[]{:S(2)}) collective-permute-start(bf16[96,512]{1,0:T(8,128)(2,1)S(1)} %collective-permute-done.14.refs_12_), channel_id=1, source_target_pairs={{8,0},{16,8},{24,16},{28,24},{20,28},{12,20},{4,12},{0,4},{9,1},{1... | collective-permute-start | bytes 294920 | tf_op jit(solution)/shard_map/ppermute | solution.py:551
  54.8 0.5 collective-permute-start.11
  55.3 1.8 %unpack_roots.1 = (bf16[1536,512]{1,0:T(8,128)(2,1)S(1)}, bf16[1536,512]{1,0:T(8,128)(2,1)S(1)}) custom-call(s32[1]{0:T(128)} %bitcast.me_ref, s32[1,8]{1,0:T(1,128)S(1)} %bitcast.3, bf16[224,512]{1,0:T(8,128)(2,1)S(1)} %pack_roots.1.refs_0_, bf16[224,512]{1,0:T(8,128)(2,1)S(1)} %collective-permute-done.22.refs_1_, ...), custom_call_target="tpu_custom_call" | custom-call | tf_op jit(solution)/shard_map/unpack_roots/pallas_call | solution.py:351
  57.2 2.1 %begin.1 = (bf16[1536,512]{1,0:T(8,128)(2,1)S(1)}, bf16[1536,512]{1,0:T(8,128)(2,1)S(1)}, f32[3,512,512]{2,1,0:T(8,128)S(1)}) custom-call(s32[1]{0:T(128)} %bitcast.me_ref, bf16[192,512]{1,0:T(8,128)(2,1)S(1)} %add_own.1.refs_0_, bf16[96,512]{1,0:T(8,128)(2,1)S(1)} %collective-permute-done.8.refs_1_, bf16[96,512]{1,0:T(8,128)(2,1)S(1)} %collective-permute-done.16.refs_2_, ...), custom_call_target="tpu_custom_call" | custom-call | tf_op jit(solution)/shard_map/begin/pallas_call | solution.py:386
  59.3 0.2 collective-permute-done.11.refs_0_
  59.4 2.3 %finish.1 = (bf16[1536,512]{1,0:T(8,128)(2,1)}, f32[192,512]{1,0:T(8,128)}, f32[192,512]{1,0:T(8,128)}) custom-call(s32[1]{0:T(128)} %bitcast.me_ref, s32[1,8]{1,0:T(1,128)S(1)} %bitcast.4, bf16[96,512]{1,0:T(8,128)(2,1)S(1)} %collective-permute-done.11.refs_0_, bf16[96,512]{1,0:T(8,128)(2,1)S(1)} %collective-permute-done.15.refs_1_, ...), custom_call_target="tpu_custom_call" | custom-call | tf_op jit(solution)/shard_map/finish/pallas_call | solution.py:500
  (41 shorter events, 0.4 us)
Async XLA Ops:
  0.6 1.4 %copy-start = (bf16[1,1536,512]{2,1,0:T(8,128)(2,1)S(1)}, bf16[1,1536,512]{2,1,0:T(8,128)(2,1)}, u32[]{:S(2)}) copy-start(bf16[1,1536,512]{2,1,0:T(8,128)(2,1)} %own_ref.13) | copy-start | bytes 4718596
  2.1 5.9 %collective-permute-start.4 = (bf16[96,512]{1,0:T(8,128)(2,1)S(1)}, bf16[96,512]{1,0:T(8,128)(2,1)S(1)}, u32[]{:S(2)}, u32[]{:S(2)}) collective-permute-start(bf16[96,512]{1,0:T(8,128)(2,1)S(1)} %get-tuple-element.11), channel_id=1, source_target_pairs={{8,0},{16,8},{24,16},{28,24},{20,28},{12,20},{4,12},{0,4},{9,1},{1... | collective-permute-start | bytes 294920 | tf_op jit(solution)/shard_map/ppermute | solution.py:551
  5.1 5.1 %copy-start.4 = (bf16[192,512]{1,0:T(8,128)(2,1)S(1)}, bf16[192,512]{1,0:T(8,128)(2,1)}, u32[]{:S(2)}) copy-start(bf16[192,512]{1,0:T(8,128)(2,1)} %l_ref.1) | copy-start | bytes 589828
  5.1 5.1 %copy-start.5 = (bf16[192,512]{1,0:T(8,128)(2,1)S(1)}, bf16[192,512]{1,0:T(8,128)(2,1)}, u32[]{:S(2)}) copy-start(bf16[192,512]{1,0:T(8,128)(2,1)} %r_ref.1) | copy-start | bytes 589828
  5.1 5.1 %copy-start.6 = (s32[8]{0:T(128)S(1)}, s32[8]{0:T(128)}, u32[]{:S(2)}) copy-start(s32[8]{0:T(128)} %param.7) | copy-start | bytes 100
  5.1 4.7 %collective-permute-start = (bf16[96,512]{1,0:T(8,128)(2,1)S(1)}, bf16[96,512]{1,0:T(8,128)(2,1)S(1)}, u32[]{:S(2)}, u32[]{:S(2)}) collective-permute-start(bf16[96,512]{1,0:T(8,128)(2,1)S(1)} %get-tuple-element.10), channel_id=1, source_target_pairs={{0,8},{8,16},{16,24},{24,28},{28,20},{20,12},{12,4},{4,0},{1,9},{9... | collective-permute-start | bytes 294920 | tf_op jit(solution)/shard_map/ppermute | solution.py:548
  8.0 7.9 %copy-start.1 = (bf16[1,1536,512]{2,1,0:T(8,128)(2,1)S(1)}, bf16[1,1536,512]{2,1,0:T(8,128)(2,1)}, u32[]{:S(2)}) copy-start(bf16[1,1536,512]{2,1,0:T(8,128)(2,1)} %own_ref.13) | copy-start | bytes 4718596
  8.0 7.9 %collective-permute-start.5 = (bf16[192,512]{1,0:T(8,128)(2,1)S(1)}, bf16[192,512]{1,0:T(8,128)(2,1)S(1)}, u32[]{:S(2)}, u32[]{:S(2)}) collective-permute-start(bf16[192,512]{1,0:T(8,128)(2,1)S(1)} %add_send.9), channel_id=1, source_target_pairs={{8,0},{16,8},{24,16},{28,24},{20,28},{12,20},{4,12},{0,4},{9,1},{1... | collective-permute-start | bytes 589832 | tf_op jit(solution)/shard_map/ppermute | solution.py:551
  9.8 7.9 %collective-permute-start.1 = (bf16[192,512]{1,0:T(8,128)(2,1)S(1)}, bf16[192,512]{1,0:T(8,128)(2,1)S(1)}, u32[]{:S(2)}, u32[]{:S(2)}) collective-permute-start(bf16[192,512]{1,0:T(8,128)(2,1)S(1)} %add_send.6), channel_id=1, source_target_pairs={{0,8},{8,16},{16,24},{24,28},{28,20},{20,12},{12,4},{4,0},{1,9},{9... | collective-permute-start | bytes 589832 | tf_op jit(solution)/shard_map/ppermute | solution.py:548
  10.4 10.4 %collective-permute-start.23 = (bf16[224,512]{1,0:T(8,128)(2,1)S(1)}, bf16[224,512]{1,0:T(8,128)(2,1)S(1)}, u32[]{:S(2)}, u32[]{:S(2)}) collective-permute-start(bf16[224,512]{1,0:T(8,128)(2,1)S(1)} %pack_roots.1.refs_0_), channel_id=1, source_target_pairs={{8,0},{16,8},{24,16},{28,24},{20,28},{12,20},{4,12},{0,4},{9,1},{1... | collective-permute-start | bytes 688136 | tf_op jit(solution)/shard_map/ppermute | solution.py:551
  12.3 10.3 %collective-permute-start.22 = (bf16[224,512]{1,0:T(8,128)(2,1)S(1)}, bf16[224,512]{1,0:T(8,128)(2,1)S(1)}, u32[]{:S(2)}, u32[]{:S(2)}) collective-permute-start(bf16[224,512]{1,0:T(8,128)(2,1)S(1)} %pack_roots.1.refs_0_), channel_id=1, source_target_pairs={{0,8},{8,16},{16,24},{24,28},{28,20},{20,12},{12,4},{4,0},{1,9},{9... | collective-permute-start | bytes 688136 | tf_op jit(solution)/shard_map/ppermute | solution.py:548
  15.9 9.1 %collective-permute-start.6 = (bf16[192,512]{1,0:T(8,128)(2,1)S(1)}, bf16[192,512]{1,0:T(8,128)(2,1)S(1)}, u32[]{:S(2)}, u32[]{:S(2)}) collective-permute-start(bf16[192,512]{1,0:T(8,128)(2,1)S(1)} %add_send.10), channel_id=1, source_target_pairs={{8,0},{16,8},{24,16},{28,24},{20,28},{12,20},{4,12},{0,4},{9,1},{1... | collective-permute-start | bytes 589832 | tf_op jit(solution)/shard_map/ppermute | solution.py:551
  17.8 9.1 %collective-permute-start.2 = (bf16[192,512]{1,0:T(8,128)(2,1)S(1)}, bf16[192,512]{1,0:T(8,128)(2,1)S(1)}, u32[]{:S(2)}, u32[]{:S(2)}) collective-permute-start(bf16[192,512]{1,0:T(8,128)(2,1)S(1)} %add_send.7), channel_id=1, source_target_pairs={{0,8},{8,16},{16,24},{24,28},{28,20},{20,12},{12,4},{4,0},{1,9},{9... | collective-permute-start | bytes 589832 | tf_op jit(solution)/shard_map/ppermute | solution.py:548
  20.8 9.1 %collective-permute-start.25 = (bf16[224,512]{1,0:T(8,128)(2,1)S(1)}, bf16[224,512]{1,0:T(8,128)(2,1)S(1)}, u32[]{:S(2)}, u32[]{:S(2)}) collective-permute-start(bf16[224,512]{1,0:T(8,128)(2,1)S(1)} %collective-permute-done.23.refs_2_), channel_id=1, source_target_pairs={{8,0},{16,8},{24,16},{28,24},{20,28},{12,20},{4,12},{0,4},{9,1},{1... | collective-permute-start | bytes 688136 | tf_op jit(solution)/shard_map/ppermute | solution.py:551
  22.6 9.1 %collective-permute-start.24 = (bf16[224,512]{1,0:T(8,128)(2,1)S(1)}, bf16[224,512]{1,0:T(8,128)(2,1)S(1)}, u32[]{:S(2)}, u32[]{:S(2)}) collective-permute-start(bf16[224,512]{1,0:T(8,128)(2,1)S(1)} %collective-permute-done.22.refs_1_), channel_id=1, source_target_pairs={{0,8},{8,16},{16,24},{24,28},{28,20},{20,12},{12,4},{4,0},{1,9},{9... | collective-permute-start | bytes 688136 | tf_op jit(solution)/shard_map/ppermute | solution.py:548
  25.1 9.1 %collective-permute-start.7 = (bf16[192,512]{1,0:T(8,128)(2,1)S(1)}, bf16[192,512]{1,0:T(8,128)(2,1)S(1)}, u32[]{:S(2)}, u32[]{:S(2)}) collective-permute-start(bf16[192,512]{1,0:T(8,128)(2,1)S(1)} %add_send.11), channel_id=1, source_target_pairs={{8,0},{16,8},{24,16},{28,24},{20,28},{12,20},{4,12},{0,4},{9,1},{1... | collective-permute-start | bytes 589832 | tf_op jit(solution)/shard_map/ppermute | solution.py:551
  26.9 9.0 %collective-permute-start.3 = (bf16[192,512]{1,0:T(8,128)(2,1)S(1)}, bf16[192,512]{1,0:T(8,128)(2,1)S(1)}, u32[]{:S(2)}, u32[]{:S(2)}) collective-permute-start(bf16[192,512]{1,0:T(8,128)(2,1)S(1)} %add_send.8), channel_id=1, source_target_pairs={{0,8},{8,16},{16,24},{24,28},{28,20},{20,12},{12,4},{4,0},{1,9},{9... | collective-permute-start | bytes 589832 | tf_op jit(solution)/shard_map/ppermute | solution.py:548
  29.9 8.5 %collective-permute-start.27 = (bf16[224,512]{1,0:T(8,128)(2,1)S(1)}, bf16[224,512]{1,0:T(8,128)(2,1)S(1)}, u32[]{:S(2)}, u32[]{:S(2)}) collective-permute-start(bf16[224,512]{1,0:T(8,128)(2,1)S(1)} %collective-permute-done.25.refs_4_), channel_id=1, source_target_pairs={{8,0},{16,8},{24,16},{28,24},{20,28},{12,20},{4,12},{0,4},{9,1},{1... | collective-permute-start | bytes 688136 | tf_op jit(solution)/shard_map/ppermute | solution.py:551
  31.7 11.8 %collective-permute-start.26 = (bf16[224,512]{1,0:T(8,128)(2,1)S(1)}, bf16[224,512]{1,0:T(8,128)(2,1)S(1)}, u32[]{:S(2)}, u32[]{:S(2)}) collective-permute-start(bf16[224,512]{1,0:T(8,128)(2,1)S(1)} %collective-permute-done.24.refs_3_), channel_id=1, source_target_pairs={{0,8},{8,16},{16,24},{24,28},{28,20},{20,12},{12,4},{4,0},{1,9},{9... | collective-permute-start | bytes 688136 | tf_op jit(solution)/shard_map/ppermute | solution.py:548
  36.1 5.1 %collective-permute-start.12 = (bf16[96,512]{1,0:T(8,128)(2,1)S(1)}, bf16[96,512]{1,0:T(8,128)(2,1)S(1)}, u32[]{:S(2)}, u32[]{:S(2)}) collective-permute-start(bf16[96,512]{1,0:T(8,128)(2,1)S(1)} %get-tuple-element.17), channel_id=1, source_target_pairs={{8,0},{16,8},{24,16},{28,24},{20,28},{12,20},{4,12},{0,4},{9,1},{1... | collective-permute-start | bytes 294920 | tf_op jit(solution)/shard_map/ppermute | solution.py:551
  37.7 5.6 %collective-permute-start.8 = (bf16[96,512]{1,0:T(8,128)(2,1)S(1)}, bf16[96,512]{1,0:T(8,128)(2,1)S(1)}, u32[]{:S(2)}, u32[]{:S(2)}) collective-permute-start(bf16[96,512]{1,0:T(8,128)(2,1)S(1)} %get-tuple-element.18), channel_id=1, source_target_pairs={{0,8},{8,16},{16,24},{24,28},{28,20},{20,12},{12,4},{4,0},{1,9},{9... | collective-permute-start | bytes 294920 | tf_op jit(solution)/shard_map/ppermute | solution.py:548
  38.1 7.2 %collective-permute-start.17 = (bf16[96,512]{1,0:T(8,128)(2,1)S(1)}, bf16[96,512]{1,0:T(8,128)(2,1)S(1)}, u32[]{:S(2)}, u32[]{:S(2)}) collective-permute-start(bf16[96,512]{1,0:T(8,128)(2,1)S(1)} %get-tuple-element.17), channel_id=1, source_target_pairs={{0,8},{8,16},{16,24},{24,28},{28,20},{20,12},{12,4},{4,0},{1,9},{9... | collective-permute-start | bytes 294920 | tf_op jit(solution)/shard_map/ppermute | solution.py:548
  38.4 7.2 %collective-permute-start.16 = (bf16[96,512]{1,0:T(8,128)(2,1)S(1)}, bf16[96,512]{1,0:T(8,128)(2,1)S(1)}, u32[]{:S(2)}, u32[]{:S(2)}) collective-permute-start(bf16[96,512]{1,0:T(8,128)(2,1)S(1)} %get-tuple-element.18), channel_id=1, source_target_pairs={{8,0},{16,8},{24,16},{28,24},{20,28},{12,20},{4,12},{0,4},{9,1},{1... | collective-permute-start | bytes 294920 | tf_op jit(solution)/shard_map/ppermute | solution.py:551
  41.2 6.2 %collective-permute-start.13 = (bf16[96,512]{1,0:T(8,128)(2,1)S(1)}, bf16[96,512]{1,0:T(8,128)(2,1)S(1)}, u32[]{:S(2)}, u32[]{:S(2)}) collective-permute-start(bf16[96,512]{1,0:T(8,128)(2,1)S(1)} %collective-permute-done.12.refs_4_), channel_id=1, source_target_pairs={{8,0},{16,8},{24,16},{28,24},{20,28},{12,20},{4,12},{0,4},{9,1},{1... | collective-permute-start | bytes 294920 | tf_op jit(solution)/shard_map/ppermute | solution.py:551
  43.3 5.7 %collective-permute-start.9 = (bf16[96,512]{1,0:T(8,128)(2,1)S(1)}, bf16[96,512]{1,0:T(8,128)(2,1)S(1)}, u32[]{:S(2)}, u32[]{:S(2)}) collective-permute-start(bf16[96,512]{1,0:T(8,128)(2,1)S(1)} %collective-permute-done.8.refs_1_), channel_id=1, source_target_pairs={{0,8},{8,16},{16,24},{24,28},{28,20},{20,12},{12,4},{4,0},{1,9},{9... | collective-permute-start | bytes 294920 | tf_op jit(solution)/shard_map/ppermute | solution.py:548
  43.5 5.9 %collective-permute-start.29 = (bf16[112,512]{1,0:T(8,128)(2,1)S(1)}, bf16[112,512]{1,0:T(8,128)(2,1)S(1)}, u32[]{:S(2)}, u32[]{:S(2)}) collective-permute-start(bf16[112,512]{1,0:T(8,128)(2,1)S(1)} %slice.19), channel_id=1, source_target_pairs={{8,0},{16,8},{24,16},{28,24},{20,28},{12,20},{4,12},{0,4},{9,1},{1... | collective-permute-start | bytes 344072 | tf_op jit(solution)/shard_map/ppermute | solution.py:551
  45.4 5.7 %collective-permute-start.19 = (bf16[96,512]{1,0:T(8,128)(2,1)S(1)}, bf16[96,512]{1,0:T(8,128)(2,1)S(1)}, u32[]{:S(2)}, u32[]{:S(2)}) collective-permute-start(bf16[96,512]{1,0:T(8,128)(2,1)S(1)} %collective-permute-done.17.refs_3_), channel_id=1, source_target_pairs={{0,8},{8,16},{16,24},{24,28},{28,20},{20,12},{12,4},{4,0},{1,9},{9... | collective-permute-start | bytes 294920 | tf_op jit(solution)/shard_map/ppermute | solution.py:548
  45.6 6.1 %collective-permute-start.18 = (bf16[96,512]{1,0:T(8,128)(2,1)S(1)}, bf16[96,512]{1,0:T(8,128)(2,1)S(1)}, u32[]{:S(2)}, u32[]{:S(2)}) collective-permute-start(bf16[96,512]{1,0:T(8,128)(2,1)S(1)} %collective-permute-done.16.refs_2_), channel_id=1, source_target_pairs={{8,0},{16,8},{24,16},{28,24},{20,28},{12,20},{4,12},{0,4},{9,1},{1... | collective-permute-start | bytes 294920 | tf_op jit(solution)/shard_map/ppermute | solution.py:551
  47.4 5.9 %collective-permute-start.14 = (bf16[96,512]{1,0:T(8,128)(2,1)S(1)}, bf16[96,512]{1,0:T(8,128)(2,1)S(1)}, u32[]{:S(2)}, u32[]{:S(2)}) collective-permute-start(bf16[96,512]{1,0:T(8,128)(2,1)S(1)} %collective-permute-done.13.refs_8_), channel_id=1, source_target_pairs={{8,0},{16,8},{24,16},{28,24},{20,28},{12,20},{4,12},{0,4},{9,1},{1... | collective-permute-start | bytes 294920 | tf_op jit(solution)/shard_map/ppermute | solution.py:551
  49.0 5.8 %collective-permute-start.10 = (bf16[96,512]{1,0:T(8,128)(2,1)S(1)}, bf16[96,512]{1,0:T(8,128)(2,1)S(1)}, u32[]{:S(2)}, u32[]{:S(2)}) collective-permute-start(bf16[96,512]{1,0:T(8,128)(2,1)S(1)} %collective-permute-done.9.refs_5_), channel_id=1, source_target_pairs={{0,8},{8,16},{16,24},{24,28},{28,20},{20,12},{12,4},{4,0},{1,9},{9... | collective-permute-start | bytes 294920 | tf_op jit(solution)/shard_map/ppermute | solution.py:548
  49.5 5.9 %collective-permute-start.28 = (bf16[112,512]{1,0:T(8,128)(2,1)S(1)}, bf16[112,512]{1,0:T(8,128)(2,1)S(1)}, u32[]{:S(2)}, u32[]{:S(2)}) collective-permute-start(bf16[112,512]{1,0:T(8,128)(2,1)S(1)} %slice.18), channel_id=1, source_target_pairs={{0,8},{8,16},{16,24},{24,28},{28,20},{20,12},{12,4},{4,0},{1,9},{9... | collective-permute-start | bytes 344072 | tf_op jit(solution)/shard_map/ppermute | solution.py:548
  51.1 6.0 %collective-permute-start.21 = (bf16[96,512]{1,0:T(8,128)(2,1)S(1)}, bf16[96,512]{1,0:T(8,128)(2,1)S(1)}, u32[]{:S(2)}, u32[]{:S(2)}) collective-permute-start(bf16[96,512]{1,0:T(8,128)(2,1)S(1)} %collective-permute-done.19.refs_7_), channel_id=1, source_target_pairs={{0,8},{8,16},{16,24},{24,28},{28,20},{20,12},{12,4},{4,0},{1,9},{9... | collective-permute-start | bytes 294920 | tf_op jit(solution)/shard_map/ppermute | solution.py:548
  51.8 5.4 %collective-permute-start.20 = (bf16[96,512]{1,0:T(8,128)(2,1)S(1)}, bf16[96,512]{1,0:T(8,128)(2,1)S(1)}, u32[]{:S(2)}, u32[]{:S(2)}) collective-permute-start(bf16[96,512]{1,0:T(8,128)(2,1)S(1)} %collective-permute-done.18.refs_6_), channel_id=1, source_target_pairs={{8,0},{16,8},{24,16},{28,24},{20,28},{12,20},{4,12},{0,4},{9,1},{1... | collective-permute-start | bytes 294920 | tf_op jit(solution)/shard_map/ppermute | solution.py:551
  53.3 6.0 %collective-permute-start.15 = (bf16[96,512]{1,0:T(8,128)(2,1)S(1)}, bf16[96,512]{1,0:T(8,128)(2,1)S(1)}, u32[]{:S(2)}, u32[]{:S(2)}) collective-permute-start(bf16[96,512]{1,0:T(8,128)(2,1)S(1)} %collective-permute-done.14.refs_12_), channel_id=1, source_target_pairs={{8,0},{16,8},{24,16},{28,24},{20,28},{12,20},{4,12},{0,4},{9,1},{1... | collective-permute-start | bytes 294920 | tf_op jit(solution)/shard_map/ppermute | solution.py:551
  54.8 4.6 %collective-permute-start.11 = (bf16[96,512]{1,0:T(8,128)(2,1)S(1)}, bf16[96,512]{1,0:T(8,128)(2,1)S(1)}, u32[]{:S(2)}, u32[]{:S(2)}) collective-permute-start(bf16[96,512]{1,0:T(8,128)(2,1)S(1)} %collective-permute-done.10.refs_9_), channel_id=1, source_target_pairs={{0,8},{8,16},{16,24},{24,28},{28,20},{20,12},{12,4},{4,0},{1,9},{9... | collective-permute-start | bytes 294920 | tf_op jit(solution)/shard_map/ppermute | solution.py:548
  57.1 2.3 %copy-start.2 = (f32[192,512]{1,0:T(8,128)S(1)}, f32[192,512]{1,0:T(8,128)}, u32[]{:S(2)}) copy-start(f32[192,512]{1,0:T(8,128)} %refs_7_.1) | copy-start | bytes 1179652
  57.2 2.3 %copy-start.3 = (f32[192,512]{1,0:T(8,128)S(1)}, f32[192,512]{1,0:T(8,128)}, u32[]{:S(2)}) copy-start(f32[192,512]{1,0:T(8,128)} %refs_8_.1) | copy-start | bytes 1179652

commit v6 on v5

--- a/solution.py
+++ b/solution.py
@@ -370,23 +370,32 @@
 
     def kernel(me_ref, *refs):
         parts, refs = refs[: len(pieces)], refs[len(pieces) :]
-        lroot, rroot, dir_ref, grad, rest_ref = refs
+        lroot, rroot, dir_ref, last_ref, grad, rest_ref, done, sems = refs
         for (offset, first, _), ref in zip(pieces, parts):
             place = away(me_ref[0], offset, n) * band + first
             grad[pl.ds(pl.multiple_of(place, CHUNK), ref.shape[0]), :] = ref[...]
         start = away(me_ref[0], n // 2, n) * band
         grad[pl.ds(pl.multiple_of(start, CHUNK), band), :] = jnp.zeros((band, breadth), BF16)
+        copies = []
         for b in range(nblocks):
             rows = slice(b * breadth, (b + 1) * breadth)
             mixed = jnp.dot(grad[rows], rroot[rows], preferred_element_type=F32).astype(BF16)
             block = jnp.dot(lroot[rows], mixed, preferred_element_type=F32)
-            dir_ref[rows] = block.astype(BF16)
+            if b == nblocks - 1:
+                last_ref[...] = block.astype(BF16)
+            else:
+                done[rows] = block.astype(BF16)
+                copies.append(pltpu.make_async_copy(done.at[rows], dir_ref.at[rows], sems.at[b]))
+                copies[-1].start()
             rest_ref[b] = block
+        for copy in copies:
+            copy.wait()
 
     return pl.pallas_call(
         kernel,
         out_shape=(
             jax.ShapeDtypeStruct((stacked, breadth), BF16),
+            jax.ShapeDtypeStruct((breadth, breadth), BF16),
             jax.ShapeDtypeStruct((stacked, breadth), BF16),
             jax.ShapeDtypeStruct((nblocks, breadth, breadth), F32),
         ),
@@ -395,24 +404,29 @@
             grid=(1,),
             in_specs=[whole(*x.shape) for _, _, x in pieces] + [whole(stacked, breadth)] * 2,
             out_specs=(
-                whole(stacked, breadth),
+                pl.BlockSpec(memory_space=pl.ANY),
+                whole(breadth, breadth),
                 whole(stacked, breadth),
                 whole(nblocks, breadth, breadth),
             ),
+            scratch_shapes=[
+                pltpu.VMEM((stacked, breadth), BF16),
+                pltpu.SemaphoreType.DMA((nblocks,)),
+            ],
         ),
         compiler_params=params(),
         name="begin",
     )(me, *[x for _, _, x in pieces], left_root, right_root)
 
 
-def finish(me, owner, pieces, directions, grad, rest, left_root, right_root, left_factor, right_factor, n):
+def finish(me, owner, pieces, directions, last, grad, rest, left_root, right_root, left_factor, right_factor, n):
     stacked, breadth = left_root.shape
     band = stacked // n
     nblocks = stacked // breadth
 
     def kernel(me_ref, owner_ref, *refs):
         parts, refs = refs[: len(pieces)], refs[len(pieces) :]
-        part_ref, grad_ref, rest_ref, lroot, rroot, lfac, rfac, *refs = refs
+        _, final_ref, grad_ref, rest_ref, lroot, rroot, lfac, rfac, *refs = refs
         dir_ref, lout_ref, rout_ref, late, block, lout, rout, sems = refs
         far = away(me_ref[0], n // 2, n) * band
         for (_, first, _), ref in zip(pieces, parts):
@@ -429,15 +443,12 @@
         def copy(slot, number):
             return pltpu.make_async_copy(block.at[slot], dir_ref.at[span(number)], sems.at[slot])
 
-        def keep(b):
-            rows = slice(b * breadth, (b + 1) * breadth)
-            return pltpu.make_async_copy(part_ref.at[rows], dir_ref.at[rows], sems.at[4 + b])
-
-        for b in range(nblocks):
-
-            @pl.when((first_block != b) & (last_block != b))
-            def _():
-                keep(b).start()
+        bottom = pl.ds((nblocks - 1) * breadth, breadth)
+        keep = pltpu.make_async_copy(final_ref, dir_ref.at[bottom], sems.at[4])
+
+        @pl.when(last_block != nblocks - 1)
+        def _():
+            keep.start()
 
         def complete(slot, number):
             some = jnp.where(row == number, late[...].astype(F32), 0.0).astype(BF16)
@@ -487,11 +498,9 @@
         def _():
             copy(1, last_block).wait()
 
-        for b in range(nblocks):
-
-            @pl.when((first_block != b) & (last_block != b))
-            def _():
-                keep(b).wait()
+        @pl.when(last_block != nblocks - 1)
+        def _():
+            keep.wait()
 
         for out in outs:
             out.wait()
@@ -505,7 +514,7 @@
             grid=(1,),
             in_specs=[whole(1, n)]
             + [whole(*x.shape) for _, _, x in pieces]
-            + [whole(stacked, breadth)] * 2
+            + [pl.BlockSpec(memory_space=pl.ANY), whole(breadth, breadth), whole(stacked, breadth)]
             + [whole(nblocks, breadth, breadth)]
             + [whole(stacked, breadth)] * 2
             + [whole(band, breadth)] * 2,
@@ -515,9 +524,10 @@
                 pltpu.VMEM((2, breadth, breadth), BF16),
                 pltpu.VMEM((band, breadth), F32),
                 pltpu.VMEM((band, breadth), F32),
-                pltpu.SemaphoreType.DMA((4 + nblocks,)),
+                pltpu.SemaphoreType.DMA((5,)),
             ],
         ),
+        input_output_aliases={2 + len(pieces): 0},
         compiler_params=params(),
         name="finish",
     )(
@@ -525,6 +535,7 @@
         owner,
         *[x for _, _, x in pieces],
         directions,
+        last,
         grad,
         rest,
         left_root,

time: 62 us -> 61.7 us (level)
  transfers between devices with their start and end apart: 30 -> 30, of which waited for: 12 -> 11; matrix products, arithmetic and copies ran while one was open for 0% -> 0% of each run, Pallas kernels for 7% -> 8%
where the time goes in v6:
time: 61.7 us; the launch traced here: 61.6 us
  starting transfers between devices  32.9 us (53%)
  waiting for transfers between devices  19.5 us (32%)
  Pallas kernels  6.84 us (11%)
  local copies, waits for them, and re-layouts  1.47 us (2%)
  between operations  0.84 us (1%)
    ppermute x15, starting transfers between devices, send_left(): return lax.ppermute(x, 'dp', backward)  27.3 us
    ppermute x15, waiting for transfers between devices, send_left(): return lax.ppermute(x, 'dp', backward)  16.5 us
    ppermute x15, starting transfers between devices, send_right(): return lax.ppermute(x, 'dp', onward)  5.65 us
    ppermute x15, waiting for transfers between devices, send_right(): return lax.ppermute(x, 'dp', onward)  2.99 us
    pallas_call x1, Pallas kernels, begin(): pl.pallas_call(kernel, out_shape=(jax.ShapeDtypeStruct((stacked, breadth)...  2.31 us
    pallas_call x1, Pallas kernels, finish(): pl.pallas_call(kernel, out_shape=(jax.ShapeDtypeStruct((stacked, breadth)...  2.03 us
    pallas_call x1, Pallas kernels, unpack_roots(): pl.pallas_call(kernel, out_shape=(out, out), grid_spec=pltpu.PrefetchScal...  1.78 us
    unnamed x14, local copies, waits for them, and re-layouts  1.43 us
  transfers between devices with their start and end apart: 30, of which 11 were waited for; matrix products, arithmetic and copies ran while one was open for 0% of the time, Pallas kernels for 8%

profile of v6, /device:TPU:0, one launch (start us, length us, event | category | flops | bytes accessed | tf_op | source)
XLA Modules:
  0.0 61.6 jit_solution(3679325346432168124)
XLA Ops:
  0.6 1.4 %copy-done = bf16[1,1536,512]{2,1,0:T(8,128)(2,1)S(1)} copy-done((bf16[1,1536,512]{2,1,0:T(8,128)(2,1)S(1)}, bf16[1,1536,512]{2,1,0:T(8,128)(2,1)}, u32[]{:S(2)}) %copy-start) | copy-done | bytes 1572888
  2.1 3.0 %collective-permute-start.4 = (bf16[96,512]{1,0:T(8,128)(2,1)S(1)}, bf16[96,512]{1,0:T(8,128)(2,1)S(1)}, u32[]{:S(2)}, u32[]{:S(2)}) collective-permute-start(bf16[96,512]{1,0:T(8,128)(2,1)S(1)} %get-tuple-element.12), channel_id=1, source_target_pairs={{8,0},{16,8},{24,16},{28,24},{20,28},{12,20},{4,12},{0,4},{9,1},{1... | collective-permute-start | bytes 294920 | tf_op jit(solution)/shard_map/ppermute | solution.py:562
  5.1 0.2 collective-permute-start
  5.2 2.7 %collective-permute-done.4.a_ref = bf16[96,512]{1,0:T(8,128)(2,1)S(1)} collective-permute-done((bf16[96,512]{1,0:T(8,128)(2,1)S(1)}, bf16[96,512]{1,0:T(8,128)(2,1)S(1)}, u32[]{:S(2)}, u32[]{:S(2)}) %collective-permute-start.4) | collective-permute-done | bytes 98336 | tf_op jit(solution)/shard_map/ppermute | solution.py:562
  8.0 1.8 %collective-permute-start.5 = (bf16[192,512]{1,0:T(8,128)(2,1)S(1)}, bf16[192,512]{1,0:T(8,128)(2,1)S(1)}, u32[]{:S(2)}, u32[]{:S(2)}) collective-permute-start(bf16[192,512]{1,0:T(8,128)(2,1)S(1)} %add_send.9), channel_id=1, source_target_pairs={{8,0},{16,8},{24,16},{28,24},{20,28},{12,20},{4,12},{0,4},{9,1},{1... | collective-permute-start | bytes 589832 | tf_op jit(solution)/shard_map/ppermute | solution.py:562
  9.8 0.3 collective-permute-start.1
  10.2 0.3 pack_roots.1.refs_0_
  10.5 1.7 %collective-permute-start.23 = (bf16[224,512]{1,0:T(8,128)(2,1)S(1)}, bf16[224,512]{1,0:T(8,128)(2,1)S(1)}, u32[]{:S(2)}, u32[]{:S(2)}) collective-permute-start(bf16[224,512]{1,0:T(8,128)(2,1)S(1)} %pack_roots.1.refs_0_), channel_id=1, source_target_pairs={{8,0},{16,8},{24,16},{28,24},{20,28},{12,20},{4,12},{0,4},{9,1},{1... | collective-permute-start | bytes 688136 | tf_op jit(solution)/shard_map/ppermute | solution.py:562
  12.2 0.4 collective-permute-start.22
  12.6 3.3 %collective-permute-done.5.a_ref = bf16[192,512]{1,0:T(8,128)(2,1)S(1)} collective-permute-done((bf16[192,512]{1,0:T(8,128)(2,1)S(1)}, bf16[192,512]{1,0:T(8,128)(2,1)S(1)}, u32[]{:S(2)}, u32[]{:S(2)}) %collective-permute-start.5) | collective-permute-done | bytes 196640 | tf_op jit(solution)/shard_map/ppermute | solution.py:562
  15.9 1.8 %collective-permute-start.6 = (bf16[192,512]{1,0:T(8,128)(2,1)S(1)}, bf16[192,512]{1,0:T(8,128)(2,1)S(1)}, u32[]{:S(2)}, u32[]{:S(2)}) collective-permute-start(bf16[192,512]{1,0:T(8,128)(2,1)S(1)} %add_send.10), channel_id=1, source_target_pairs={{8,0},{16,8},{24,16},{28,24},{20,28},{12,20},{4,12},{0,4},{9,1},{1... | collective-permute-start | bytes 589832 | tf_op jit(solution)/shard_map/ppermute | solution.py:562
  17.7 0.1 add_send.7
  17.8 0.3 collective-permute-start.2
  18.1 2.7 %collective-permute-done.23.refs_2_ = bf16[224,512]{1,0:T(8,128)(2,1)S(1)} collective-permute-done((bf16[224,512]{1,0:T(8,128)(2,1)S(1)}, bf16[224,512]{1,0:T(8,128)(2,1)S(1)}, u32[]{:S(2)}, u32[]{:S(2)}) %collective-permute-start.23) | collective-permute-done | bytes 229408 | tf_op jit(solution)/shard_map/ppermute | solution.py:562
  20.8 1.7 %collective-permute-start.25 = (bf16[224,512]{1,0:T(8,128)(2,1)S(1)}, bf16[224,512]{1,0:T(8,128)(2,1)S(1)}, u32[]{:S(2)}, u32[]{:S(2)}) collective-permute-start(bf16[224,512]{1,0:T(8,128)(2,1)S(1)} %collective-permute-done.23.refs_2_), channel_id=1, source_target_pairs={{8,0},{16,8},{24,16},{28,24},{20,28},{12,20},{4,12},{0,4},{9,1},{1... | collective-permute-start | bytes 688136 | tf_op jit(solution)/shard_map/ppermute | solution.py:562
  22.5 0.1 collective-permute-done.22.refs_1_
  22.6 0.3 collective-permute-start.24
  22.9 2.1 %collective-permute-done.6.a_ref = bf16[192,512]{1,0:T(8,128)(2,1)S(1)} collective-permute-done((bf16[192,512]{1,0:T(8,128)(2,1)S(1)}, bf16[192,512]{1,0:T(8,128)(2,1)S(1)}, u32[]{:S(2)}, u32[]{:S(2)}) %collective-permute-start.6) | collective-permute-done | bytes 196640 | tf_op jit(solution)/shard_map/ppermute | solution.py:562
  25.1 1.8 %collective-permute-start.7 = (bf16[192,512]{1,0:T(8,128)(2,1)S(1)}, bf16[192,512]{1,0:T(8,128)(2,1)S(1)}, u32[]{:S(2)}, u32[]{:S(2)}) collective-permute-start(bf16[192,512]{1,0:T(8,128)(2,1)S(1)} %add_send.11), channel_id=1, source_target_pairs={{8,0},{16,8},{24,16},{28,24},{20,28},{12,20},{4,12},{0,4},{9,1},{1... | collective-permute-start | bytes 589832 | tf_op jit(solution)/shard_map/ppermute | solution.py:562
  26.9 0.3 collective-permute-start.3
  27.3 2.7 %collective-permute-done.25.refs_4_ = bf16[224,512]{1,0:T(8,128)(2,1)S(1)} collective-permute-done((bf16[224,512]{1,0:T(8,128)(2,1)S(1)}, bf16[224,512]{1,0:T(8,128)(2,1)S(1)}, u32[]{:S(2)}, u32[]{:S(2)}) %collective-permute-start.25) | collective-permute-done | bytes 229408 | tf_op jit(solution)/shard_map/ppermute | solution.py:562
  29.9 1.7 %collective-permute-start.27 = (bf16[224,512]{1,0:T(8,128)(2,1)S(1)}, bf16[224,512]{1,0:T(8,128)(2,1)S(1)}, u32[]{:S(2)}, u32[]{:S(2)}) collective-permute-start(bf16[224,512]{1,0:T(8,128)(2,1)S(1)} %collective-permute-done.25.refs_4_), channel_id=1, source_target_pairs={{8,0},{16,8},{24,16},{28,24},{20,28},{12,20},{4,12},{0,4},{9,1},{1... | collective-permute-start | bytes 688136 | tf_op jit(solution)/shard_map/ppermute | solution.py:562
  31.7 0.1 collective-permute-done.24.refs_3_
  31.7 0.3 collective-permute-start.26
  32.0 2.1 %collective-permute-done.7.l_ref = bf16[192,512]{1,0:T(8,128)(2,1)S(1)} collective-permute-done((bf16[192,512]{1,0:T(8,128)(2,1)S(1)}, bf16[192,512]{1,0:T(8,128)(2,1)S(1)}, u32[]{:S(2)}, u32[]{:S(2)}) %collective-permute-start.7) | collective-permute-done | bytes 196640 | tf_op jit(solution)/shard_map/ppermute | solution.py:562
  34.1 1.8 %collective-permute-done.3.r_ref = bf16[192,512]{1,0:T(8,128)(2,1)S(1)} collective-permute-done((bf16[192,512]{1,0:T(8,128)(2,1)S(1)}, bf16[192,512]{1,0:T(8,128)(2,1)S(1)}, u32[]{:S(2)}, u32[]{:S(2)}) %collective-permute-start.3) | collective-permute-done | bytes 196640 | tf_op jit(solution)/shard_map/ppermute | solution.py:559
  36.0 0.1 add_own.1.refs_0_
  36.1 1.6 %collective-permute-start.12 = (bf16[96,512]{1,0:T(8,128)(2,1)S(1)}, bf16[96,512]{1,0:T(8,128)(2,1)S(1)}, u32[]{:S(2)}, u32[]{:S(2)}) collective-permute-start(bf16[96,512]{1,0:T(8,128)(2,1)S(1)} %get-tuple-element.19), channel_id=1, source_target_pairs={{8,0},{16,8},{24,16},{28,24},{20,28},{12,20},{4,12},{0,4},{9,1},{1... | collective-permute-start | bytes 294920 | tf_op jit(solution)/shard_map/ppermute | solution.py:562
  37.7 0.4 collective-permute-start.8
  38.1 0.3 collective-permute-start.17
  38.4 1.7 %collective-permute-start.16 = (bf16[96,512]{1,0:T(8,128)(2,1)S(1)}, bf16[96,512]{1,0:T(8,128)(2,1)S(1)}, u32[]{:S(2)}, u32[]{:S(2)}) collective-permute-start(bf16[96,512]{1,0:T(8,128)(2,1)S(1)} %get-tuple-element.20), channel_id=1, source_target_pairs={{8,0},{16,8},{24,16},{28,24},{20,28},{12,20},{4,12},{0,4},{9,1},{1... | collective-permute-start | bytes 294920 | tf_op jit(solution)/shard_map/ppermute | solution.py:562
  40.2 1.0 %collective-permute-done.12.refs_4_ = bf16[96,512]{1,0:T(8,128)(2,1)S(1)} collective-permute-done((bf16[96,512]{1,0:T(8,128)(2,1)S(1)}, bf16[96,512]{1,0:T(8,128)(2,1)S(1)}, u32[]{:S(2)}, u32[]{:S(2)}) %collective-permute-start.12) | collective-permute-done | bytes 98336 | tf_op jit(solution)/shard_map/ppermute | solution.py:562
  41.2 2.1 %collective-permute-start.13 = (bf16[96,512]{1,0:T(8,128)(2,1)S(1)}, bf16[96,512]{1,0:T(8,128)(2,1)S(1)}, u32[]{:S(2)}, u32[]{:S(2)}) collective-permute-start(bf16[96,512]{1,0:T(8,128)(2,1)S(1)} %collective-permute-done.12.refs_4_), channel_id=1, source_target_pairs={{8,0},{16,8},{24,16},{28,24},{20,28},{12,20},{4,12},{0,4},{9,1},{1... | collective-permute-start | bytes 294920 | tf_op jit(solution)/shard_map/ppermute | solution.py:562
  43.3 0.2 collective-permute-start.9
  43.5 1.8 %collective-permute-start.29 = (bf16[112,512]{1,0:T(8,128)(2,1)S(1)}, bf16[112,512]{1,0:T(8,128)(2,1)S(1)}, u32[]{:S(2)}, u32[]{:S(2)}) collective-permute-start(bf16[112,512]{1,0:T(8,128)(2,1)S(1)} %slice.19), channel_id=1, source_target_pairs={{8,0},{16,8},{24,16},{28,24},{20,28},{12,20},{4,12},{0,4},{9,1},{1... | collective-permute-start | bytes 344072 | tf_op jit(solution)/shard_map/ppermute | solution.py:562
  45.4 0.2 collective-permute-start.19
  45.6 1.8 %collective-permute-start.18 = (bf16[96,512]{1,0:T(8,128)(2,1)S(1)}, bf16[96,512]{1,0:T(8,128)(2,1)S(1)}, u32[]{:S(2)}, u32[]{:S(2)}) collective-permute-start(bf16[96,512]{1,0:T(8,128)(2,1)S(1)} %collective-permute-done.16.refs_2_), channel_id=1, source_target_pairs={{8,0},{16,8},{24,16},{28,24},{20,28},{12,20},{4,12},{0,4},{9,1},{1... | collective-permute-start | bytes 294920 | tf_op jit(solution)/shard_map/ppermute | solution.py:562
  47.4 1.6 %collective-permute-start.14 = (bf16[96,512]{1,0:T(8,128)(2,1)S(1)}, bf16[96,512]{1,0:T(8,128)(2,1)S(1)}, u32[]{:S(2)}, u32[]{:S(2)}) collective-permute-start(bf16[96,512]{1,0:T(8,128)(2,1)S(1)} %collective-permute-done.13.refs_8_), channel_id=1, source_target_pairs={{8,0},{16,8},{24,16},{28,24},{20,28},{12,20},{4,12},{0,4},{9,1},{1... | collective-permute-start | bytes 294920 | tf_op jit(solution)/shard_map/ppermute | solution.py:562
  49.0 0.5 collective-permute-start.10
  49.5 0.7 %collective-permute-start.28 = (bf16[112,512]{1,0:T(8,128)(2,1)S(1)}, bf16[112,512]{1,0:T(8,128)(2,1)S(1)}, u32[]{:S(2)}, u32[]{:S(2)}) collective-permute-start(bf16[112,512]{1,0:T(8,128)(2,1)S(1)} %slice.18), channel_id=1, source_target_pairs={{0,8},{8,16},{16,24},{24,28},{28,20},{20,12},{12,4},{4,0},{1,9},{9... | collective-permute-start | bytes 344072 | tf_op jit(solution)/shard_map/ppermute | solution.py:559
  50.2 0.9 %collective-permute-done.19.refs_7_ = bf16[96,512]{1,0:T(8,128)(2,1)S(1)} collective-permute-done((bf16[96,512]{1,0:T(8,128)(2,1)S(1)}, bf16[96,512]{1,0:T(8,128)(2,1)S(1)}, u32[]{:S(2)}, u32[]{:S(2)}) %collective-permute-start.19) | collective-permute-done | bytes 98336 | tf_op jit(solution)/shard_map/ppermute | solution.py:559
  51.1 0.6 %collective-permute-start.21 = (bf16[96,512]{1,0:T(8,128)(2,1)S(1)}, bf16[96,512]{1,0:T(8,128)(2,1)S(1)}, u32[]{:S(2)}, u32[]{:S(2)}) collective-permute-start(bf16[96,512]{1,0:T(8,128)(2,1)S(1)} %collective-permute-done.19.refs_7_), channel_id=1, source_target_pairs={{0,8},{8,16},{16,24},{24,28},{28,20},{20,12},{12,4},{4,0},{1,9},{9... | collective-permute-start | bytes 294920 | tf_op jit(solution)/shard_map/ppermute | solution.py:559
  51.8 1.5 %collective-permute-start.20 = (bf16[96,512]{1,0:T(8,128)(2,1)S(1)}, bf16[96,512]{1,0:T(8,128)(2,1)S(1)}, u32[]{:S(2)}, u32[]{:S(2)}) collective-permute-start(bf16[96,512]{1,0:T(8,128)(2,1)S(1)} %collective-permute-done.18.refs_6_), channel_id=1, source_target_pairs={{8,0},{16,8},{24,16},{28,24},{20,28},{12,20},{4,12},{0,4},{9,1},{1... | collective-permute-start | bytes 294920 | tf_op jit(solution)/shard_map/ppermute | solution.py:562
  53.3 1.5 %collective-permute-start.15 = (bf16[96,512]{1,0:T(8,128)(2,1)S(1)}, bf16[96,512]{1,0:T(8,128)(2,1)S(1)}, u32[]{:S(2)}, u32[]{:S(2)}) collective-permute-start(bf16[96,512]{1,0:T(8,128)(2,1)S(1)} %collective-permute-done.14.refs_12_), channel_id=1, source_target_pairs={{8,0},{16,8},{24,16},{28,24},{20,28},{12,20},{4,12},{0,4},{9,1},{1... | collective-permute-start | bytes 294920 | tf_op jit(solution)/shard_map/ppermute | solution.py:562
  54.8 0.5 collective-permute-start.11
  55.3 1.8 %unpack_roots.1 = (bf16[1536,512]{1,0:T(8,128)(2,1)S(1)}, bf16[1536,512]{1,0:T(8,128)(2,1)S(1)}) custom-call(s32[1]{0:T(128)} %bitcast.me_ref, s32[1,8]{1,0:T(1,128)S(1)} %bitcast.3, bf16[224,512]{1,0:T(8,128)(2,1)S(1)} %pack_roots.1.refs_0_, bf16[224,512]{1,0:T(8,128)(2,1)S(1)} %collective-permute-done.22.refs_1_, ...), custom_call_target="tpu_custom_call" | custom-call | tf_op jit(solution)/shard_map/unpack_roots/pallas_call | solution.py:351
  57.2 2.3 %begin.1 = (bf16[1536,512]{1,0:T(8,128)(2,1)}, bf16[512,512]{1,0:T(8,128)(2,1)S(1)}, bf16[1536,512]{1,0:T(8,128)(2,1)S(1)}, f32[3,512,512]{2,1,0:T(8,128)S(1)}) custom-call(s32[1]{0:T(128)} %bitcast.me_ref, bf16[192,512]{1,0:T(8,128)(2,1)S(1)} %add_own.1.refs_0_, bf16[96,512]{1,0:T(8,128)(2,1)S(1)} %collective-permute-done.8.refs_1_, ...), custom_call_target="tpu_custom_call" | custom-call | tf_op jit(solution)/shard_map/begin/pallas_call | solution.py:394
  59.5 2.0 %finish.1 = (bf16[1536,512]{1,0:T(8,128)(2,1)}, f32[192,512]{1,0:T(8,128)}, f32[192,512]{1,0:T(8,128)}) custom-call(s32[1]{0:T(128)} %bitcast.me_ref, s32[1,8]{1,0:T(1,128)S(1)} %bitcast.4, bf16[96,512]{1,0:T(8,128)(2,1)S(1)} %collective-permute-done.11.refs_0_, ...), custom_call_target="tpu_custom_call", output_to_operand_aliasing={{0}: (4, {})} | custom-call | tf_op jit(solution)/shard_map/finish/pallas_call | solution.py:509
  (41 shorter events, 0.4 us)
Async XLA Ops:
  0.6 1.4 %copy-start = (bf16[1,1536,512]{2,1,0:T(8,128)(2,1)S(1)}, bf16[1,1536,512]{2,1,0:T(8,128)(2,1)}, u32[]{:S(2)}) copy-start(bf16[1,1536,512]{2,1,0:T(8,128)(2,1)} %own_ref.13) | copy-start | bytes 4718596
  2.1 5.9 %collective-permute-start.4 = (bf16[96,512]{1,0:T(8,128)(2,1)S(1)}, bf16[96,512]{1,0:T(8,128)(2,1)S(1)}, u32[]{:S(2)}, u32[]{:S(2)}) collective-permute-start(bf16[96,512]{1,0:T(8,128)(2,1)S(1)} %get-tuple-element.12), channel_id=1, source_target_pairs={{8,0},{16,8},{24,16},{28,24},{20,28},{12,20},{4,12},{0,4},{9,1},{1... | collective-permute-start | bytes 294920 | tf_op jit(solution)/shard_map/ppermute | solution.py:562
  5.1 5.1 %copy-start.4 = (bf16[192,512]{1,0:T(8,128)(2,1)S(1)}, bf16[192,512]{1,0:T(8,128)(2,1)}, u32[]{:S(2)}) copy-start(bf16[192,512]{1,0:T(8,128)(2,1)} %l_ref.1) | copy-start | bytes 589828
  5.1 5.1 %copy-start.5 = (bf16[192,512]{1,0:T(8,128)(2,1)S(1)}, bf16[192,512]{1,0:T(8,128)(2,1)}, u32[]{:S(2)}) copy-start(bf16[192,512]{1,0:T(8,128)(2,1)} %r_ref.1) | copy-start | bytes 589828
  5.1 5.1 %copy-start.6 = (s32[8]{0:T(128)S(1)}, s32[8]{0:T(128)}, u32[]{:S(2)}) copy-start(s32[8]{0:T(128)} %param.7) | copy-start | bytes 100
  5.1 4.7 %collective-permute-start = (bf16[96,512]{1,0:T(8,128)(2,1)S(1)}, bf16[96,512]{1,0:T(8,128)(2,1)S(1)}, u32[]{:S(2)}, u32[]{:S(2)}) collective-permute-start(bf16[96,512]{1,0:T(8,128)(2,1)S(1)} %get-tuple-element.11), channel_id=1, source_target_pairs={{0,8},{8,16},{16,24},{24,28},{28,20},{20,12},{12,4},{4,0},{1,9},{9... | collective-permute-start | bytes 294920 | tf_op jit(solution)/shard_map/ppermute | solution.py:559
  8.0 7.9 %copy-start.1 = (bf16[1,1536,512]{2,1,0:T(8,128)(2,1)S(1)}, bf16[1,1536,512]{2,1,0:T(8,128)(2,1)}, u32[]{:S(2)}) copy-start(bf16[1,1536,512]{2,1,0:T(8,128)(2,1)} %own_ref.13) | copy-start | bytes 4718596
  8.0 7.9 %collective-permute-start.5 = (bf16[192,512]{1,0:T(8,128)(2,1)S(1)}, bf16[192,512]{1,0:T(8,128)(2,1)S(1)}, u32[]{:S(2)}, u32[]{:S(2)}) collective-permute-start(bf16[192,512]{1,0:T(8,128)(2,1)S(1)} %add_send.9), channel_id=1, source_target_pairs={{8,0},{16,8},{24,16},{28,24},{20,28},{12,20},{4,12},{0,4},{9,1},{1... | collective-permute-start | bytes 589832 | tf_op jit(solution)/shard_map/ppermute | solution.py:562
  9.8 7.9 %collective-permute-start.1 = (bf16[192,512]{1,0:T(8,128)(2,1)S(1)}, bf16[192,512]{1,0:T(8,128)(2,1)S(1)}, u32[]{:S(2)}, u32[]{:S(2)}) collective-permute-start(bf16[192,512]{1,0:T(8,128)(2,1)S(1)} %add_send.6), channel_id=1, source_target_pairs={{0,8},{8,16},{16,24},{24,28},{28,20},{20,12},{12,4},{4,0},{1,9},{9... | collective-permute-start | bytes 589832 | tf_op jit(solution)/shard_map/ppermute | solution.py:559
  10.5 10.3 %collective-permute-start.23 = (bf16[224,512]{1,0:T(8,128)(2,1)S(1)}, bf16[224,512]{1,0:T(8,128)(2,1)S(1)}, u32[]{:S(2)}, u32[]{:S(2)}) collective-permute-start(bf16[224,512]{1,0:T(8,128)(2,1)S(1)} %pack_roots.1.refs_0_), channel_id=1, source_target_pairs={{8,0},{16,8},{24,16},{28,24},{20,28},{12,20},{4,12},{0,4},{9,1},{1... | collective-permute-start | bytes 688136 | tf_op jit(solution)/shard_map/ppermute | solution.py:562
  12.2 10.4 %collective-permute-start.22 = (bf16[224,512]{1,0:T(8,128)(2,1)S(1)}, bf16[224,512]{1,0:T(8,128)(2,1)S(1)}, u32[]{:S(2)}, u32[]{:S(2)}) collective-permute-start(bf16[224,512]{1,0:T(8,128)(2,1)S(1)} %pack_roots.1.refs_0_), channel_id=1, source_target_pairs={{0,8},{8,16},{16,24},{24,28},{28,20},{20,12},{12,4},{4,0},{1,9},{9... | collective-permute-start | bytes 688136 | tf_op jit(solution)/shard_map/ppermute | solution.py:559
  15.9 9.1 %collective-permute-start.6 = (bf16[192,512]{1,0:T(8,128)(2,1)S(1)}, bf16[192,512]{1,0:T(8,128)(2,1)S(1)}, u32[]{:S(2)}, u32[]{:S(2)}) collective-permute-start(bf16[192,512]{1,0:T(8,128)(2,1)S(1)} %add_send.10), channel_id=1, source_target_pairs={{8,0},{16,8},{24,16},{28,24},{20,28},{12,20},{4,12},{0,4},{9,1},{1... | collective-permute-start | bytes 589832 | tf_op jit(solution)/shard_map/ppermute | solution.py:562
  17.8 9.1 %collective-permute-start.2 = (bf16[192,512]{1,0:T(8,128)(2,1)S(1)}, bf16[192,512]{1,0:T(8,128)(2,1)S(1)}, u32[]{:S(2)}, u32[]{:S(2)}) collective-permute-start(bf16[192,512]{1,0:T(8,128)(2,1)S(1)} %add_send.7), channel_id=1, source_target_pairs={{0,8},{8,16},{16,24},{24,28},{28,20},{20,12},{12,4},{4,0},{1,9},{9... | collective-permute-start | bytes 589832 | tf_op jit(solution)/shard_map/ppermute | solution.py:559
  20.8 9.1 %collective-permute-start.25 = (bf16[224,512]{1,0:T(8,128)(2,1)S(1)}, bf16[224,512]{1,0:T(8,128)(2,1)S(1)}, u32[]{:S(2)}, u32[]{:S(2)}) collective-permute-start(bf16[224,512]{1,0:T(8,128)(2,1)S(1)} %collective-permute-done.23.refs_2_), channel_id=1, source_target_pairs={{8,0},{16,8},{24,16},{28,24},{20,28},{12,20},{4,12},{0,4},{9,1},{1... | collective-permute-start | bytes 688136 | tf_op jit(solution)/shard_map/ppermute | solution.py:562
  22.6 9.1 %collective-permute-start.24 = (bf16[224,512]{1,0:T(8,128)(2,1)S(1)}, bf16[224,512]{1,0:T(8,128)(2,1)S(1)}, u32[]{:S(2)}, u32[]{:S(2)}) collective-permute-start(bf16[224,512]{1,0:T(8,128)(2,1)S(1)} %collective-permute-done.22.refs_1_), channel_id=1, source_target_pairs={{0,8},{8,16},{16,24},{24,28},{28,20},{20,12},{12,4},{4,0},{1,9},{9... | collective-permute-start | bytes 688136 | tf_op jit(solution)/shard_map/ppermute | solution.py:559
  25.1 9.1 %collective-permute-start.7 = (bf16[192,512]{1,0:T(8,128)(2,1)S(1)}, bf16[192,512]{1,0:T(8,128)(2,1)S(1)}, u32[]{:S(2)}, u32[]{:S(2)}) collective-permute-start(bf16[192,512]{1,0:T(8,128)(2,1)S(1)} %add_send.11), channel_id=1, source_target_pairs={{8,0},{16,8},{24,16},{28,24},{20,28},{12,20},{4,12},{0,4},{9,1},{1... | collective-permute-start | bytes 589832 | tf_op jit(solution)/shard_map/ppermute | solution.py:562
  26.9 9.0 %collective-permute-start.3 = (bf16[192,512]{1,0:T(8,128)(2,1)S(1)}, bf16[192,512]{1,0:T(8,128)(2,1)S(1)}, u32[]{:S(2)}, u32[]{:S(2)}) collective-permute-start(bf16[192,512]{1,0:T(8,128)(2,1)S(1)} %add_send.8), channel_id=1, source_target_pairs={{0,8},{8,16},{16,24},{24,28},{28,20},{20,12},{12,4},{4,0},{1,9},{9... | collective-permute-start | bytes 589832 | tf_op jit(solution)/shard_map/ppermute | solution.py:559
  29.9 8.5 %collective-permute-start.27 = (bf16[224,512]{1,0:T(8,128)(2,1)S(1)}, bf16[224,512]{1,0:T(8,128)(2,1)S(1)}, u32[]{:S(2)}, u32[]{:S(2)}) collective-permute-start(bf16[224,512]{1,0:T(8,128)(2,1)S(1)} %collective-permute-done.25.refs_4_), channel_id=1, source_target_pairs={{8,0},{16,8},{24,16},{28,24},{20,28},{12,20},{4,12},{0,4},{9,1},{1... | collective-permute-start | bytes 688136 | tf_op jit(solution)/shard_map/ppermute | solution.py:562
  31.7 11.8 %collective-permute-start.26 = (bf16[224,512]{1,0:T(8,128)(2,1)S(1)}, bf16[224,512]{1,0:T(8,128)(2,1)S(1)}, u32[]{:S(2)}, u32[]{:S(2)}) collective-permute-start(bf16[224,512]{1,0:T(8,128)(2,1)S(1)} %collective-permute-done.24.refs_3_), channel_id=1, source_target_pairs={{0,8},{8,16},{16,24},{24,28},{28,20},{20,12},{12,4},{4,0},{1,9},{9... | collective-permute-start | bytes 688136 | tf_op jit(solution)/shard_map/ppermute | solution.py:559
  36.1 5.1 %collective-permute-start.12 = (bf16[96,512]{1,0:T(8,128)(2,1)S(1)}, bf16[96,512]{1,0:T(8,128)(2,1)S(1)}, u32[]{:S(2)}, u32[]{:S(2)}) collective-permute-start(bf16[96,512]{1,0:T(8,128)(2,1)S(1)} %get-tuple-element.19), channel_id=1, source_target_pairs={{8,0},{16,8},{24,16},{28,24},{20,28},{12,20},{4,12},{0,4},{9,1},{1... | collective-permute-start | bytes 294920 | tf_op jit(solution)/shard_map/ppermute | solution.py:562
  37.7 5.6 %collective-permute-start.8 = (bf16[96,512]{1,0:T(8,128)(2,1)S(1)}, bf16[96,512]{1,0:T(8,128)(2,1)S(1)}, u32[]{:S(2)}, u32[]{:S(2)}) collective-permute-start(bf16[96,512]{1,0:T(8,128)(2,1)S(1)} %get-tuple-element.20), channel_id=1, source_target_pairs={{0,8},{8,16},{16,24},{24,28},{28,20},{20,12},{12,4},{4,0},{1,9},{9... | collective-permute-start | bytes 294920 | tf_op jit(solution)/shard_map/ppermute | solution.py:559
  38.1 7.2 %collective-permute-start.17 = (bf16[96,512]{1,0:T(8,128)(2,1)S(1)}, bf16[96,512]{1,0:T(8,128)(2,1)S(1)}, u32[]{:S(2)}, u32[]{:S(2)}) collective-permute-start(bf16[96,512]{1,0:T(8,128)(2,1)S(1)} %get-tuple-element.19), channel_id=1, source_target_pairs={{0,8},{8,16},{16,24},{24,28},{28,20},{20,12},{12,4},{4,0},{1,9},{9... | collective-permute-start | bytes 294920 | tf_op jit(solution)/shard_map/ppermute | solution.py:559
  38.4 7.2 %collective-permute-start.16 = (bf16[96,512]{1,0:T(8,128)(2,1)S(1)}, bf16[96,512]{1,0:T(8,128)(2,1)S(1)}, u32[]{:S(2)}, u32[]{:S(2)}) collective-permute-start(bf16[96,512]{1,0:T(8,128)(2,1)S(1)} %get-tuple-element.20), channel_id=1, source_target_pairs={{8,0},{16,8},{24,16},{28,24},{20,28},{12,20},{4,12},{0,4},{9,1},{1... | collective-permute-start | bytes 294920 | tf_op jit(solution)/shard_map/ppermute | solution.py:562
  41.2 6.2 %collective-permute-start.13 = (bf16[96,512]{1,0:T(8,128)(2,1)S(1)}, bf16[96,512]{1,0:T(8,128)(2,1)S(1)}, u32[]{:S(2)}, u32[]{:S(2)}) collective-permute-start(bf16[96,512]{1,0:T(8,128)(2,1)S(1)} %collective-permute-done.12.refs_4_), channel_id=1, source_target_pairs={{8,0},{16,8},{24,16},{28,24},{20,28},{12,20},{4,12},{0,4},{9,1},{1... | collective-permute-start | bytes 294920 | tf_op jit(solution)/shard_map/ppermute | solution.py:562
  43.3 5.7 %collective-permute-start.9 = (bf16[96,512]{1,0:T(8,128)(2,1)S(1)}, bf16[96,512]{1,0:T(8,128)(2,1)S(1)}, u32[]{:S(2)}, u32[]{:S(2)}) collective-permute-start(bf16[96,512]{1,0:T(8,128)(2,1)S(1)} %collective-permute-done.8.refs_1_), channel_id=1, source_target_pairs={{0,8},{8,16},{16,24},{24,28},{28,20},{20,12},{12,4},{4,0},{1,9},{9... | collective-permute-start | bytes 294920 | tf_op jit(solution)/shard_map/ppermute | solution.py:559
  43.5 5.9 %collective-permute-start.29 = (bf16[112,512]{1,0:T(8,128)(2,1)S(1)}, bf16[112,512]{1,0:T(8,128)(2,1)S(1)}, u32[]{:S(2)}, u32[]{:S(2)}) collective-permute-start(bf16[112,512]{1,0:T(8,128)(2,1)S(1)} %slice.19), channel_id=1, source_target_pairs={{8,0},{16,8},{24,16},{28,24},{20,28},{12,20},{4,12},{0,4},{9,1},{1... | collective-permute-start | bytes 344072 | tf_op jit(solution)/shard_map/ppermute | solution.py:562
  45.4 5.7 %collective-permute-start.19 = (bf16[96,512]{1,0:T(8,128)(2,1)S(1)}, bf16[96,512]{1,0:T(8,128)(2,1)S(1)}, u32[]{:S(2)}, u32[]{:S(2)}) collective-permute-start(bf16[96,512]{1,0:T(8,128)(2,1)S(1)} %collective-permute-done.17.refs_3_), channel_id=1, source_target_pairs={{0,8},{8,16},{16,24},{24,28},{28,20},{20,12},{12,4},{4,0},{1,9},{9... | collective-permute-start | bytes 294920 | tf_op jit(solution)/shard_map/ppermute | solution.py:559
  45.6 6.1 %collective-permute-start.18 = (bf16[96,512]{1,0:T(8,128)(2,1)S(1)}, bf16[96,512]{1,0:T(8,128)(2,1)S(1)}, u32[]{:S(2)}, u32[]{:S(2)}) collective-permute-start(bf16[96,512]{1,0:T(8,128)(2,1)S(1)} %collective-permute-done.16.refs_2_), channel_id=1, source_target_pairs={{8,0},{16,8},{24,16},{28,24},{20,28},{12,20},{4,12},{0,4},{9,1},{1... | collective-permute-start | bytes 294920 | tf_op jit(solution)/shard_map/ppermute | solution.py:562
  47.4 5.9 %collective-permute-start.14 = (bf16[96,512]{1,0:T(8,128)(2,1)S(1)}, bf16[96,512]{1,0:T(8,128)(2,1)S(1)}, u32[]{:S(2)}, u32[]{:S(2)}) collective-permute-start(bf16[96,512]{1,0:T(8,128)(2,1)S(1)} %collective-permute-done.13.refs_8_), channel_id=1, source_target_pairs={{8,0},{16,8},{24,16},{28,24},{20,28},{12,20},{4,12},{0,4},{9,1},{1... | collective-permute-start | bytes 294920 | tf_op jit(solution)/shard_map/ppermute | solution.py:562
  49.0 5.8 %collective-permute-start.10 = (bf16[96,512]{1,0:T(8,128)(2,1)S(1)}, bf16[96,512]{1,0:T(8,128)(2,1)S(1)}, u32[]{:S(2)}, u32[]{:S(2)}) collective-permute-start(bf16[96,512]{1,0:T(8,128)(2,1)S(1)} %collective-permute-done.9.refs_5_), channel_id=1, source_target_pairs={{0,8},{8,16},{16,24},{24,28},{28,20},{20,12},{12,4},{4,0},{1,9},{9... | collective-permute-start | bytes 294920 | tf_op jit(solution)/shard_map/ppermute | solution.py:559
  49.5 5.9 %collective-permute-start.28 = (bf16[112,512]{1,0:T(8,128)(2,1)S(1)}, bf16[112,512]{1,0:T(8,128)(2,1)S(1)}, u32[]{:S(2)}, u32[]{:S(2)}) collective-permute-start(bf16[112,512]{1,0:T(8,128)(2,1)S(1)} %slice.18), channel_id=1, source_target_pairs={{0,8},{8,16},{16,24},{24,28},{28,20},{20,12},{12,4},{4,0},{1,9},{9... | collective-permute-start | bytes 344072 | tf_op jit(solution)/shard_map/ppermute | solution.py:559
  51.1 6.0 %collective-permute-start.21 = (bf16[96,512]{1,0:T(8,128)(2,1)S(1)}, bf16[96,512]{1,0:T(8,128)(2,1)S(1)}, u32[]{:S(2)}, u32[]{:S(2)}) collective-permute-start(bf16[96,512]{1,0:T(8,128)(2,1)S(1)} %collective-permute-done.19.refs_7_), channel_id=1, source_target_pairs={{0,8},{8,16},{16,24},{24,28},{28,20},{20,12},{12,4},{4,0},{1,9},{9... | collective-permute-start | bytes 294920 | tf_op jit(solution)/shard_map/ppermute | solution.py:559
  51.8 5.4 %collective-permute-start.20 = (bf16[96,512]{1,0:T(8,128)(2,1)S(1)}, bf16[96,512]{1,0:T(8,128)(2,1)S(1)}, u32[]{:S(2)}, u32[]{:S(2)}) collective-permute-start(bf16[96,512]{1,0:T(8,128)(2,1)S(1)} %collective-permute-done.18.refs_6_), channel_id=1, source_target_pairs={{8,0},{16,8},{24,16},{28,24},{20,28},{12,20},{4,12},{0,4},{9,1},{1... | collective-permute-start | bytes 294920 | tf_op jit(solution)/shard_map/ppermute | solution.py:562
  53.3 6.2 %collective-permute-start.15 = (bf16[96,512]{1,0:T(8,128)(2,1)S(1)}, bf16[96,512]{1,0:T(8,128)(2,1)S(1)}, u32[]{:S(2)}, u32[]{:S(2)}) collective-permute-start(bf16[96,512]{1,0:T(8,128)(2,1)S(1)} %collective-permute-done.14.refs_12_), channel_id=1, source_target_pairs={{8,0},{16,8},{24,16},{28,24},{20,28},{12,20},{4,12},{0,4},{9,1},{1... | collective-permute-start | bytes 294920 | tf_op jit(solution)/shard_map/ppermute | solution.py:562
  54.8 4.7 %collective-permute-start.11 = (bf16[96,512]{1,0:T(8,128)(2,1)S(1)}, bf16[96,512]{1,0:T(8,128)(2,1)S(1)}, u32[]{:S(2)}, u32[]{:S(2)}) collective-permute-start(bf16[96,512]{1,0:T(8,128)(2,1)S(1)} %collective-permute-done.10.refs_9_), channel_id=1, source_target_pairs={{0,8},{8,16},{16,24},{24,28},{28,20},{20,12},{12,4},{4,0},{1,9},{9... | collective-permute-start | bytes 294920 | tf_op jit(solution)/shard_map/ppermute | solution.py:559
  57.1 2.4 %copy-start.2 = (f32[192,512]{1,0:T(8,128)S(1)}, f32[192,512]{1,0:T(8,128)}, u32[]{:S(2)}) copy-start(f32[192,512]{1,0:T(8,128)} %refs_8_.1) | copy-start | bytes 1179652
  57.2 2.4 %copy-start.3 = (f32[192,512]{1,0:T(8,128)S(1)}, f32[192,512]{1,0:T(8,128)}, u32[]{:S(2)}) copy-start(f32[192,512]{1,0:T(8,128)} %refs_9_.1) | copy-start | bytes 1179652

commit v7 on v6

--- a/solution.py
+++ b/solution.py
@@ -473,8 +473,8 @@
             return BETA * lfac[...] + (1.0 - BETA) * left, BETA * rfac[...] + (1.0 - BETA) * right
 
         complete(0, first_block)
+        copy(0, first_block).start()
         lout[...], rout[...] = renewed(own_first)
-        copy(0, first_block).start()
 
         @pl.when(last_block != first_block)
         def _():

time: 61.7 us -> 62.1 us (level)
  no operation moved by 1% of the time
where the time goes in v7:
time: 62.1 us; the launch traced here: 61.6 us
  starting transfers between devices  32.9 us (53%)
  waiting for transfers between devices  19.5 us (31%)
  Pallas kernels  6.84 us (11%)
  local copies, waits for them, and re-layouts  1.47 us (2%)
  between operations  0.84 us (1%)
    ppermute x15, starting transfers between devices, send_left(): return lax.ppermute(x, 'dp', backward)  27.3 us
    ppermute x15, waiting for transfers between devices, send_left(): return lax.ppermute(x, 'dp', backward)  16.5 us
    ppermute x15, starting transfers between devices, send_right(): return lax.ppermute(x, 'dp', onward)  5.65 us
    ppermute x15, waiting for transfers between devices, send_right(): return lax.ppermute(x, 'dp', onward)  2.99 us
    pallas_call x1, Pallas kernels, begin(): pl.pallas_call(kernel, out_shape=(jax.ShapeDtypeStruct((stacked, breadth)...  2.31 us
    pallas_call x1, Pallas kernels, finish(): pl.pallas_call(kernel, out_shape=(jax.ShapeDtypeStruct((stacked, breadth)...  2.03 us
    pallas_call x1, Pallas kernels, unpack_roots(): pl.pallas_call(kernel, out_shape=(out, out), grid_spec=pltpu.PrefetchScal...  1.78 us
    unnamed x14, local copies, waits for them, and re-layouts  1.43 us
  transfers between devices with their start and end apart: 30, of which 11 were waited for; matrix products, arithmetic and copies ran while one was open for 0% of the time, Pallas kernels for 8%

profile of v7, /device:TPU:0, one launch (start us, length us, event | category | flops | bytes accessed | tf_op | source)
XLA Modules:
  0.0 61.6 jit_solution(3679325346432168124)
XLA Ops:
  0.6 1.4 %copy-done = bf16[1,1536,512]{2,1,0:T(8,128)(2,1)S(1)} copy-done((bf16[1,1536,512]{2,1,0:T(8,128)(2,1)S(1)}, bf16[1,1536,512]{2,1,0:T(8,128)(2,1)}, u32[]{:S(2)}) %copy-start) | copy-done | bytes 1572888
  2.1 3.0 %collective-permute-start.4 = (bf16[96,512]{1,0:T(8,128)(2,1)S(1)}, bf16[96,512]{1,0:T(8,128)(2,1)S(1)}, u32[]{:S(2)}, u32[]{:S(2)}) collective-permute-start(bf16[96,512]{1,0:T(8,128)(2,1)S(1)} %get-tuple-element.12), channel_id=1, source_target_pairs={{8,0},{16,8},{24,16},{28,24},{20,28},{12,20},{4,12},{0,4},{9,1},{1... | collective-permute-start | bytes 294920 | tf_op jit(solution)/shard_map/ppermute | solution.py:562
  5.1 0.2 collective-permute-start
  5.2 2.7 %collective-permute-done.4.a_ref = bf16[96,512]{1,0:T(8,128)(2,1)S(1)} collective-permute-done((bf16[96,512]{1,0:T(8,128)(2,1)S(1)}, bf16[96,512]{1,0:T(8,128)(2,1)S(1)}, u32[]{:S(2)}, u32[]{:S(2)}) %collective-permute-start.4) | collective-permute-done | bytes 98336 | tf_op jit(solution)/shard_map/ppermute | solution.py:562
  8.0 1.8 %collective-permute-start.5 = (bf16[192,512]{1,0:T(8,128)(2,1)S(1)}, bf16[192,512]{1,0:T(8,128)(2,1)S(1)}, u32[]{:S(2)}, u32[]{:S(2)}) collective-permute-start(bf16[192,512]{1,0:T(8,128)(2,1)S(1)} %add_send.9), channel_id=1, source_target_pairs={{8,0},{16,8},{24,16},{28,24},{20,28},{12,20},{4,12},{0,4},{9,1},{1... | collective-permute-start | bytes 589832 | tf_op jit(solution)/shard_map/ppermute | solution.py:562
  9.8 0.3 collective-permute-start.1
  10.2 0.3 pack_roots.1.refs_0_
  10.5 1.7 %collective-permute-start.23 = (bf16[224,512]{1,0:T(8,128)(2,1)S(1)}, bf16[224,512]{1,0:T(8,128)(2,1)S(1)}, u32[]{:S(2)}, u32[]{:S(2)}) collective-permute-start(bf16[224,512]{1,0:T(8,128)(2,1)S(1)} %pack_roots.1.refs_0_), channel_id=1, source_target_pairs={{8,0},{16,8},{24,16},{28,24},{20,28},{12,20},{4,12},{0,4},{9,1},{1... | collective-permute-start | bytes 688136 | tf_op jit(solution)/shard_map/ppermute | solution.py:562
  12.2 0.4 collective-permute-start.22
  12.6 3.3 %collective-permute-done.5.a_ref = bf16[192,512]{1,0:T(8,128)(2,1)S(1)} collective-permute-done((bf16[192,512]{1,0:T(8,128)(2,1)S(1)}, bf16[192,512]{1,0:T(8,128)(2,1)S(1)}, u32[]{:S(2)}, u32[]{:S(2)}) %collective-permute-start.5) | collective-permute-done | bytes 196640 | tf_op jit(solution)/shard_map/ppermute | solution.py:562
  15.9 1.8 %collective-permute-start.6 = (bf16[192,512]{1,0:T(8,128)(2,1)S(1)}, bf16[192,512]{1,0:T(8,128)(2,1)S(1)}, u32[]{:S(2)}, u32[]{:S(2)}) collective-permute-start(bf16[192,512]{1,0:T(8,128)(2,1)S(1)} %add_send.10), channel_id=1, source_target_pairs={{8,0},{16,8},{24,16},{28,24},{20,28},{12,20},{4,12},{0,4},{9,1},{1... | collective-permute-start | bytes 589832 | tf_op jit(solution)/shard_map/ppermute | solution.py:562
  17.7 0.1 add_send.7
  17.8 0.3 collective-permute-start.2
  18.1 2.7 %collective-permute-done.23.refs_2_ = bf16[224,512]{1,0:T(8,128)(2,1)S(1)} collective-permute-done((bf16[224,512]{1,0:T(8,128)(2,1)S(1)}, bf16[224,512]{1,0:T(8,128)(2,1)S(1)}, u32[]{:S(2)}, u32[]{:S(2)}) %collective-permute-start.23) | collective-permute-done | bytes 229408 | tf_op jit(solution)/shard_map/ppermute | solution.py:562
  20.8 1.7 %collective-permute-start.25 = (bf16[224,512]{1,0:T(8,128)(2,1)S(1)}, bf16[224,512]{1,0:T(8,128)(2,1)S(1)}, u32[]{:S(2)}, u32[]{:S(2)}) collective-permute-start(bf16[224,512]{1,0:T(8,128)(2,1)S(1)} %collective-permute-done.23.refs_2_), channel_id=1, source_target_pairs={{8,0},{16,8},{24,16},{28,24},{20,28},{12,20},{4,12},{0,4},{9,1},{1... | collective-permute-start | bytes 688136 | tf_op jit(solution)/shard_map/ppermute | solution.py:562
  22.5 0.1 collective-permute-done.22.refs_1_
  22.6 0.3 collective-permute-start.24
  22.9 2.1 %collective-permute-done.6.a_ref = bf16[192,512]{1,0:T(8,128)(2,1)S(1)} collective-permute-done((bf16[192,512]{1,0:T(8,128)(2,1)S(1)}, bf16[192,512]{1,0:T(8,128)(2,1)S(1)}, u32[]{:S(2)}, u32[]{:S(2)}) %collective-permute-start.6) | collective-permute-done | bytes 196640 | tf_op jit(solution)/shard_map/ppermute | solution.py:562
  25.1 1.8 %collective-permute-start.7 = (bf16[192,512]{1,0:T(8,128)(2,1)S(1)}, bf16[192,512]{1,0:T(8,128)(2,1)S(1)}, u32[]{:S(2)}, u32[]{:S(2)}) collective-permute-start(bf16[192,512]{1,0:T(8,128)(2,1)S(1)} %add_send.11), channel_id=1, source_target_pairs={{8,0},{16,8},{24,16},{28,24},{20,28},{12,20},{4,12},{0,4},{9,1},{1... | collective-permute-start | bytes 589832 | tf_op jit(solution)/shard_map/ppermute | solution.py:562
  26.9 0.3 collective-permute-start.3
  27.3 2.7 %collective-permute-done.25.refs_4_ = bf16[224,512]{1,0:T(8,128)(2,1)S(1)} collective-permute-done((bf16[224,512]{1,0:T(8,128)(2,1)S(1)}, bf16[224,512]{1,0:T(8,128)(2,1)S(1)}, u32[]{:S(2)}, u32[]{:S(2)}) %collective-permute-start.25) | collective-permute-done | bytes 229408 | tf_op jit(solution)/shard_map/ppermute | solution.py:562
  29.9 1.7 %collective-permute-start.27 = (bf16[224,512]{1,0:T(8,128)(2,1)S(1)}, bf16[224,512]{1,0:T(8,128)(2,1)S(1)}, u32[]{:S(2)}, u32[]{:S(2)}) collective-permute-start(bf16[224,512]{1,0:T(8,128)(2,1)S(1)} %collective-permute-done.25.refs_4_), channel_id=1, source_target_pairs={{8,0},{16,8},{24,16},{28,24},{20,28},{12,20},{4,12},{0,4},{9,1},{1... | collective-permute-start | bytes 688136 | tf_op jit(solution)/shard_map/ppermute | solution.py:562
  31.7 0.1 collective-permute-done.24.refs_3_
  31.7 0.3 collective-permute-start.26
  32.0 2.1 %collective-permute-done.7.l_ref = bf16[192,512]{1,0:T(8,128)(2,1)S(1)} collective-permute-done((bf16[192,512]{1,0:T(8,128)(2,1)S(1)}, bf16[192,512]{1,0:T(8,128)(2,1)S(1)}, u32[]{:S(2)}, u32[]{:S(2)}) %collective-permute-start.7) | collective-permute-done | bytes 196640 | tf_op jit(solution)/shard_map/ppermute | solution.py:562
  34.1 1.8 %collective-permute-done.3.r_ref = bf16[192,512]{1,0:T(8,128)(2,1)S(1)} collective-permute-done((bf16[192,512]{1,0:T(8,128)(2,1)S(1)}, bf16[192,512]{1,0:T(8,128)(2,1)S(1)}, u32[]{:S(2)}, u32[]{:S(2)}) %collective-permute-start.3) | collective-permute-done | bytes 196640 | tf_op jit(solution)/shard_map/ppermute | solution.py:559
  36.0 0.1 add_own.1.refs_0_
  36.1 1.6 %collective-permute-start.12 = (bf16[96,512]{1,0:T(8,128)(2,1)S(1)}, bf16[96,512]{1,0:T(8,128)(2,1)S(1)}, u32[]{:S(2)}, u32[]{:S(2)}) collective-permute-start(bf16[96,512]{1,0:T(8,128)(2,1)S(1)} %get-tuple-element.19), channel_id=1, source_target_pairs={{8,0},{16,8},{24,16},{28,24},{20,28},{12,20},{4,12},{0,4},{9,1},{1... | collective-permute-start | bytes 294920 | tf_op jit(solution)/shard_map/ppermute | solution.py:562
  37.7 0.4 collective-permute-start.8
  38.1 0.3 collective-permute-start.17
  38.4 1.7 %collective-permute-start.16 = (bf16[96,512]{1,0:T(8,128)(2,1)S(1)}, bf16[96,512]{1,0:T(8,128)(2,1)S(1)}, u32[]{:S(2)}, u32[]{:S(2)}) collective-permute-start(bf16[96,512]{1,0:T(8,128)(2,1)S(1)} %get-tuple-element.20), channel_id=1, source_target_pairs={{8,0},{16,8},{24,16},{28,24},{20,28},{12,20},{4,12},{0,4},{9,1},{1... | collective-permute-start | bytes 294920 | tf_op jit(solution)/shard_map/ppermute | solution.py:562
  40.2 1.0 %collective-permute-done.12.refs_4_ = bf16[96,512]{1,0:T(8,128)(2,1)S(1)} collective-permute-done((bf16[96,512]{1,0:T(8,128)(2,1)S(1)}, bf16[96,512]{1,0:T(8,128)(2,1)S(1)}, u32[]{:S(2)}, u32[]{:S(2)}) %collective-permute-start.12) | collective-permute-done | bytes 98336 | tf_op jit(solution)/shard_map/ppermute | solution.py:562
  41.2 2.1 %collective-permute-start.13 = (bf16[96,512]{1,0:T(8,128)(2,1)S(1)}, bf16[96,512]{1,0:T(8,128)(2,1)S(1)}, u32[]{:S(2)}, u32[]{:S(2)}) collective-permute-start(bf16[96,512]{1,0:T(8,128)(2,1)S(1)} %collective-permute-done.12.refs_4_), channel_id=1, source_target_pairs={{8,0},{16,8},{24,16},{28,24},{20,28},{12,20},{4,12},{0,4},{9,1},{1... | collective-permute-start | bytes 294920 | tf_op jit(solution)/shard_map/ppermute | solution.py:562
  43.3 0.2 collective-permute-start.9
  43.5 1.8 %collective-permute-start.29 = (bf16[112,512]{1,0:T(8,128)(2,1)S(1)}, bf16[112,512]{1,0:T(8,128)(2,1)S(1)}, u32[]{:S(2)}, u32[]{:S(2)}) collective-permute-start(bf16[112,512]{1,0:T(8,128)(2,1)S(1)} %slice.19), channel_id=1, source_target_pairs={{8,0},{16,8},{24,16},{28,24},{20,28},{12,20},{4,12},{0,4},{9,1},{1... | collective-permute-start | bytes 344072 | tf_op jit(solution)/shard_map/ppermute | solution.py:562
  45.4 0.2 collective-permute-start.19
  45.6 1.8 %collective-permute-start.18 = (bf16[96,512]{1,0:T(8,128)(2,1)S(1)}, bf16[96,512]{1,0:T(8,128)(2,1)S(1)}, u32[]{:S(2)}, u32[]{:S(2)}) collective-permute-start(bf16[96,512]{1,0:T(8,128)(2,1)S(1)} %collective-permute-done.16.refs_2_), channel_id=1, source_target_pairs={{8,0},{16,8},{24,16},{28,24},{20,28},{12,20},{4,12},{0,4},{9,1},{1... | collective-permute-start | bytes 294920 | tf_op jit(solution)/shard_map/ppermute | solution.py:562
  47.4 1.6 %collective-permute-start.14 = (bf16[96,512]{1,0:T(8,128)(2,1)S(1)}, bf16[96,512]{1,0:T(8,128)(2,1)S(1)}, u32[]{:S(2)}, u32[]{:S(2)}) collective-permute-start(bf16[96,512]{1,0:T(8,128)(2,1)S(1)} %collective-permute-done.13.refs_8_), channel_id=1, source_target_pairs={{8,0},{16,8},{24,16},{28,24},{20,28},{12,20},{4,12},{0,4},{9,1},{1... | collective-permute-start | bytes 294920 | tf_op jit(solution)/shard_map/ppermute | solution.py:562
  49.0 0.5 collective-permute-start.10
  49.5 0.7 %collective-permute-start.28 = (bf16[112,512]{1,0:T(8,128)(2,1)S(1)}, bf16[112,512]{1,0:T(8,128)(2,1)S(1)}, u32[]{:S(2)}, u32[]{:S(2)}) collective-permute-start(bf16[112,512]{1,0:T(8,128)(2,1)S(1)} %slice.18), channel_id=1, source_target_pairs={{0,8},{8,16},{16,24},{24,28},{28,20},{20,12},{12,4},{4,0},{1,9},{9... | collective-permute-start | bytes 344072 | tf_op jit(solution)/shard_map/ppermute | solution.py:559
  50.2 0.9 %collective-permute-done.19.refs_7_ = bf16[96,512]{1,0:T(8,128)(2,1)S(1)} collective-permute-done((bf16[96,512]{1,0:T(8,128)(2,1)S(1)}, bf16[96,512]{1,0:T(8,128)(2,1)S(1)}, u32[]{:S(2)}, u32[]{:S(2)}) %collective-permute-start.19) | collective-permute-done | bytes 98336 | tf_op jit(solution)/shard_map/ppermute | solution.py:559
  51.1 0.6 %collective-permute-start.21 = (bf16[96,512]{1,0:T(8,128)(2,1)S(1)}, bf16[96,512]{1,0:T(8,128)(2,1)S(1)}, u32[]{:S(2)}, u32[]{:S(2)}) collective-permute-start(bf16[96,512]{1,0:T(8,128)(2,1)S(1)} %collective-permute-done.19.refs_7_), channel_id=1, source_target_pairs={{0,8},{8,16},{16,24},{24,28},{28,20},{20,12},{12,4},{4,0},{1,9},{9... | collective-permute-start | bytes 294920 | tf_op jit(solution)/shard_map/ppermute | solution.py:559
  51.8 1.5 %collective-permute-start.20 = (bf16[96,512]{1,0:T(8,128)(2,1)S(1)}, bf16[96,512]{1,0:T(8,128)(2,1)S(1)}, u32[]{:S(2)}, u32[]{:S(2)}) collective-permute-start(bf16[96,512]{1,0:T(8,128)(2,1)S(1)} %collective-permute-done.18.refs_6_), channel_id=1, source_target_pairs={{8,0},{16,8},{24,16},{28,24},{20,28},{12,20},{4,12},{0,4},{9,1},{1... | collective-permute-start | bytes 294920 | tf_op jit(solution)/shard_map/ppermute | solution.py:562
  53.3 1.5 %collective-permute-start.15 = (bf16[96,512]{1,0:T(8,128)(2,1)S(1)}, bf16[96,512]{1,0:T(8,128)(2,1)S(1)}, u32[]{:S(2)}, u32[]{:S(2)}) collective-permute-start(bf16[96,512]{1,0:T(8,128)(2,1)S(1)} %collective-permute-done.14.refs_12_), channel_id=1, source_target_pairs={{8,0},{16,8},{24,16},{28,24},{20,28},{12,20},{4,12},{0,4},{9,1},{1... | collective-permute-start | bytes 294920 | tf_op jit(solution)/shard_map/ppermute | solution.py:562
  54.8 0.5 collective-permute-start.11
  55.3 1.8 %unpack_roots.1 = (bf16[1536,512]{1,0:T(8,128)(2,1)S(1)}, bf16[1536,512]{1,0:T(8,128)(2,1)S(1)}) custom-call(s32[1]{0:T(128)} %bitcast.me_ref, s32[1,8]{1,0:T(1,128)S(1)} %bitcast.3, bf16[224,512]{1,0:T(8,128)(2,1)S(1)} %pack_roots.1.refs_0_, bf16[224,512]{1,0:T(8,128)(2,1)S(1)} %collective-permute-done.22.refs_1_, ...), custom_call_target="tpu_custom_call" | custom-call | tf_op jit(solution)/shard_map/unpack_roots/pallas_call | solution.py:351
  57.2 2.3 %begin.1 = (bf16[1536,512]{1,0:T(8,128)(2,1)}, bf16[512,512]{1,0:T(8,128)(2,1)S(1)}, bf16[1536,512]{1,0:T(8,128)(2,1)S(1)}, f32[3,512,512]{2,1,0:T(8,128)S(1)}) custom-call(s32[1]{0:T(128)} %bitcast.me_ref, bf16[192,512]{1,0:T(8,128)(2,1)S(1)} %add_own.1.refs_0_, bf16[96,512]{1,0:T(8,128)(2,1)S(1)} %collective-permute-done.8.refs_1_, ...), custom_call_target="tpu_custom_call" | custom-call | tf_op jit(solution)/shard_map/begin/pallas_call | solution.py:394
  59.5 2.0 %finish.1 = (bf16[1536,512]{1,0:T(8,128)(2,1)}, f32[192,512]{1,0:T(8,128)}, f32[192,512]{1,0:T(8,128)}) custom-call(s32[1]{0:T(128)} %bitcast.me_ref, s32[1,8]{1,0:T(1,128)S(1)} %bitcast.4, bf16[96,512]{1,0:T(8,128)(2,1)S(1)} %collective-permute-done.11.refs_0_, ...), custom_call_target="tpu_custom_call", output_to_operand_aliasing={{0}: (4, {})} | custom-call | tf_op jit(solution)/shard_map/finish/pallas_call | solution.py:509
  (41 shorter events, 0.4 us)
Async XLA Ops:
  0.6 1.4 %copy-start = (bf16[1,1536,512]{2,1,0:T(8,128)(2,1)S(1)}, bf16[1,1536,512]{2,1,0:T(8,128)(2,1)}, u32[]{:S(2)}) copy-start(bf16[1,1536,512]{2,1,0:T(8,128)(2,1)} %own_ref.13) | copy-start | bytes 4718596
  2.1 5.9 %collective-permute-start.4 = (bf16[96,512]{1,0:T(8,128)(2,1)S(1)}, bf16[96,512]{1,0:T(8,128)(2,1)S(1)}, u32[]{:S(2)}, u32[]{:S(2)}) collective-permute-start(bf16[96,512]{1,0:T(8,128)(2,1)S(1)} %get-tuple-element.12), channel_id=1, source_target_pairs={{8,0},{16,8},{24,16},{28,24},{20,28},{12,20},{4,12},{0,4},{9,1},{1... | collective-permute-start | bytes 294920 | tf_op jit(solution)/shard_map/ppermute | solution.py:562
  5.1 5.1 %copy-start.4 = (bf16[192,512]{1,0:T(8,128)(2,1)S(1)}, bf16[192,512]{1,0:T(8,128)(2,1)}, u32[]{:S(2)}) copy-start(bf16[192,512]{1,0:T(8,128)(2,1)} %l_ref.1) | copy-start | bytes 589828
  5.1 5.1 %copy-start.5 = (bf16[192,512]{1,0:T(8,128)(2,1)S(1)}, bf16[192,512]{1,0:T(8,128)(2,1)}, u32[]{:S(2)}) copy-start(bf16[192,512]{1,0:T(8,128)(2,1)} %r_ref.1) | copy-start | bytes 589828
  5.1 5.1 %copy-start.6 = (s32[8]{0:T(128)S(1)}, s32[8]{0:T(128)}, u32[]{:S(2)}) copy-start(s32[8]{0:T(128)} %param.7) | copy-start | bytes 100
  5.1 4.7 %collective-permute-start = (bf16[96,512]{1,0:T(8,128)(2,1)S(1)}, bf16[96,512]{1,0:T(8,128)(2,1)S(1)}, u32[]{:S(2)}, u32[]{:S(2)}) collective-permute-start(bf16[96,512]{1,0:T(8,128)(2,1)S(1)} %get-tuple-element.11), channel_id=1, source_target_pairs={{0,8},{8,16},{16,24},{24,28},{28,20},{20,12},{12,4},{4,0},{1,9},{9... | collective-permute-start | bytes 294920 | tf_op jit(solution)/shard_map/ppermute | solution.py:559
  8.0 7.9 %copy-start.1 = (bf16[1,1536,512]{2,1,0:T(8,128)(2,1)S(1)}, bf16[1,1536,512]{2,1,0:T(8,128)(2,1)}, u32[]{:S(2)}) copy-start(bf16[1,1536,512]{2,1,0:T(8,128)(2,1)} %own_ref.13) | copy-start | bytes 4718596
  8.0 7.9 %collective-permute-start.5 = (bf16[192,512]{1,0:T(8,128)(2,1)S(1)}, bf16[192,512]{1,0:T(8,128)(2,1)S(1)}, u32[]{:S(2)}, u32[]{:S(2)}) collective-permute-start(bf16[192,512]{1,0:T(8,128)(2,1)S(1)} %add_send.9), channel_id=1, source_target_pairs={{8,0},{16,8},{24,16},{28,24},{20,28},{12,20},{4,12},{0,4},{9,1},{1... | collective-permute-start | bytes 589832 | tf_op jit(solution)/shard_map/ppermute | solution.py:562
  9.8 7.9 %collective-permute-start.1 = (bf16[192,512]{1,0:T(8,128)(2,1)S(1)}, bf16[192,512]{1,0:T(8,128)(2,1)S(1)}, u32[]{:S(2)}, u32[]{:S(2)}) collective-permute-start(bf16[192,512]{1,0:T(8,128)(2,1)S(1)} %add_send.6), channel_id=1, source_target_pairs={{0,8},{8,16},{16,24},{24,28},{28,20},{20,12},{12,4},{4,0},{1,9},{9... | collective-permute-start | bytes 589832 | tf_op jit(solution)/shard_map/ppermute | solution.py:559
  10.5 10.3 %collective-permute-start.23 = (bf16[224,512]{1,0:T(8,128)(2,1)S(1)}, bf16[224,512]{1,0:T(8,128)(2,1)S(1)}, u32[]{:S(2)}, u32[]{:S(2)}) collective-permute-start(bf16[224,512]{1,0:T(8,128)(2,1)S(1)} %pack_roots.1.refs_0_), channel_id=1, source_target_pairs={{8,0},{16,8},{24,16},{28,24},{20,28},{12,20},{4,12},{0,4},{9,1},{1... | collective-permute-start | bytes 688136 | tf_op jit(solution)/shard_map/ppermute | solution.py:562
  12.2 10.4 %collective-permute-start.22 = (bf16[224,512]{1,0:T(8,128)(2,1)S(1)}, bf16[224,512]{1,0:T(8,128)(2,1)S(1)}, u32[]{:S(2)}, u32[]{:S(2)}) collective-permute-start(bf16[224,512]{1,0:T(8,128)(2,1)S(1)} %pack_roots.1.refs_0_), channel_id=1, source_target_pairs={{0,8},{8,16},{16,24},{24,28},{28,20},{20,12},{12,4},{4,0},{1,9},{9... | collective-permute-start | bytes 688136 | tf_op jit(solution)/shard_map/ppermute | solution.py:559
  15.9 9.1 %collective-permute-start.6 = (bf16[192,512]{1,0:T(8,128)(2,1)S(1)}, bf16[192,512]{1,0:T(8,128)(2,1)S(1)}, u32[]{:S(2)}, u32[]{:S(2)}) collective-permute-start(bf16[192,512]{1,0:T(8,128)(2,1)S(1)} %add_send.10), channel_id=1, source_target_pairs={{8,0},{16,8},{24,16},{28,24},{20,28},{12,20},{4,12},{0,4},{9,1},{1... | collective-permute-start | bytes 589832 | tf_op jit(solution)/shard_map/ppermute | solution.py:562
  17.8 9.1 %collective-permute-start.2 = (bf16[192,512]{1,0:T(8,128)(2,1)S(1)}, bf16[192,512]{1,0:T(8,128)(2,1)S(1)}, u32[]{:S(2)}, u32[]{:S(2)}) collective-permute-start(bf16[192,512]{1,0:T(8,128)(2,1)S(1)} %add_send.7), channel_id=1, source_target_pairs={{0,8},{8,16},{16,24},{24,28},{28,20},{20,12},{12,4},{4,0},{1,9},{9... | collective-permute-start | bytes 589832 | tf_op jit(solution)/shard_map/ppermute | solution.py:559
  20.8 9.1 %collective-permute-start.25 = (bf16[224,512]{1,0:T(8,128)(2,1)S(1)}, bf16[224,512]{1,0:T(8,128)(2,1)S(1)}, u32[]{:S(2)}, u32[]{:S(2)}) collective-permute-start(bf16[224,512]{1,0:T(8,128)(2,1)S(1)} %collective-permute-done.23.refs_2_), channel_id=1, source_target_pairs={{8,0},{16,8},{24,16},{28,24},{20,28},{12,20},{4,12},{0,4},{9,1},{1... | collective-permute-start | bytes 688136 | tf_op jit(solution)/shard_map/ppermute | solution.py:562
  22.6 9.1 %collective-permute-start.24 = (bf16[224,512]{1,0:T(8,128)(2,1)S(1)}, bf16[224,512]{1,0:T(8,128)(2,1)S(1)}, u32[]{:S(2)}, u32[]{:S(2)}) collective-permute-start(bf16[224,512]{1,0:T(8,128)(2,1)S(1)} %collective-permute-done.22.refs_1_), channel_id=1, source_target_pairs={{0,8},{8,16},{16,24},{24,28},{28,20},{20,12},{12,4},{4,0},{1,9},{9... | collective-permute-start | bytes 688136 | tf_op jit(solution)/shard_map/ppermute | solution.py:559
  25.1 9.1 %collective-permute-start.7 = (bf16[192,512]{1,0:T(8,128)(2,1)S(1)}, bf16[192,512]{1,0:T(8,128)(2,1)S(1)}, u32[]{:S(2)}, u32[]{:S(2)}) collective-permute-start(bf16[192,512]{1,0:T(8,128)(2,1)S(1)} %add_send.11), channel_id=1, source_target_pairs={{8,0},{16,8},{24,16},{28,24},{20,28},{12,20},{4,12},{0,4},{9,1},{1... | collective-permute-start | bytes 589832 | tf_op jit(solution)/shard_map/ppermute | solution.py:562
  26.9 9.0 %collective-permute-start.3 = (bf16[192,512]{1,0:T(8,128)(2,1)S(1)}, bf16[192,512]{1,0:T(8,128)(2,1)S(1)}, u32[]{:S(2)}, u32[]{:S(2)}) collective-permute-start(bf16[192,512]{1,0:T(8,128)(2,1)S(1)} %add_send.8), channel_id=1, source_target_pairs={{0,8},{8,16},{16,24},{24,28},{28,20},{20,12},{12,4},{4,0},{1,9},{9... | collective-permute-start | bytes 589832 | tf_op jit(solution)/shard_map/ppermute | solution.py:559
  29.9 8.5 %collective-permute-start.27 = (bf16[224,512]{1,0:T(8,128)(2,1)S(1)}, bf16[224,512]{1,0:T(8,128)(2,1)S(1)}, u32[]{:S(2)}, u32[]{:S(2)}) collective-permute-start(bf16[224,512]{1,0:T(8,128)(2,1)S(1)} %collective-permute-done.25.refs_4_), channel_id=1, source_target_pairs={{8,0},{16,8},{24,16},{28,24},{20,28},{12,20},{4,12},{0,4},{9,1},{1... | collective-permute-start | bytes 688136 | tf_op jit(solution)/shard_map/ppermute | solution.py:562
  31.7 11.8 %collective-permute-start.26 = (bf16[224,512]{1,0:T(8,128)(2,1)S(1)}, bf16[224,512]{1,0:T(8,128)(2,1)S(1)}, u32[]{:S(2)}, u32[]{:S(2)}) collective-permute-start(bf16[224,512]{1,0:T(8,128)(2,1)S(1)} %collective-permute-done.24.refs_3_), channel_id=1, source_target_pairs={{0,8},{8,16},{16,24},{24,28},{28,20},{20,12},{12,4},{4,0},{1,9},{9... | collective-permute-start | bytes 688136 | tf_op jit(solution)/shard_map/ppermute | solution.py:559
  36.1 5.1 %collective-permute-start.12 = (bf16[96,512]{1,0:T(8,128)(2,1)S(1)}, bf16[96,512]{1,0:T(8,128)(2,1)S(1)}, u32[]{:S(2)}, u32[]{:S(2)}) collective-permute-start(bf16[96,512]{1,0:T(8,128)(2,1)S(1)} %get-tuple-element.19), channel_id=1, source_target_pairs={{8,0},{16,8},{24,16},{28,24},{20,28},{12,20},{4,12},{0,4},{9,1},{1... | collective-permute-start | bytes 294920 | tf_op jit(solution)/shard_map/ppermute | solution.py:562
  37.7 5.6 %collective-permute-start.8 = (bf16[96,512]{1,0:T(8,128)(2,1)S(1)}, bf16[96,512]{1,0:T(8,128)(2,1)S(1)}, u32[]{:S(2)}, u32[]{:S(2)}) collective-permute-start(bf16[96,512]{1,0:T(8,128)(2,1)S(1)} %get-tuple-element.20), channel_id=1, source_target_pairs={{0,8},{8,16},{16,24},{24,28},{28,20},{20,12},{12,4},{4,0},{1,9},{9... | collective-permute-start | bytes 294920 | tf_op jit(solution)/shard_map/ppermute | solution.py:559
  38.1 7.2 %collective-permute-start.17 = (bf16[96,512]{1,0:T(8,128)(2,1)S(1)}, bf16[96,512]{1,0:T(8,128)(2,1)S(1)}, u32[]{:S(2)}, u32[]{:S(2)}) collective-permute-start(bf16[96,512]{1,0:T(8,128)(2,1)S(1)} %get-tuple-element.19), channel_id=1, source_target_pairs={{0,8},{8,16},{16,24},{24,28},{28,20},{20,12},{12,4},{4,0},{1,9},{9... | collective-permute-start | bytes 294920 | tf_op jit(solution)/shard_map/ppermute | solution.py:559
  38.4 7.2 %collective-permute-start.16 = (bf16[96,512]{1,0:T(8,128)(2,1)S(1)}, bf16[96,512]{1,0:T(8,128)(2,1)S(1)}, u32[]{:S(2)}, u32[]{:S(2)}) collective-permute-start(bf16[96,512]{1,0:T(8,128)(2,1)S(1)} %get-tuple-element.20), channel_id=1, source_target_pairs={{8,0},{16,8},{24,16},{28,24},{20,28},{12,20},{4,12},{0,4},{9,1},{1... | collective-permute-start | bytes 294920 | tf_op jit(solution)/shard_map/ppermute | solution.py:562
  41.2 6.2 %collective-permute-start.13 = (bf16[96,512]{1,0:T(8,128)(2,1)S(1)}, bf16[96,512]{1,0:T(8,128)(2,1)S(1)}, u32[]{:S(2)}, u32[]{:S(2)}) collective-permute-start(bf16[96,512]{1,0:T(8,128)(2,1)S(1)} %collective-permute-done.12.refs_4_), channel_id=1, source_target_pairs={{8,0},{16,8},{24,16},{28,24},{20,28},{12,20},{4,12},{0,4},{9,1},{1... | collective-permute-start | bytes 294920 | tf_op jit(solution)/shard_map/ppermute | solution.py:562
  43.3 5.7 %collective-permute-start.9 = (bf16[96,512]{1,0:T(8,128)(2,1)S(1)}, bf16[96,512]{1,0:T(8,128)(2,1)S(1)}, u32[]{:S(2)}, u32[]{:S(2)}) collective-permute-start(bf16[96,512]{1,0:T(8,128)(2,1)S(1)} %collective-permute-done.8.refs_1_), channel_id=1, source_target_pairs={{0,8},{8,16},{16,24},{24,28},{28,20},{20,12},{12,4},{4,0},{1,9},{9... | collective-permute-start | bytes 294920 | tf_op jit(solution)/shard_map/ppermute | solution.py:559
  43.5 5.9 %collective-permute-start.29 = (bf16[112,512]{1,0:T(8,128)(2,1)S(1)}, bf16[112,512]{1,0:T(8,128)(2,1)S(1)}, u32[]{:S(2)}, u32[]{:S(2)}) collective-permute-start(bf16[112,512]{1,0:T(8,128)(2,1)S(1)} %slice.19), channel_id=1, source_target_pairs={{8,0},{16,8},{24,16},{28,24},{20,28},{12,20},{4,12},{0,4},{9,1},{1... | collective-permute-start | bytes 344072 | tf_op jit(solution)/shard_map/ppermute | solution.py:562
  45.4 5.7 %collective-permute-start.19 = (bf16[96,512]{1,0:T(8,128)(2,1)S(1)}, bf16[96,512]{1,0:T(8,128)(2,1)S(1)}, u32[]{:S(2)}, u32[]{:S(2)}) collective-permute-start(bf16[96,512]{1,0:T(8,128)(2,1)S(1)} %collective-permute-done.17.refs_3_), channel_id=1, source_target_pairs={{0,8},{8,16},{16,24},{24,28},{28,20},{20,12},{12,4},{4,0},{1,9},{9... | collective-permute-start | bytes 294920 | tf_op jit(solution)/shard_map/ppermute | solution.py:559
  45.6 6.1 %collective-permute-start.18 = (bf16[96,512]{1,0:T(8,128)(2,1)S(1)}, bf16[96,512]{1,0:T(8,128)(2,1)S(1)}, u32[]{:S(2)}, u32[]{:S(2)}) collective-permute-start(bf16[96,512]{1,0:T(8,128)(2,1)S(1)} %collective-permute-done.16.refs_2_), channel_id=1, source_target_pairs={{8,0},{16,8},{24,16},{28,24},{20,28},{12,20},{4,12},{0,4},{9,1},{1... | collective-permute-start | bytes 294920 | tf_op jit(solution)/shard_map/ppermute | solution.py:562
  47.4 5.9 %collective-permute-start.14 = (bf16[96,512]{1,0:T(8,128)(2,1)S(1)}, bf16[96,512]{1,0:T(8,128)(2,1)S(1)}, u32[]{:S(2)}, u32[]{:S(2)}) collective-permute-start(bf16[96,512]{1,0:T(8,128)(2,1)S(1)} %collective-permute-done.13.refs_8_), channel_id=1, source_target_pairs={{8,0},{16,8},{24,16},{28,24},{20,28},{12,20},{4,12},{0,4},{9,1},{1... | collective-permute-start | bytes 294920 | tf_op jit(solution)/shard_map/ppermute | solution.py:562
  49.0 5.8 %collective-permute-start.10 = (bf16[96,512]{1,0:T(8,128)(2,1)S(1)}, bf16[96,512]{1,0:T(8,128)(2,1)S(1)}, u32[]{:S(2)}, u32[]{:S(2)}) collective-permute-start(bf16[96,512]{1,0:T(8,128)(2,1)S(1)} %collective-permute-done.9.refs_5_), channel_id=1, source_target_pairs={{0,8},{8,16},{16,24},{24,28},{28,20},{20,12},{12,4},{4,0},{1,9},{9... | collective-permute-start | bytes 294920 | tf_op jit(solution)/shard_map/ppermute | solution.py:559
  49.5 5.9 %collective-permute-start.28 = (bf16[112,512]{1,0:T(8,128)(2,1)S(1)}, bf16[112,512]{1,0:T(8,128)(2,1)S(1)}, u32[]{:S(2)}, u32[]{:S(2)}) collective-permute-start(bf16[112,512]{1,0:T(8,128)(2,1)S(1)} %slice.18), channel_id=1, source_target_pairs={{0,8},{8,16},{16,24},{24,28},{28,20},{20,12},{12,4},{4,0},{1,9},{9... | collective-permute-start | bytes 344072 | tf_op jit(solution)/shard_map/ppermute | solution.py:559
  51.1 6.0 %collective-permute-start.21 = (bf16[96,512]{1,0:T(8,128)(2,1)S(1)}, bf16[96,512]{1,0:T(8,128)(2,1)S(1)}, u32[]{:S(2)}, u32[]{:S(2)}) collective-permute-start(bf16[96,512]{1,0:T(8,128)(2,1)S(1)} %collective-permute-done.19.refs_7_), channel_id=1, source_target_pairs={{0,8},{8,16},{16,24},{24,28},{28,20},{20,12},{12,4},{4,0},{1,9},{9... | collective-permute-start | bytes 294920 | tf_op jit(solution)/shard_map/ppermute | solution.py:559
  51.8 5.4 %collective-permute-start.20 = (bf16[96,512]{1,0:T(8,128)(2,1)S(1)}, bf16[96,512]{1,0:T(8,128)(2,1)S(1)}, u32[]{:S(2)}, u32[]{:S(2)}) collective-permute-start(bf16[96,512]{1,0:T(8,128)(2,1)S(1)} %collective-permute-done.18.refs_6_), channel_id=1, source_target_pairs={{8,0},{16,8},{24,16},{28,24},{20,28},{12,20},{4,12},{0,4},{9,1},{1... | collective-permute-start | bytes 294920 | tf_op jit(solution)/shard_map/ppermute | solution.py:562
  53.3 6.2 %collective-permute-start.15 = (bf16[96,512]{1,0:T(8,128)(2,1)S(1)}, bf16[96,512]{1,0:T(8,128)(2,1)S(1)}, u32[]{:S(2)}, u32[]{:S(2)}) collective-permute-start(bf16[96,512]{1,0:T(8,128)(2,1)S(1)} %collective-permute-done.14.refs_12_), channel_id=1, source_target_pairs={{8,0},{16,8},{24,16},{28,24},{20,28},{12,20},{4,12},{0,4},{9,1},{1... | collective-permute-start | bytes 294920 | tf_op jit(solution)/shard_map/ppermute | solution.py:562
  54.8 4.7 %collective-permute-start.11 = (bf16[96,512]{1,0:T(8,128)(2,1)S(1)}, bf16[96,512]{1,0:T(8,128)(2,1)S(1)}, u32[]{:S(2)}, u32[]{:S(2)}) collective-permute-start(bf16[96,512]{1,0:T(8,128)(2,1)S(1)} %collective-permute-done.10.refs_9_), channel_id=1, source_target_pairs={{0,8},{8,16},{16,24},{24,28},{28,20},{20,12},{12,4},{4,0},{1,9},{9... | collective-permute-start | bytes 294920 | tf_op jit(solution)/shard_map/ppermute | solution.py:559
  57.1 2.4 %copy-start.2 = (f32[192,512]{1,0:T(8,128)S(1)}, f32[192,512]{1,0:T(8,128)}, u32[]{:S(2)}) copy-start(f32[192,512]{1,0:T(8,128)} %refs_8_.1) | copy-start | bytes 1179652
  57.2 2.4 %copy-start.3 = (f32[192,512]{1,0:T(8,128)S(1)}, f32[192,512]{1,0:T(8,128)}, u32[]{:S(2)}) copy-start(f32[192,512]{1,0:T(8,128)} %refs_9_.1) | copy-start | bytes 1179652
